TPU v7x, 32 devices: a whole 2x2x4 slice. The times are simulated.
32 devices in a mesh: dp: 16 (over z, y, core), ctx: 2 (over x).
Axes of the slice: x: 2, y: 2, z: 4, core: 2. Of those that a mesh axis runs over, the one named last changes fastest.
Arguments:
- tokens: bfloat16 [16384, 576], P(('dp', 'ctx')), may hold values from -6 to 6
- q_weight: bfloat16 [331776], P(('dp', 'ctx')), may hold values from -0.25 to 0.25
- k_weight: bfloat16 [110592], P(('dp', 'ctx')), may hold values from -0.25 to 0.25
- v_weight: bfloat16 [110592], P(('dp', 'ctx')), may hold values from -0.25 to 0.25
- o_weight: bfloat16 [331776], P(('dp', 'ctx')), may hold values from -3 to 3
- gate_weight: bfloat16 [884736], P(('dp', 'ctx')), may hold values from -0.25 to 0.25
- up_weight: bfloat16 [884736], P(('dp', 'ctx')), may hold values from -0.25 to 0.25
- down_weight: bfloat16 [884736], P(('dp', 'ctx')), may hold values from -0.15625 to 0.15625
- vectors: bfloat16 [2112], P(('dp', 'ctx')), may hold values from -1.2 to 1.25
- doc_lengths: int32 [16, 4], P('dp'), may hold values from 1 to 1024, as said below
- cotangent: bfloat16 [16384, 576], P(('dp', 'ctx')), may hold values from -6 to 6
Outputs:
- layer_out: bfloat16 [16384, 576], P(('dp', 'ctx'))
- input_grad: float32 [16384, 576], P(('dp', 'ctx'))
- q_weight_grad: float32 [331776], P(('dp', 'ctx'))
- k_weight_grad: float32 [110592], P(('dp', 'ctx'))
- v_weight_grad: float32 [110592], P(('dp', 'ctx'))
- o_weight_grad: float32 [331776], P(('dp', 'ctx'))
- gate_weight_grad: float32 [884736], P(('dp', 'ctx'))
- up_weight_grad: float32 [884736], P(('dp', 'ctx'))
- down_weight_grad: float32 [884736], P(('dp', 'ctx'))
- vectors_grad: float32 [2112], P(('dp', 'ctx'))
Inputs may be any that keep to these rules, and one draw needn't show every extreme that they name: `doc_lengths`: each row holds 4 document lengths that sum to 1024.
All inputs are finite; a program needn't handle non-finite values.
Results may differ from a plain program's by a relative error of at most 0.013.
Values may be sent and summed in bfloat16 or wider, within the bound.
No kernel may reach another device: no remote copies, remote signals or barrier semaphores. Data moves between devices by JAX's collectives and lax.ppermute only.
A program may use at most 128 MiB of HBM per device.

v0:
```python
import functools

import jax
import jax.numpy as jnp
import numpy as np
from jax import lax
from jax.experimental import pallas as pl
from jax.experimental.pallas import tpu as pltpu
from jax.sharding import PartitionSpec as P

KV_HEADS = 3
HEAD_DIM = 64

EPS = 1e-06
THETA = 100000.0
NEG_FILL = -1e30
AXES = ("dp", "ctx")
BF = jnp.bfloat16
F32 = jnp.float32


def times(left, right):
    return jnp.dot(left, right, preferred_element_type=F32)


def inner_rows(left, right):
    return lax.dot_general(left, right, (((0,), (0,)), ((), ())), preferred_element_type=F32)


def times_back(left, right):
    return lax.dot_general(left, right, (((1,), (1,)), ((), ())), preferred_element_type=F32)


def norm_back(values, inv, gain, grad):
    scaled = grad * gain
    dot = jnp.mean(scaled * values, axis=-1, keepdims=True)
    grad_values = inv * scaled - values * (inv * inv * inv * dot)
    grad_gain = jnp.sum(grad * values * inv, axis=0)
    return grad_values, grad_gain


def turn(values, cosine, sine):
    half = values.shape[-1] // 2
    first = values[..., :half]
    second = values[..., half:]
    return jnp.concatenate(
        [first * cosine - second * sine, second * cosine + first * sine], axis=-1
    )


def doc_layout(lengths, count):
    ends = jnp.cumsum(lengths)
    place = jnp.arange(count, dtype=jnp.int32)
    segment = jnp.sum((place[:, None] >= ends[None, :-1]).astype(jnp.int32), axis=1)
    starts = ends - lengths
    picked = segment[:, None] == jnp.arange(lengths.shape[0], dtype=jnp.int32)[None, :]
    first = jnp.sum(jnp.where(picked, starts[None, :], 0), axis=1)
    return place - first


def fill_bias(bias, info, docs, short, own=None):
    total, rows = bias.shape
    row_q = lax.broadcasted_iota(jnp.int32, (1, rows), 1) + info[2]
    first = jnp.zeros_like(row_q)
    for j in range(docs - 1):
        first = jnp.where(row_q >= info[3 + j], info[3 + j], first)
    parts = ((0, total, 0),)
    if own is not None:
        parts = ((0, total, info[2] if own else info[1]),)
    elif short < total:
        parts = ((0, total - short, info[1]), (total - short, total, info[2]))
    for start, stop, base in parts:
        row_k = lax.broadcasted_iota(jnp.int32, (stop - start, rows), 0)
        allowed = (row_k >= first - base) & (row_k <= row_q - base)
        bias[start:stop] = jnp.where(allowed, 0.0, NEG_FILL)


def key_range(full, total, short, rows, block, at, causal):
    start = 0 if full else total - short
    stop = total - rows + (at + 1) * block if causal else total
    return start, stop


def key_parts(kv_refs):
    at = 0
    for kv_ref in kv_refs:
        yield slice(at, at + kv_ref.shape[0]), kv_ref
        at += kv_ref.shape[0]


def attn_fwd_kernel(
    heads, block, short, causal, docs, info, q_ref, *refs,
):
    kv_refs, (out_ref, lse_ref, qs, ks, vts, bias, out_t) = refs[:-7], refs[-7:]
    rows = q_ref.shape[0]
    total = bias.shape[0]
    kv_width = KV_HEADS * HEAD_DIM
    group = heads // KV_HEADS
    fill_bias(bias, info, docs, short)
    for h in range(heads):
        qs[h] = q_ref[:, h * HEAD_DIM : (h + 1) * HEAD_DIM] * BF(HEAD_DIM**-0.5)
    for at, kv_ref in key_parts(kv_refs):
        for g in range(KV_HEADS):
            ks[g, at] = kv_ref[:, g * HEAD_DIM : (g + 1) * HEAD_DIM]
        vts[:, at] = jnp.transpose(kv_ref[:, kv_width:].astype(F32)).astype(BF)

    def run(full):
        @pl.loop(0, KV_HEADS)
        def _(g):
            v_rows = pl.ds(pl.multiple_of(g * HEAD_DIM, HEAD_DIM), HEAD_DIM)
            for j in range(group):
                h = g * group + j
                out_rows = pl.ds(pl.multiple_of(h * HEAD_DIM, HEAD_DIM), HEAD_DIM)
                for at in range(rows // block):
                    start, stop = key_range(full, total, short, rows, block, at, causal)
                    cols = slice(at * block, (at + 1) * block)
                    s = times_back(ks[g, start:stop], qs[h, cols])
                    s = s + bias[start:stop, cols]
                    top = jnp.max(s, axis=0, keepdims=True)
                    p = jnp.exp(s - top)
                    total_p = jnp.sum(p, axis=0, keepdims=True)
                    o = times(vts[v_rows, start:stop], p.astype(BF))
                    out_t[out_rows, cols] = o / total_p
                    lse_ref[h, :, cols] = top + jnp.log(total_p)

    pl.when(info[0] != 0)(lambda: run(True))
    pl.when(info[0] == 0)(lambda: run(False))
    out_ref[...] = jnp.transpose(out_t[...]).astype(BF)


def attn_own_kernel(
    heads, block, docs, info, q_ref, kv_ref, acc, top_ref, sum_ref, qs, ks, vts, bias
):
    rows = q_ref.shape[0]
    kv_width = KV_HEADS * HEAD_DIM
    group = heads // KV_HEADS
    fill_bias(bias, info, docs, rows, own=True)
    for h in range(heads):
        qs[h] = q_ref[:, h * HEAD_DIM : (h + 1) * HEAD_DIM] * BF(HEAD_DIM**-0.5)
    for g in range(KV_HEADS):
        ks[g] = kv_ref[:, g * HEAD_DIM : (g + 1) * HEAD_DIM]
    vts[...] = jnp.transpose(kv_ref[:, kv_width:].astype(F32)).astype(BF)

    @pl.loop(0, heads)
    def _(h):
        g = h // group
        v_rows = pl.ds(pl.multiple_of(g * HEAD_DIM, HEAD_DIM), HEAD_DIM)
        out_rows = pl.ds(pl.multiple_of(h * HEAD_DIM, HEAD_DIM), HEAD_DIM)
        for at in range(rows // block):
            stop = (at + 1) * block
            cols = slice(at * block, stop)
            s = times_back(ks[g, :stop], qs[h, cols]) + bias[:stop, cols]
            top = jnp.max(s, axis=0, keepdims=True)
            p = jnp.exp(s - top)
            top_ref[h, :, cols] = top
            sum_ref[h, :, cols] = jnp.sum(p, axis=0, keepdims=True)
            acc[out_rows, cols] = times(vts[v_rows, :stop], p.astype(BF))


def attn_others_kernel(
    heads, block, docs, info, q_ref, kv_ref, acc, top_ref, sum_ref, out_ref, lse_ref,
    qs, ks, vts, bias, out_t,
):
    rows = q_ref.shape[0]
    kv_width = KV_HEADS * HEAD_DIM
    group = heads // KV_HEADS

    @pl.when(info[0] == 0)
    def _():
        for h in range(heads):
            at = slice(h * HEAD_DIM, (h + 1) * HEAD_DIM)
            out_t[at] = acc[at] / sum_ref[h]
            lse_ref[h] = top_ref[h] + jnp.log(sum_ref[h])

    @pl.when(info[0] != 0)
    def _():
        fill_bias(bias, info, docs, rows, own=False)
        for h in range(heads):
            qs[h] = q_ref[:, h * HEAD_DIM : (h + 1) * HEAD_DIM] * BF(HEAD_DIM**-0.5)
        for g in range(KV_HEADS):
            ks[g] = kv_ref[:, g * HEAD_DIM : (g + 1) * HEAD_DIM]
        vts[...] = jnp.transpose(kv_ref[:, kv_width:].astype(F32)).astype(BF)

        @pl.loop(0, heads)
        def _(h):
            g = h // group
            v_rows = pl.ds(pl.multiple_of(g * HEAD_DIM, HEAD_DIM), HEAD_DIM)
            out_rows = pl.ds(pl.multiple_of(h * HEAD_DIM, HEAD_DIM), HEAD_DIM)
            for at in range(rows // block):
                cols = slice(at * block, (at + 1) * block)
                s = times_back(ks[g], qs[h, cols]) + bias[:, cols]
                own = top_ref[h, :, cols]
                top = jnp.maximum(own, jnp.max(s, axis=0, keepdims=True))
                scale = jnp.exp(own - top)
                p = jnp.exp(s - top)
                total_p = sum_ref[h, :, cols] * scale + jnp.sum(p, axis=0, keepdims=True)
                o = acc[out_rows, cols] * scale + times(vts[v_rows], p.astype(BF))
                out_t[out_rows, cols] = o / total_p
                lse_ref[h, :, cols] = top + jnp.log(total_p)

    out_ref[...] = jnp.transpose(out_t[...]).astype(BF)


def attn_grad_kernel(
    heads, block, docs, own, info, q_ref, kv_ref, do_ref, lse_ref, delta_ref, *refs
):
    refs, (qs, dos, ks, vs, kts, bias, dk, dv) = refs[:-8], refs[-8:]
    if own:
        before, dq_ref, dkv_ref, dq_t = refs
    else:
        dq_t, dkv_ref = refs
    rows = q_ref.shape[0]
    kv_width = KV_HEADS * HEAD_DIM
    group = heads // KV_HEADS
    dk[...] = jnp.zeros_like(dk)
    dv[...] = jnp.zeros_like(dv)

    def run():
        fill_bias(bias, info, docs, rows, own=own)
        for h in range(heads):
            at = slice(h * HEAD_DIM, (h + 1) * HEAD_DIM)
            qs[h] = q_ref[:, at] * BF(HEAD_DIM**-0.5)
            dos[h] = do_ref[:, at]
        for g in range(KV_HEADS):
            lo = g * HEAD_DIM
            ks[g] = kv_ref[:, lo : lo + HEAD_DIM]
            vs[g] = kv_ref[:, kv_width + lo : kv_width + lo + HEAD_DIM]
        kts[...] = jnp.transpose(kv_ref[:, :kv_width].astype(F32)).astype(BF)

        @pl.loop(0, heads)
        def _(h):
            g = h // group
            k_rows = pl.ds(pl.multiple_of(g * HEAD_DIM, HEAD_DIM), HEAD_DIM)
            out_rows = pl.ds(pl.multiple_of(h * HEAD_DIM, HEAD_DIM), HEAD_DIM)
            for at in range(rows // block):
                stop = (at + 1) * block if own else rows
                cols = slice(at * block, (at + 1) * block)
                q = qs[h, cols]
                do = dos[h, cols]
                s = times_back(ks[g, :stop], q) + bias[:stop, cols]
                p = jnp.exp(s - lse_ref[h, :, cols])
                dp = times_back(vs[g, :stop], do)
                ds = (p * (dp - delta_ref[h, :, cols])).astype(BF)
                dk[g, :stop] += times(ds, q)
                dv[g, :stop] += times(p.astype(BF), do)
                dq = times(kts[k_rows, :stop], ds) * HEAD_DIM**-0.5
                dq_t[out_rows, cols] = before[out_rows, cols] + dq if own else dq

    if own:
        run()
        dq_ref[...] = jnp.transpose(dq_t[...])
    else:
        pl.when(info[0] != 0)(run)

        @pl.when(info[0] == 0)
        def _():
            dq_t[...] = jnp.zeros_like(dq_t)

    for g in range(KV_HEADS):
        lo = g * HEAD_DIM
        dkv_ref[:, lo : lo + HEAD_DIM] = dk[g].astype(dkv_ref.dtype)
        dkv_ref[:, kv_width + lo : kv_width + lo + HEAD_DIM] = dv[g].astype(dkv_ref.dtype)


def attn_bwd_kernel(
    heads, block, short, causal, docs, g0, g1, parts, info, q_ref, do_ref, lse_ref, *refs,
):
    kv_refs, outs, scratch = refs[:parts], refs[parts:-9], refs[-9:]
    qs, ks, vs, kts, dos, bias, dq_t, dk, dv = scratch
    rows = q_ref.shape[0]
    total = bias.shape[0]
    kv_width = KV_HEADS * HEAD_DIM
    group = heads // KV_HEADS
    keys = g1 - g0
    fill_bias(bias, info, docs, short)
    for h in range(keys * group):
        lanes = slice((g0 * group + h) * HEAD_DIM, (g0 * group + h + 1) * HEAD_DIM)
        qs[h] = q_ref[:, lanes] * BF(HEAD_DIM**-0.5)
        dos[h] = do_ref[:, lanes]
    for g in range(keys):
        lo = (g0 + g) * HEAD_DIM
        for at, kv_ref in key_parts(kv_refs):
            ks[g, at] = kv_ref[:, lo : lo + HEAD_DIM]
            vs[g, at] = kv_ref[:, kv_width + lo : kv_width + lo + HEAD_DIM]
        kts[g] = jnp.transpose(ks[g].astype(F32)).astype(BF)
    dk[...] = jnp.zeros_like(dk)
    dv[...] = jnp.zeros_like(dv)

    def run(full):
        @pl.loop(0, keys * group)
        def _(h):
            g = h // group if keys > 1 else 0
            out_rows = pl.ds(pl.multiple_of(h * HEAD_DIM, HEAD_DIM), HEAD_DIM)
            for at in range(rows // block):
                start, stop = key_range(full, total, short, rows, block, at, causal)
                cols = slice(at * block, (at + 1) * block)
                q = qs[h, cols]
                do = dos[h, cols]
                s = times_back(ks[g, start:stop], q)
                p = jnp.exp(s + bias[start:stop, cols] - lse_ref[g0 * group + h, :, cols])
                dp = times_back(vs[g, start:stop], do)
                t = p * dp
                inner = jnp.sum(t, axis=0, keepdims=True)
                ds = (t - p * inner).astype(BF)
                dk[g, start:stop] += times(ds, q)
                dv[g, start:stop] += times(p.astype(BF), do)
                dq_t[out_rows, cols] = times(kts[g, :, start:stop], ds) * HEAD_DIM**-0.5

    pl.when(info[0] != 0)(lambda: run(True))
    pl.when(info[0] == 0)(lambda: run(False))
    outs[0][...] = jnp.transpose(dq_t[...])
    cut = total - outs[1].shape[0]
    for part, out in ((slice(cut, total), outs[1]),) + tuple((slice(0, cut), o) for o in outs[2:]):
        for g in range(keys):
            lo = g * HEAD_DIM
            out[:, lo : lo + HEAD_DIM] = dk[g, part].astype(out.dtype)
            lo += keys * HEAD_DIM
            out[:, lo : lo + HEAD_DIM] = dv[g, part].astype(out.dtype)


VM = pl.BlockSpec(memory_space=pltpu.VMEM)
SM = pl.BlockSpec(memory_space=pltpu.SMEM)


def cost_of(micros):
    return pl.CostEstimate(
        flops=int(micros * 1.1e9), bytes_accessed=2**20, transcendentals=0
    )


def attention(q, kv, info, docs, short, causal):
    rows, width = q.shape
    total = sum(part.shape[0] for part in kv)
    heads = width // HEAD_DIM
    block = min(rows, 256)
    return pl.pallas_call(
        functools.partial(attn_fwd_kernel, heads, block, short, causal, docs),
        out_shape=(
            jax.ShapeDtypeStruct((rows, width), BF),
            jax.ShapeDtypeStruct((heads, 1, rows), F32),
        ),
        in_specs=[SM] + [VM] * (1 + len(kv)),
        out_specs=(VM, VM),
        scratch_shapes=[
            pltpu.VMEM((heads, rows, HEAD_DIM), BF),
            pltpu.VMEM((KV_HEADS, total, HEAD_DIM), BF),
            pltpu.VMEM((KV_HEADS * HEAD_DIM, total), BF),
            pltpu.VMEM((total, rows), F32),
            pltpu.VMEM((width, rows), F32),
        ],
        compiler_params=pltpu.CompilerParams(vmem_limit_bytes=20 * 2**20),
        cost_estimate=cost_of(14),
        name="attn_fwd",
    )(info, q, *kv)


def attention_own(q, kv, info, docs):
    rows, width = q.shape
    heads = width // HEAD_DIM
    stat = jax.ShapeDtypeStruct((heads, 1, rows), F32)
    return pl.pallas_call(
        functools.partial(attn_own_kernel, heads, min(rows, 256), docs),
        out_shape=(jax.ShapeDtypeStruct((width, rows), F32), stat, stat),
        in_specs=[SM, VM, VM],
        out_specs=(VM, VM, VM),
        scratch_shapes=attn_scratch(rows, heads),
        compiler_params=pltpu.CompilerParams(vmem_limit_bytes=16 * 2**20),
        cost_estimate=cost_of(6),
        name="attn_own",
    )(info, q, kv)


def attn_scratch(rows, heads):
    return [
        pltpu.VMEM((heads, rows, HEAD_DIM), BF),
        pltpu.VMEM((KV_HEADS, rows, HEAD_DIM), BF),
        pltpu.VMEM((KV_HEADS * HEAD_DIM, rows), BF),
        pltpu.VMEM((rows, rows), F32),
    ]


def attention_grad(q, kv, grad_out, lse, delta, info, docs, before=None):
    rows, width = q.shape
    heads = width // HEAD_DIM
    own = before is not None
    turned = jax.ShapeDtypeStruct((width, rows), F32)
    if own:
        outs = [jax.ShapeDtypeStruct((rows, width), F32), jax.ShapeDtypeStruct(kv.shape, F32)]
    else:
        outs = [turned, jax.ShapeDtypeStruct(kv.shape, BF)]
    by_head = pltpu.VMEM((heads, rows, HEAD_DIM), BF)
    by_key = pltpu.VMEM((KV_HEADS, rows, HEAD_DIM), BF)
    sums = pltpu.VMEM((KV_HEADS, rows, HEAD_DIM), F32)
    return pl.pallas_call(
        functools.partial(attn_grad_kernel, heads, min(rows, 256), docs, own),
        out_shape=outs,
        in_specs=[SM] + [VM] * (6 if own else 5),
        out_specs=[VM] * 2,
        scratch_shapes=([pltpu.VMEM((width, rows), F32)] if own else []) + [
            by_head, by_head, by_key, by_key, pltpu.VMEM((KV_HEADS * HEAD_DIM, rows), BF),
            pltpu.VMEM((rows, rows), F32), sums, sums,
        ],
        compiler_params=pltpu.CompilerParams(vmem_limit_bytes=20 * 2**20),
        cost_estimate=cost_of(9 if own else 10),
        name="attn_grad_own" if own else "attn_grad_others",
    )(info, q, kv, grad_out, lse, delta, *([before] if own else []))


def attention_others(q, kv, acc, top, total, info, docs):
    rows, width = q.shape
    heads = width // HEAD_DIM
    return pl.pallas_call(
        functools.partial(attn_others_kernel, heads, min(rows, 256), docs),
        out_shape=(
            jax.ShapeDtypeStruct((rows, width), BF),
            jax.ShapeDtypeStruct((heads, 1, rows), F32),
        ),
        in_specs=[SM] + [VM] * 5,
        out_specs=(VM, VM),
        scratch_shapes=attn_scratch(rows, heads) + [pltpu.VMEM((width, rows), F32)],
        compiler_params=pltpu.CompilerParams(vmem_limit_bytes=16 * 2**20),
        cost_estimate=cost_of(10),
        name="attn_others",
    )(info, q, kv, acc, top, total)


def attention_back(q, kv, grad_out, lse, info, docs, short, causal, g0, g1):
    rows, width = q.shape
    total = sum(part.shape[0] for part in kv)
    heads = width // HEAD_DIM
    block = min(rows, 256)
    keys = g1 - g0
    mine = heads // KV_HEADS * keys
    outs = [jax.ShapeDtypeStruct((rows, mine * HEAD_DIM), F32)]
    if causal:
        outs.append(jax.ShapeDtypeStruct((rows, 2 * keys * HEAD_DIM), F32))
        outs.append(jax.ShapeDtypeStruct((total - rows, 2 * keys * HEAD_DIM), BF))
    else:
        outs.append(jax.ShapeDtypeStruct((total, 2 * keys * HEAD_DIM), F32))
    return pl.pallas_call(
        functools.partial(attn_bwd_kernel, heads, block, short, causal, docs, g0, g1, len(kv)),
        out_shape=outs,
        in_specs=[SM] + [VM] * (3 + len(kv)),
        out_specs=[VM] * len(outs),
        scratch_shapes=[
            pltpu.VMEM((mine, rows, HEAD_DIM), BF),
            pltpu.VMEM((keys, total, HEAD_DIM), BF),
            pltpu.VMEM((keys, total, HEAD_DIM), BF),
            pltpu.VMEM((keys, HEAD_DIM, total), BF),
            pltpu.VMEM((mine, rows, HEAD_DIM), BF),
            pltpu.VMEM((total, rows), F32),
            pltpu.VMEM((mine * HEAD_DIM, rows), F32),
            pltpu.VMEM((keys, total, HEAD_DIM), F32),
            pltpu.VMEM((keys, total, HEAD_DIM), F32),
        ],
        compiler_params=pltpu.CompilerParams(vmem_limit_bytes=20 * 2**20),
        cost_estimate=cost_of(20),
        name="attn_bwd",
    )(info, q, grad_out, lse, *kv)


TAIL = 2
MAIN = 16
PIECES = MAIN // TAIL


class Blocks:
    def __init__(self, dp_count, ctx_count):
        self.count = dp_count * ctx_count
        self.x = 1
        self.core = ctx_count
        self.y = 2 * ctx_count
        self.z = 4 * ctx_count
        self.zs = dp_count // 4
        self.masks = []
        for p in range(self.count):
            z, x = p % self.zs, p // self.zs % 2
            y, core = p // (2 * self.zs) % 2, p // (4 * self.zs)
            self.masks.append(x * self.x + y * self.y + core * self.core + z * self.z)

    def swap(self, values, mask):
        perm = [(i, i ^ mask) for i in range(self.count)]
        return lax.ppermute(values, AXES, perm)

    def along_z(self, mine):
        return jnp.stack([mine] + [self.swap(mine, d * self.z) for d in range(1, self.zs)])

    def add(self, keep, got):
        return (keep.astype(F32) + got.astype(F32)).astype(BF)

    def sum_z(self, held):
        got = [self.swap(held[d], d * self.z).astype(F32) for d in range(1, self.zs)]
        return functools.reduce(jnp.add, got, held[0].astype(F32))


class Sizes:
    def __init__(self, width, ff, dp, ctx, vec, kv_width):
        count = dp * ctx
        self.zs, self.ctx = dp // 4, ctx
        self.width, self.ff, self.count, self.vec = width, ff, count, vec
        self.rows = width // count
        self.f_rows = ff // count
        up = lambda n: (n + 127) // 128 * 128
        self.wide = up(width)
        self.qkv = width + 2 * kv_width
        self.a_width = up(self.qkv)
        self.tall = (self.rows + 1 + 7) // 8 * 8
        self.downs = self.f_rows // MAIN
        self.piece = 2 * ff // PIECES
        self.gate = 0
        self.tail = ff
        self.tail_o = self.tail + self.piece
        self.out = self.tail_o + 128
        self.down0 = self.out + self.wide
        self.first = self.down0 + self.wide
        self.second = ff + (self.downs - 1) * self.wide
        self.back_first = self.down0 + (self.downs - 1) * self.wide
        self.back_second = ff + self.wide
        self.flat = self.a_width + 2 * self.wide

    def down_at(self, c):
        return (0, self.down0) if c == 0 else (1, self.ff + (c - 1) * self.wide)

    def down_back_at(self, c):
        return (0, self.down0 + c * self.wide) if c < self.downs - 1 else (1, self.ff)

    def fits(self):
        return (
            self.rows == MAIN + TAIL
            and self.f_rows % MAIN == 0
            and self.piece % 128 == 0
            and self.ff % 256 == 0
            and self.wide <= 128 * PIECES
            and self.vec <= 128
        )


def wire_kernel(
    size, g_ref, u_ref, o_ref, d_ref, xt_ref, cott_ref, out1, out2, x_any, cot_any,
    tail, tail_o, x_ref, cot_ref, sems,
):
    ff, width = size.ff, size.width
    x_ref[...] = jnp.transpose(xt_ref[...].astype(F32)).astype(BF)
    cot_ref[...] = jnp.transpose(cott_ref[...].astype(F32)).astype(BF)
    copies = fetch((x_ref, cot_ref), (x_any, cot_any), sems)
    out1[:, : ff] = g_ref[:MAIN]
    out2[:, : ff] = u_ref[:MAIN]
    out1[:, size.out : size.out + size.wide] = jnp.zeros((MAIN, size.wide), BF)
    out1[:, size.out : size.out + width] = o_ref[:MAIN]
    tail_o[...] = jnp.zeros_like(tail_o)
    odd = [ref[MAIN:].astype(F32) for ref in (g_ref, u_ref, o_ref)]
    for c in range(PIECES):
        src = odd[c * size.piece // ff]
        at = c * size.piece % ff
        tail[c * TAIL : (c + 1) * TAIL] = src[:, at : at + size.piece]
        used = min(128, width - c * 128)
        if used > 0:
            tail_o[c * TAIL : (c + 1) * TAIL, :used] = odd[2][:, c * 128 : c * 128 + used]
    out1[:, size.tail : size.tail + size.piece] = tail[...].astype(BF)
    out1[:, size.tail_o : size.tail_o + 128] = tail_o[...].astype(BF)
    for c in range(size.downs):
        which, at = size.down_at(c)
        out = (out1, out2)[which]
        out[:, at : at + size.wide] = jnp.zeros((MAIN, size.wide), BF)
        out[:, at : at + width] = d_ref[c * MAIN : (c + 1) * MAIN]
    for copy in copies:
        copy.wait()


def over(values, by):
    scale = 2**16 // by + 1
    whole = (values * scale) >> 16
    return whole, values - whole * by


def mask_of(size, p):
    z, rest = p % size.zs, p // size.zs
    x, y, core = rest % 2, rest // 2 % 2, rest // 4
    return x + core * size.ctx + y * (2 * size.ctx) + z * (4 * size.ctx)


def lanes(count):
    return lax.broadcasted_iota(jnp.int32, (1, count), 1)


def place_matrix(size, me, tall):
    if tall:
        p, inside = over(lanes(size.count * size.tall), size.tall)
        feature = jnp.where(inside < size.rows, size.rows * (me ^ mask_of(size, p)) + inside, -1)
    else:
        s = lanes(size.count * (MAIN + TAIL))
        tail = s - size.count * MAIN
        p = jnp.where(tail < 0, s // MAIN, tail // TAIL)
        inside = jnp.where(tail < 0, s % MAIN, MAIN + tail % TAIL)
        feature = size.rows * (me ^ mask_of(size, p)) + inside
    at = lax.broadcasted_iota(jnp.int32, (size.width, feature.shape[1]), 0)
    return jnp.where(at == feature, 1.0, 0.0).astype(BF)


def vector_places(size, me):
    at = lanes(size.flat)
    ends = (size.a_width, size.a_width + size.wide)
    part = jnp.where(at < ends[0], 0, jnp.where(at < ends[1], 1, 2))
    inside = at - jnp.where(part == 0, 0, jnp.where(part == 1, ends[0], ends[1]))
    start = jnp.where(part == 0, 0, jnp.where(part == 1, size.qkv, size.qkv + size.width))
    used = inside < jnp.where(part == 0, size.qkv, size.width)
    owner, lane = over(start + inside, size.vec)
    rows = lax.broadcasted_iota(jnp.int32, (128, size.flat), 0)
    spread = jnp.where((rows == lane) & used, 1.0, 0.0).astype(BF)
    p = lax.broadcasted_iota(jnp.int32, (size.count, 1), 0)
    return spread, (owner == (me ^ mask_of(size, p))) & used


def swap_halves(u):
    rolled_back = pltpu.roll(u, 128 - HEAD_DIM // 2, 1)
    rolled = pltpu.roll(u, HEAD_DIM // 2, 1)
    lane = lax.broadcasted_iota(jnp.int32, u.shape, 1)
    return jnp.where(lane % HEAD_DIM < HEAD_DIM // 2, rolled_back, rolled)


def fetch(sources, targets, sems):
    copies = [
        pltpu.make_async_copy(src, dst, sems.at[i])
        for i, (src, dst) in enumerate(zip(sources, targets))
    ]
    for copy in copies:
        copy.start()
    return copies


def pre_kernel(
    size, me_ref, x_ref, wm_ref, wo_ref, cos_ref, sin_ref,
    q_ref, kv_ref, n1t_ref, flat_ref, w, qkv,
):
    me = me_ref[0]
    half = wm_ref.shape[0]
    w[:half] = wm_ref[...]
    w[half:] = wo_ref[...]
    place = place_matrix(size, me, True)
    spread, mine = vector_places(size, me)
    shape = (size.count, 2 * half)
    row = lax.broadcasted_iota(jnp.int32, shape, 0) * size.tall + size.rows
    row = jnp.where(lax.broadcasted_iota(jnp.int32, shape, 1) == row, 1.0, 0.0).astype(BF)
    packed = times(row, w[:, :128]).astype(BF)
    flat = jnp.sum(jnp.where(mine, times(packed, spread), 0.0), axis=0, keepdims=True)
    flat_ref[...] = flat
    gain = flat[:, size.a_width : size.a_width + size.width]
    x = x_ref[...].astype(F32)
    inv = lax.rsqrt(jnp.mean(x * x, axis=-1, keepdims=True) + EPS)
    n1 = (x * inv * gain).astype(BF)
    n1a = times(n1, place)
    n1t_ref[...] = jnp.transpose(n1a).astype(BF)
    qkv[...] = times(n1a.astype(BF), w[...]) + flat[:, : size.a_width]
    kv_width = kv_ref.shape[1] // 2
    for t in range((size.width + kv_width) // 128):
        u = qkv[:, t * 128 : (t + 1) * 128]
        qkv[:, t * 128 : (t + 1) * 128] = u * cos_ref[...] + swap_halves(u) * sin_ref[...]
    q_ref[...] = qkv[:, : size.width].astype(BF)
    kv_ref[...] = qkv[:, size.width : size.qkv].astype(BF)


def tail_place(size, back):
    odd, count = size.count * TAIL, size.count * MAIN
    row = lax.broadcasted_iota(jnp.int32, (count, count), 1 if back else 0)
    at = lax.broadcasted_iota(jnp.int32, (count, count), 0 if back else 1)
    c, q = row // odd, row % odd
    want = (q // TAIL) * MAIN + c * TAIL + q % TAIL
    return jnp.where(at == want, 1.0, 0.0).astype(BF)


def mlp_kernel(
    size, me_ref, attn_ref, x_ref, cot_ref, flat_ref,
    b1_00, b1_01, b1_10, b1_11, b2_00, b2_01, b2_10, b2_11,
    out_ref, keep1, give1, keep2, give2, gmid_ref, gattn_ref, ggain_ref, delta_ref,
    wg, wu, wo, wd, mid, n2s, n2t, place, acc, gacc, dwd, tails, tail_o, packed,
):
    me = me_ref[0]
    width, ff = size.width, size.ff
    part = b1_00.shape[0]
    half, main = 2 * part, 4 * part
    rows_z = part // 2
    place[...] = place_matrix(size, me, False)
    first = (b1_00, b1_01, b1_10, b1_11)
    second = (b2_00, b2_01, b2_10, b2_11)
    room = size.piece + 128
    for i, b1 in enumerate(first):
        rows = slice(i * part, (i + 1) * part)
        wg[rows] = b1[:, :ff]
        wo[rows] = b1[:, size.out : size.out + size.wide]
        packed[rows] = b1[:, size.tail : size.tail + room]
    for i, b2 in enumerate(second):
        for y in range(2):
            at = (i // 2) * half + y * part + (i % 2) * rows_z
            wu[at : at + rows_z] = b2[y * rows_z : (y + 1) * rows_z, :ff]
    odd = size.count * TAIL
    got = times(tail_place(size, False), packed[...]).astype(BF)
    for c in range(PIECES):
        rows = slice(c * odd, (c + 1) * odd)
        target = wg if c * size.piece < ff else wu
        at = c * size.piece % ff
        target[main:, at : at + size.piece] = got[rows, : size.piece]
        if c * 128 < size.wide:
            wo[main:, c * 128 : (c + 1) * 128] = got[rows, size.piece :]
    zs = rows_z // MAIN
    for p in range(size.count):
        z, x, y, core = p % zs, p // zs % 2, p // (2 * zs) % 2, p // (4 * zs)
        owner = me ^ mask_of(size, p)
        for c in range(size.downs):
            which, at = size.down_at(c)
            src, row = (second[2 * core + x], y * zs + z) if which else (
                first[2 * core + y], x * zs + z
            )
            to = pl.multiple_of(owner * size.f_rows + c * MAIN, MAIN)
            wd[pl.ds(to, MAIN), :] = src[row * MAIN : (row + 1) * MAIN, at : at + size.wide]
    attn_s = times(attn_ref[...], place[...])
    m = x_ref[...].astype(F32) + times(attn_s.astype(BF), wo[:, :width])
    mid[...] = m
    inv = lax.rsqrt(jnp.mean(m * m, axis=-1, keepdims=True) + EPS)
    lo = size.a_width + size.wide
    gain = flat_ref[:, lo : lo + width]
    n2 = (m * inv * gain).astype(BF)
    spread = times(n2, place[...])
    n2s[...] = spread.astype(BF)
    n2t[...] = jnp.transpose(spread).astype(BF)
    acc[...] = jnp.zeros_like(acc)
    gacc[...] = jnp.zeros_like(gacc)
    step = 512 if ff % 512 == 0 else 256

    @pl.loop(0, ff // step)
    def _(b):
        at = pl.multiple_of(b * step, step)
        cols = pl.ds(at, step)
        gate = times(n2s[...], wg[:, cols])
        up = times(n2s[...], wu[:, cols])
        sig = 1.0 / (1.0 + jnp.exp(-gate))
        act = gate * sig
        h = act * up
        gh = times_back(cot_ref[...], wd[cols, :width])
        gg = (gh * up * (sig * (1.0 + gate * (1.0 - sig)))).astype(BF)
        gu = (gh * act).astype(BF)
        acc[...] += times(h.astype(BF), wd[cols, :width])
        dwd[cols, :width] = times(jnp.transpose(h).astype(BF), cot_ref[...]).astype(BF)
        gacc[...] += times_back(gg, wg[:, cols]) + times_back(gu, wu[:, cols])
        for k, (grad, keep, give) in enumerate(((gg, keep1, give1), (gu, keep2, give2))):
            dw = times(n2t[...], grad).astype(BF)
            keep[:, cols] = dw[:half]
            give[:, cols] = dw[half:main]
            tails[:, pl.ds(pl.multiple_of(k * ff + at, 128), step)] = dw[main:]

    m = mid[...]
    inv = lax.rsqrt(jnp.mean(m * m, axis=-1, keepdims=True) + EPS)
    out_ref[...] = jnp.transpose(m + acc[...]).astype(BF)
    gn2 = times_back(gacc[...].astype(BF), place[...])
    scaled = gn2 * gain
    dot = jnp.mean(scaled * m, axis=-1, keepdims=True)
    ggain_ref[...] = jnp.sum(gn2 * m * inv, axis=0, keepdims=True)
    gmid = cot_ref[...].astype(F32) + inv * scaled - m * (inv * inv * inv * dot)
    gmid_ref[...] = gmid
    branch = gmid.astype(BF)
    gattn = times_back(branch, wo[:, :width]).astype(BF)
    gattn = times_back(gattn, place[...]).astype(BF)
    gattn_ref[...] = gattn
    both = jnp.transpose(gattn.astype(F32) * attn_ref[...].astype(F32))
    for h in range(width // HEAD_DIM):
        at = slice(h * HEAD_DIM, (h + 1) * HEAD_DIM)
        delta_ref[h] = jnp.sum(both[at], axis=0, keepdims=True)
    dwo = times(jnp.transpose(attn_s).astype(BF), branch).astype(BF)
    tail_o[...] = jnp.zeros_like(tail_o)
    tail_o[:, :width] = dwo[main:]
    terms = ((keep1, keep2), (give1, give2))
    for i, (term, _) in enumerate(terms):
        term[:, size.out : size.out + width] = dwo[i * half : (i + 1) * half]
    packed[...] = jnp.zeros_like(packed)
    for c in range(PIECES):
        rows = slice(c * odd, (c + 1) * odd)
        packed[rows, : size.piece] = tails[:, c * size.piece : (c + 1) * size.piece]
        if c * 128 < size.wide:
            packed[rows, size.piece :] = tail_o[:, c * 128 : (c + 1) * 128]
    wire = times(tail_place(size, True), packed[...]).astype(BF)
    for i, (term, _) in enumerate(terms):
        rows = slice(i * half, (i + 1) * half)
        term[:, size.tail : size.tail + room] = wire[rows]
    for p in range(size.count):
        to = terms[p // (size.count // 2)]
        rows = slice(p * MAIN % half, p * MAIN % half + MAIN)
        owner = me ^ mask_of(size, p)
        for c in range(size.downs):
            which, at = size.down_back_at(c)
            src = pl.multiple_of(owner * size.f_rows + c * MAIN, MAIN)
            to[which][rows, at : at + size.wide] = dwd[pl.ds(src, MAIN), :]


def post_kernel(
    size, me_ref, dq_ref, dkv_ref, got_ref, cos_ref, sin_ref, n1t_ref,
    wm_ref, wo_ref, x_ref, gmid_ref, flat_ref, ggain_ref,
    gx_ref, keep_ref, give_ref, turn_buf, grad, vec_row,
):
    me = me_ref[0]
    width = size.width
    half = wm_ref.shape[0]
    place = place_matrix(size, me, True)
    kv_width = KV_HEADS * HEAD_DIM
    turned = width + kv_width
    dkv = dkv_ref[...] + got_ref[...].astype(F32)
    turn_buf[:, :width] = dq_ref[...]
    turn_buf[:, width:] = dkv[:, :kv_width]
    grad[...] = jnp.zeros_like(grad)
    grad[:, turned : turned + kv_width] = dkv[:, kv_width:].astype(BF)
    for t in range(turned // 128):
        u = turn_buf[:, t * 128 : (t + 1) * 128]
        back = u * cos_ref[...] - swap_halves(u) * sin_ref[...]
        grad[:, t * 128 : (t + 1) * 128] = back.astype(BF)
    g = grad[...]
    gn1 = jnp.zeros((g.shape[0], width), F32)
    for part, w_ref in enumerate((wm_ref, wo_ref)):
        values = times_back(g, w_ref[...]).astype(BF)
        gn1 += times_back(values, place[:, part * half : (part + 1) * half])
    x = x_ref[...].astype(F32)
    inv = lax.rsqrt(jnp.mean(x * x, axis=-1, keepdims=True) + EPS)
    gain = flat_ref[:, size.a_width : size.a_width + width]
    scaled = gn1 * gain
    dot = jnp.mean(scaled * x, axis=-1, keepdims=True)
    gx_ref[...] = jnp.transpose(gmid_ref[...] + inv * scaled - x * (inv * inv * inv * dot))
    vec_row[...] = jnp.zeros_like(vec_row)
    vec_row[:, : size.a_width] = jnp.sum(g.astype(F32), axis=0, keepdims=True)
    vec_row[:, size.a_width : size.a_width + width] = jnp.sum(gn1 * x * inv, axis=0, keepdims=True)
    lo = size.a_width + size.wide
    vec_row[:, lo : lo + width] = ggain_ref[...]
    spread, mine = vector_places(size, me)
    packed = times_back(jnp.where(mine, vec_row[...], 0.0).astype(BF), spread)
    shape = (half, size.count)
    for part, term in ((0, keep_ref), (1, give_ref)):
        rows = slice(part * half, (part + 1) * half)
        dw = times(n1t_ref[rows], g)
        term[...] = dw.astype(BF)
        want = lax.broadcasted_iota(jnp.int32, shape, 1) * size.tall + size.rows - part * half
        here = lax.broadcasted_iota(jnp.int32, shape, 0) == want
        extra = times(jnp.where(here, 1.0, 0.0).astype(BF), packed.astype(BF))
        term[:, :128] = (dw[:, :128] + extra).astype(BF)


def call(kernel, name, out_shape, scratch, micros, args, vmem, any_in=(), any_out=(), scalar=True):
    shapes = [jax.ShapeDtypeStruct(s, t) for s, t in out_shape]
    here = pl.BlockSpec(memory_space=pl.ANY)
    specs = [here if i in any_in else VM for i in range(len(args))]
    if scalar:
        specs[0] = SM
    return pl.pallas_call(
        kernel,
        out_shape=shapes,
        in_specs=specs,
        out_specs=[here if i in any_out else VM for i in range(len(shapes))],
        scratch_shapes=[
            pltpu.SemaphoreType.DMA(s) if t is None else pltpu.VMEM(s, t) for s, t in scratch
        ],
        compiler_params=pltpu.CompilerParams(vmem_limit_bytes=vmem * 2**20),
        cost_estimate=cost_of(micros),
        name=name,
    )(*args)


def pad_to(values, rows, columns):
    return jnp.pad(values, ((0, rows - values.shape[0]), (0, columns - values.shape[1])))


def tail_pack(rows, piece):
    rows = pad_to(rows, TAIL, PIECES * piece)
    return rows.reshape(TAIL, PIECES, piece).transpose(1, 0, 2).reshape(MAIN, piece)


def tail_unpack(wire, used):
    piece = wire.shape[1]
    rows = wire.reshape(PIECES, TAIL, piece).transpose(1, 0, 2).reshape(TAIL, PIECES * piece)
    return rows[:, :used]


def tie(*values):
    return lax.optimization_barrier(values)


def local_blocks(size, blocks, pos, args):
    (
        tokens, q_weight, k_weight, v_weight, o_weight, gate_weight, up_weight, down_weight,
        vectors, cotangent,
    ) = args
    tok_rows, width = tokens.shape
    ff, rows = size.ff, size.rows
    kv_width = KV_HEADS * HEAD_DIM
    ctx_index = lax.axis_index("ctx")
    me = (lax.axis_index("dp") * lax.axis_size("ctx") + ctx_index).astype(jnp.int32).reshape(1)
    half = size.count // 2
    info, docs, cos, sin = pos

    joined_w = jnp.concatenate(
        [w.reshape(rows, -1) for w in (q_weight, k_weight, v_weight)], axis=1
    )
    vec_row = pad_to(vectors.reshape(1, -1), size.tall - rows, size.a_width)
    wire_a = jnp.concatenate([pad_to(joined_w, rows, size.a_width), vec_row], axis=0)
    za = blocks.along_z(wire_a)
    xa = jnp.stack([za, blocks.swap(za, blocks.x)])
    _, flat_w = tie(za, (gate_weight, up_weight, o_weight, down_weight))
    w_rows = [w.reshape(rows, -1) for w in flat_w[:3]]
    wire_1, wire_2, tokens, cotangent = call(
        functools.partial(wire_kernel, size),
        "wire",
        [
            ((MAIN, size.first), BF), ((MAIN, size.second), BF), ((tok_rows, width), BF),
            ((tok_rows, width), BF),
        ],
        [
            ((MAIN, size.piece), F32), ((MAIN, 128), F32), ((tok_rows, width), BF),
            ((tok_rows, width), BF), ((2,), None),
        ],
        1,
        w_rows + [flat_w[3].reshape(size.f_rows, width), tokens.T, cotangent.T],
        10,
        any_out=(2, 3),
        scalar=False,
    )
    xa, wire_1, wire_2 = tie(xa, wire_1, wire_2)
    ya = blocks.swap(xa, blocks.y)
    z1 = blocks.along_z(wire_1)
    z1, wire_2, ya = tie(z1, wire_2, ya)
    z2 = blocks.along_z(wire_2)
    x1 = jnp.stack([z1, blocks.swap(z1, blocks.x)])
    a_mine = jnp.stack([xa, ya]).reshape(half * size.tall, size.a_width)
    a_other = blocks.swap(a_mine, blocks.core)

    a_rows = size.count * size.tall
    q_rot, kv_mine, n1t, flat = call(
        functools.partial(pre_kernel, size),
        "norm_qkv",
        [
            ((tok_rows, width), BF), ((tok_rows, 2 * kv_width), BF), ((a_rows, tok_rows), BF),
            ((1, size.flat), F32),
        ],
        [((a_rows, size.a_width), BF), ((tok_rows, size.a_width), F32)],
        3,
        (me, tokens, a_mine, a_other, cos, sin),
        16,
    )
    kv_got = blocks.swap(kv_mine, blocks.x)
    own = attention_own(q_rot, kv_mine, info, docs)
    z2, x1 = tie(z2, x1, kv_mine)[:2]
    y2 = jnp.stack([z2, blocks.swap(z2, blocks.y)])
    b1_parts = [b.reshape(half // 2 * MAIN, -1) for b in (x1, blocks.swap(x1, blocks.y))]
    b2_parts = [b.reshape(half // 2 * MAIN, -1) for b in (y2, blocks.swap(y2, blocks.x))]
    attn, lse = attention_others(q_rot, kv_got, *own, info, docs)

    b1_parts[1:] = [b1_parts[1], blocks.swap(b1_parts[0], blocks.core)]
    b2_parts[1:] = [b2_parts[1], blocks.swap(b2_parts[0], blocks.core)]
    attn, b2_parts[1] = tie(attn, b2_parts[1])
    attn, b1_parts[1] = tie(attn, b1_parts[1])
    b2_parts.append(blocks.swap(b2_parts[1], blocks.core))
    b1_parts.append(blocks.swap(b1_parts[1], blocks.core))
    main = size.count * MAIN
    slots = main + size.count * TAIL
    layer_out, keep1, give1, keep2, give2, grad_mid, grad_attn, grad_gain, delta = call(
        functools.partial(mlp_kernel, size),
        "feed_forward",
        [
            ((width, tok_rows), BF),
            ((main // 2, size.back_first), BF), ((main // 2, size.back_first), BF),
            ((main // 2, size.back_second), BF), ((main // 2, size.back_second), BF),
            ((tok_rows, width), F32), ((tok_rows, width), BF), ((1, width), F32),
            ((width // HEAD_DIM, 1, tok_rows), F32),
        ],
        [
            ((slots, ff), BF), ((slots, ff), BF), ((slots, size.wide), BF), ((ff, size.wide), BF),
            ((tok_rows, width), F32), ((tok_rows, slots), BF), ((slots, tok_rows), BF),
            ((width, slots), BF), ((tok_rows, width), F32), ((tok_rows, slots), F32),
            ((ff, size.wide), BF), ((size.count * TAIL, 2 * ff), BF),
            ((size.count * TAIL, size.wide), BF), ((main, size.piece + 128), BF),
        ],
        21,
        (
            me, attn, tokens, cotangent, flat, *b1_parts, *b2_parts,
        ),
        28,
    )

    got1 = blocks.swap(give1, blocks.core)
    got2 = blocks.swap(give2, blocks.core)
    shape = (2, 2, blocks.zs, MAIN, -1)
    h1 = blocks.add(keep1, got1).reshape(shape)
    h2 = blocks.add(keep2, got2).reshape(shape)
    dq_others, give_kv = attention_grad(q_rot, kv_got, grad_attn, lse, delta, info, docs)
    got_kv = blocks.swap(give_kv, blocks.x)
    dq_others, h1, h2 = tie(dq_others, h1, h2)
    h1 = blocks.add(h1[0], blocks.swap(h1[1], blocks.y))
    h2 = blocks.add(h2[:, 0], blocks.swap(h2[:, 1], blocks.x))
    grad_q_rot, own_kv = attention_grad(
        q_rot, kv_mine, grad_attn, lse, delta, info, docs, dq_others
    )
    got_kv, h1, h2 = tie(got_kv, h1, h2)
    h1 = blocks.add(h1[0], blocks.swap(h1[1], blocks.x))
    h2 = blocks.add(h2[0], blocks.swap(h2[1], blocks.y))

    gx, keep_a, give_a = call(
        functools.partial(post_kernel, size),
        "norm_qkv_back",
        [
            ((width, tok_rows), F32), ((a_rows // 2, size.a_width), BF),
            ((a_rows // 2, size.a_width), BF),
        ],
        [
            ((tok_rows, width + kv_width), F32), ((tok_rows, size.a_width), BF),
            ((1, size.flat), F32),
        ],
        6,
        (
            me, grad_q_rot, own_kv, got_kv, cos, sin, n1t, a_mine,
            a_other, tokens, grad_mid, flat, grad_gain,
        ),
        24,
    )
    held = blocks.add(keep_a, blocks.swap(give_a, blocks.core))
    held, h2 = tie(held, h2)
    held = held.reshape(2, 2, blocks.zs, size.tall, size.a_width)
    held = blocks.add(held[0], blocks.swap(held[1], blocks.y))
    held, share2, h1 = tie(held, blocks.sum_z(h2), h1)
    held = blocks.add(held[0], blocks.swap(held[1], blocks.x))
    held, share1 = tie(held, blocks.sum_z(h1))
    share_a = blocks.sum_z(held)

    tails = tail_unpack(share1[:, size.tail : size.tail + size.piece], 2 * ff)
    tail_o = tail_unpack(share1[:, size.tail_o : size.tail_o + 128], width)
    share_out = jnp.concatenate([share1[:, size.out : size.out + width], tail_o], axis=0)
    share_gate = jnp.concatenate([share1[:, :ff], tails[:, :ff]], axis=0)
    share_up = jnp.concatenate([share2[:, :ff], tails[:, ff:]], axis=0)
    downs = [size.down_back_at(c) for c in range(size.downs)]
    share_down = jnp.concatenate(
        [(share1, share2)[which][:, at : at + width] for which, at in downs], axis=0
    )
    ends = (width, width + kv_width, size.qkv)
    return (
        layer_out.T, gx.T, share_a[:rows, : ends[0]].reshape(-1),
        share_a[:rows, ends[0] : ends[1]].reshape(-1),
        share_a[:rows, ends[1] : ends[2]].reshape(-1),
        share_out.reshape(-1), share_gate.reshape(-1), share_up.reshape(-1),
        share_down.reshape(-1), share_a[rows, : size.vec],
    )


def local(
    tokens, q_weight, k_weight, v_weight, o_weight, gate_weight, up_weight, down_weight,
    vectors, doc_lengths, cotangent,
):
    tok_rows, width = tokens.shape
    ctx_count = lax.axis_size("ctx")
    dp_count = lax.axis_size("dp")
    count = dp_count * ctx_count
    seq_tokens = tok_rows * ctx_count
    ctx_index = lax.axis_index("ctx")
    heads = width // HEAD_DIM
    kv_width = KV_HEADS * HEAD_DIM
    ff = gate_weight.shape[0] * count // width

    position_all = doc_layout(doc_lengths[0], seq_tokens)
    offset = ctx_index * tok_rows
    position_mine = lax.dynamic_slice_in_dim(position_all, offset, tok_rows)
    docs = doc_lengths.shape[1]
    others = (ctx_count - 1 - ctx_index) * tok_rows
    heads_of = jnp.stack([ctx_index, others, offset]).astype(jnp.int32)
    info = jnp.concatenate([heads_of, jnp.cumsum(doc_lengths[0])[:-1].astype(jnp.int32)])
    half = HEAD_DIM // 2
    freq = THETA ** (-jnp.arange(half, dtype=F32) * 2.0 / HEAD_DIM)
    position_f = position_mine.astype(F32)[:, None]

    whole_rows = width % count == 0 and ff % count == 0
    if whole_rows and ctx_count == 2 and dp_count % 4 == 0 and count & (count - 1) == 0:
        size = Sizes(width, ff, dp_count, ctx_count, vectors.shape[0], kv_width)
        if size.fits() and (width + kv_width) % 128 == 0:
            angle = position_f * jnp.tile(freq, 128 // half)[None, :]
            sign = np.where(np.arange(128) % HEAD_DIM < half, -1.0, 1.0).astype(np.float32)
            pos = (info, docs, jnp.cos(angle), jnp.sin(angle) * sign)
            args = (
                tokens, q_weight, k_weight, v_weight, o_weight, gate_weight, up_weight,
                down_weight, vectors, cotangent,
            )
            return local_blocks(size, Blocks(dp_count, ctx_count), pos, args)

    angle = position_f * freq[None, :]
    cosine = jnp.cos(angle)[:, None, :]
    sine = jnp.sin(angle)[:, None, :]
    inputs = tokens.astype(F32)
    inv_first = lax.rsqrt(jnp.mean(inputs * inputs, axis=-1, keepdims=True) + EPS)

    def whole(part):
        return lax.all_gather(part, AXES, axis=0, tiled=True)

    w_qkv = jnp.concatenate(
        [whole(w).reshape(width, -1) for w in (q_weight, k_weight, v_weight)], axis=1
    )
    w_out = whole(o_weight).reshape(width, width)
    w_gate = whole(gate_weight).reshape(width, ff)
    w_up = whole(up_weight).reshape(width, ff)
    w_down = whole(down_weight).reshape(ff, width)
    flat = whole(vectors).astype(F32)
    ends = [width, width + kv_width, width + 2 * kv_width, 2 * width + 2 * kv_width]
    gain_attn = flat[ends[2] : ends[3]]
    gain_mlp = flat[ends[3] : ends[3] + width]

    n_first = (inputs * inv_first * gain_attn).astype(BF)
    qkv = times(n_first, w_qkv) + flat[: ends[2]]
    q_rot = turn(qkv[:, :width].reshape(tok_rows, heads, HEAD_DIM), cosine, sine)
    q_rot = q_rot.astype(BF).reshape(tok_rows, width)
    k_rot = turn(qkv[:, width : ends[1]].reshape(tok_rows, KV_HEADS, HEAD_DIM), cosine, sine)
    k_rot = k_rot.astype(BF).reshape(tok_rows, kv_width)
    kv_mine = jnp.concatenate([k_rot, qkv[:, ends[1] :].astype(BF)], axis=1)
    kv = (lax.all_gather(kv_mine, "ctx", axis=0, tiled=True),)
    info = info.at[0].set(1)
    attn, lse = attention(q_rot, kv, info, docs, seq_tokens, False)
    mid = inputs + times(attn, w_out)
    inv_second = lax.rsqrt(jnp.mean(mid * mid, axis=-1, keepdims=True) + EPS)
    n_second = (mid * inv_second * gain_mlp).astype(BF)
    gate = times(n_second, w_gate)
    up_val = times(n_second, w_up)
    sig = jax.nn.sigmoid(gate)
    act = gate * sig
    hidden = (act * up_val).astype(BF)
    layer_out = (mid + times(hidden, w_down)).astype(BF)

    grad_wdown = inner_rows(hidden, cotangent)
    grad_hidden = times_back(cotangent, w_down)
    grad_gate = (grad_hidden * up_val * (sig * (1.0 + gate * (1.0 - sig)))).astype(BF)
    grad_up = (grad_hidden * act).astype(BF)
    grad_wgate = inner_rows(n_second, grad_gate)
    grad_wup = inner_rows(n_second, grad_up)
    grad_n2 = times_back(grad_gate, w_gate) + times_back(grad_up, w_up)
    grad_mid_norm, grad_gain_mlp = norm_back(mid, inv_second, gain_mlp, grad_n2)
    grad_mid = cotangent.astype(F32) + grad_mid_norm
    grad_branch = grad_mid.astype(BF)
    grad_wout = inner_rows(attn, grad_branch)
    grad_attn = times_back(grad_branch, w_out).astype(BF)
    grad_q_rot, grad_kv = attention_back(
        q_rot, kv, grad_attn, lse, info, docs, seq_tokens, False, 0, KV_HEADS
    )
    grad_kv_mine = lax.psum_scatter(
        grad_kv.astype(BF), "ctx", scatter_dimension=0, tiled=True
    ).astype(F32)
    grad_q = turn(grad_q_rot.reshape(tok_rows, heads, HEAD_DIM), cosine, -sine)
    grad_k = turn(
        grad_kv_mine[:, :kv_width].reshape(tok_rows, KV_HEADS, HEAD_DIM), cosine, -sine
    )
    grad_qkv = jnp.concatenate(
        [
            grad_q.reshape(tok_rows, width).astype(BF),
            grad_k.reshape(tok_rows, kv_width).astype(BF),
            grad_kv_mine[:, kv_width:].astype(BF),
        ],
        axis=1,
    )
    grad_wqkv = inner_rows(n_first, grad_qkv)
    grad_bias = jnp.sum(grad_qkv.astype(F32), axis=0)
    grad_n1 = times_back(grad_qkv, w_qkv)
    grad_x_norm, grad_gain_attn = norm_back(inputs, inv_first, gain_attn, grad_n1)
    input_grad = grad_mid + grad_x_norm
    used = 3 * width + 2 * kv_width
    padding = jnp.zeros((vectors.shape[0] * count - used,), F32)
    vector_term = jnp.concatenate([grad_bias, grad_gain_attn, grad_gain_mlp, padding])

    def shares(term):
        return lax.psum_scatter(term.reshape(-1), AXES, scatter_dimension=0, tiled=True)

    return (
        layer_out, input_grad, shares(grad_wqkv[:, :width]),
        shares(grad_wqkv[:, width : ends[1]]), shares(grad_wqkv[:, ends[1] :]),
        shares(grad_wout), shares(grad_wgate), shares(grad_wup), shares(grad_wdown),
        shares(vector_term),
    )


def solution(mesh):
    split = P(AXES)
    rows = P(AXES, None)
    in_specs = (rows,) + (split,) * 8 + (P("dp", None), rows)
    out_specs = (rows, rows) + (split,) * 8
    return jax.shard_map(local, mesh=mesh, in_specs=in_specs, out_specs=out_specs, check_vma=False)
```

profile of v0, /device:TPU:0, one launch (start us, length us, event | category | flops | bytes accessed | tf_op | source)
XLA Modules:
  0.0 185.3 jit_solution(3833173959647868643)
XLA Ops:
  0.7 0.9 reshape.148
  1.6 0.8 reshape.149
  2.4 0.8 reshape.147
  3.3 0.7 fusion.17
  3.9 4.1 %collective-permute-start.1 = (bf16[24,1024]{1,0:T(8,128)(2,1)S(1)}, bf16[24,1024]{1,0:T(8,128)(2,1)S(1)}, u32[]{:S(2)}, u32[]{:S(2)}) collective-permute-start(bf16[24,1024]{1,0:T(8,128)(2,1)S(1)} %fusion.17), channel_id=1, source_target_pairs={{0,16},{1,17},{2,18},{3,19},{4,20},{5,21},{6,22},{7,23},{8,24},{9,... | collective-permute-start | bytes 147464 | tf_op jit(solution)/shard_map/ppermute | solution.py:483
  8.0 1.6 collective-permute-start
  9.6 0.8 reduce-window.4
  12.1 3.4 %collective-permute-done.2 = bf16[24,1024]{1,0:T(8,128)(2,1)S(1)} collective-permute-done((bf16[24,1024]{1,0:T(8,128)(2,1)S(1)}, bf16[24,1024]{1,0:T(8,128)(2,1)S(1)}, u32[]{:S(2)}, u32[]{:S(2)}) %collective-permute-start.2) | collective-permute-done | bytes 49184 | tf_op jit(solution)/shard_map/ppermute | solution.py:483
  15.5 1.6 collective-permute-start.3
  17.1 1.6 fusion.6
  19.2 0.9 wire.1
  20.1 1.2 collective-permute-done.3
  21.3 0.7 collective-permute-start.6
  22.0 3.7 %collective-permute-start.4 = (bf16[16,3328]{1,0:T(8,128)(2,1)S(1)}, bf16[16,3328]{1,0:T(8,128)(2,1)S(1)}, u32[]{:S(2)}, u32[]{:S(2)}) collective-permute-start(bf16[16,3328]{1,0:T(8,128)(2,1)S(1)} %get-tuple-element.76), channel_id=1, source_target_pairs={{0,8},{1,9},{2,10},{3,11},{4,12},{5,13},{6,14},{7,15},{8,0},{9,1},... | collective-permute-start | bytes 319496 | tf_op jit(solution)/shard_map/ppermute | solution.py:483
  25.9 1.5 collective-permute-start.7
  27.4 0.7 collective-permute-done.6
  28.1 2.8 %collective-permute-done.5 = bf16[16,3328]{1,0:T(8,128)(2,1)S(1)} collective-permute-done((bf16[16,3328]{1,0:T(8,128)(2,1)S(1)}, bf16[16,3328]{1,0:T(8,128)(2,1)S(1)}, u32[]{:S(2)}, u32[]{:S(2)}) %collective-permute-start.5) | collective-permute-done | bytes 106528 | tf_op jit(solution)/shard_map/ppermute | solution.py:483
  30.9 2.7 %collective-permute-done.7 = bf16[2,4,24,1024]{3,2,1,0:T(8,128)(2,1)S(1)} collective-permute-done((bf16[2,4,24,1024]{3,2,1,0:T(8,128)(2,1)S(1)}, bf16[2,4,24,1024]{3,2,1,0:T(8,128)(2,1)S(1)}, u32[]{:S(2)}, u32[]{:S(2)}) %collective-permute-start.7) | collective-permute-done | bytes 393248 | tf_op jit(solution)/shard_map/ppermute | solution.py:483
  33.6 0.7 collective-permute-start.12
  34.4 0.7 collective-permute-start.11
  35.1 2.9 %collective-permute-start.10 = (bf16[16,2816]{1,0:T(8,128)(2,1)S(1)}, bf16[16,2816]{1,0:T(8,128)(2,1)S(1)}, u32[]{:S(2)}, u32[]{:S(2)}) collective-permute-start(bf16[16,2816]{1,0:T(8,128)(2,1)S(1)} %get-tuple-element.85), channel_id=1, source_target_pairs={{0,8},{1,9},{2,10},{3,11},{4,12},{5,13},{6,14},{7,15},{8,0},{9,1},... | collective-permute-start | bytes 270344 | tf_op jit(solution)/shard_map/ppermute | solution.py:483
  38.0 1.5 collective-permute-start.13
  40.1 1.6 collective-permute-done.11
  41.8 4.4 %collective-permute-done.13 = bf16[4,16,3328]{2,1,0:T(8,128)(2,1)S(1)} collective-permute-done((bf16[4,16,3328]{2,1,0:T(8,128)(2,1)S(1)}, bf16[4,16,3328]{2,1,0:T(8,128)(2,1)S(1)}, u32[]{:S(2)}, u32[]{:S(2)}) %collective-permute-start.13) | collective-permute-done | bytes 426016 | tf_op jit(solution)/shard_map/ppermute | solution.py:483
  46.2 2.7 %norm_qkv.1 = (bf16[512,576]{1,0:T(8,128)(2,1)S(1)}, bf16[512,384]{1,0:T(8,128)(2,1)S(1)}, bf16[768,512]{1,0:T(8,128)(2,1)S(1)}, f32[1,2304]{1,0:T(1,128)S(1)}) custom-call(s32[1]{0:T(128)} %bitcast.me_ref, bf16[512,576]{1,0:T(8,128)(2,1)S(1)} %get-tuple-element.72.x_ref, bf16[384,1024]{1,0:T(8,128)(2,1)S(1)} %bitcast.117, ...), custom_call_target="tpu_custom_call" | custom-call | flops 3300000000 | bytes 1048576 | tf_op jit(solution)/shard_map/norm_qkv/pallas_call | solution.py:848
  49.0 1.6 collective-permute-start.9
  50.5 1.5 collective-permute-start.14
  52.5 6.5 %attn_own.1 = (f32[576,512]{1,0:T(8,128)S(1)}, f32[9,1,512]{2,1,0:T(1,128)S(1)}, f32[9,1,512]{2,1,0:T(1,128)S(1)}) custom-call(s32[6]{0:T(128)S(1)} %pad_add_fusion.info, bf16[512,576]{1,0:T(8,128)(2,1)S(1)} %get-tuple-element.79.q_ref, bf16[512,384]{1,0:T(8,128)(2,1)S(1)} %get-tuple-element.80.kv_ref), custom_call_target="tpu_custom_call" | custom-call | flops 6600000000 | bytes 1048576 | tf_op jit(solution)/shard_map/attn_own/pallas_call | solution.py:361
  59.0 2.8 %collective-permute-done.14 = bf16[4,16,2816]{2,1,0:T(8,128)(2,1)S(1)} collective-permute-done((bf16[4,16,2816]{2,1,0:T(8,128)(2,1)S(1)}, bf16[4,16,2816]{2,1,0:T(8,128)(2,1)S(1)}, u32[]{:S(2)}, u32[]{:S(2)}) %collective-permute-start.14) | collective-permute-done | bytes 360480 | tf_op jit(solution)/shard_map/ppermute | solution.py:483
  62.5 1.1 attn_others.1
  63.6 14.1 %collective-permute-done.15 = bf16[2,4,16,2816]{3,2,1,0:T(8,128)(2,1)S(1)} collective-permute-done((bf16[2,4,16,2816]{3,2,1,0:T(8,128)(2,1)S(1)}, bf16[2,4,16,2816]{3,2,1,0:T(8,128)(2,1)S(1)}, u32[]{:S(2)}, u32[]{:S(2)}) %collective-permute-start.15) | collective-permute-done | bytes 720928 | tf_op jit(solution)/shard_map/ppermute | solution.py:483
  78.2 2.9 %collective-permute-done.19.b2_10 = bf16[128,2816]{1,0:T(8,128)(2,1)S(1)} collective-permute-done((bf16[128,2816]{1,0:T(8,128)(2,1)S(1)}, bf16[128,2816]{1,0:T(8,128)(2,1)S(1)}, u32[]{:S(2)}, u32[]{:S(2)}) %collective-permute-start.19) | collective-permute-done | bytes 720928 | tf_op jit(solution)/shard_map/ppermute | solution.py:483
  81.1 1.0 collective-permute-done.20.b2_11
  82.2 19.1 %feed_forward.1 = (bf16[576,512]{1,0:T(8,128)(2,1)}, bf16[256,3968]{1,0:T(8,128)(2,1)S(1)}, bf16[256,3968]{1,0:T(8,128)(2,1)S(1)}, bf16[256,2176]{1,0:T(8,128)(2...) custom-call(s32[1]{0:T(128)} %bitcast.me_ref, ...), custom_call_target="tpu_custom_call" | custom-call | flops 23100000256 | bytes 1048576 | tf_op jit(solution)/shard_map/feed_forward/pallas_call | solution.py:848
  101.7 1.2 attn_grad_others.1
  102.9 9.6 %collective-permute-start.23 = (bf16[512,384]{1,0:T(8,128)(2,1)S(1)}, bf16[512,384]{1,0:T(8,128)(2,1)S(1)}, u32[]{:S(2)}, u32[]{:S(2)}) collective-permute-start(bf16[512,384]{1,0:T(8,128)(2,1)S(1)} %get-tuple-element.107), channel_id=1, source_target_pairs={{0,1},{1,0},{2,3},{3,2},{4,5},{5,4},{6,7},{7,6},{8,9},{9,8},{10,11... | collective-permute-start | bytes 1179656 | tf_op jit(solution)/shard_map/ppermute | solution.py:483
  113.6 1.6 collective-permute-start.24
  115.2 9.1 %attn_grad_own.1 = (f32[512,576]{1,0:T(8,128)S(1)}, f32[512,384]{1,0:T(8,128)S(1)}) custom-call(s32[6]{0:T(128)S(1)} %pad_add_fusion.info, bf16[512,576]{1,0:T(8,128)(2,1)S(1)} %get-tuple-element.79.q_ref, bf16[512,384]{1,0:T(8,128)(2,1)S(1)} %get-tuple-element.80.kv_ref, bf16[512,576]{1,0:T(8,128)(2,1)S(1)} %get-tuple-element.96.do_ref, ...), custom_call_target="tpu_custom_call" | custom-call | flops 9900000256 | bytes 1048576 | tf_op jit(solution)/shard_map/attn_grad_own/pallas_call | solution.py:394
  124.3 9.6 %collective-permute-done.25 = bf16[2,4,16,2176]{3,2,1,0:T(8,128)(2,1)S(1)} collective-permute-done((bf16[2,4,16,2176]{3,2,1,0:T(8,128)(2,1)S(1)}, bf16[2,4,16,2176]{3,2,1,0:T(8,128)(2,1)S(1)}, u32[]{:S(2)}, u32[]{:S(2)}) %collective-permute-start.25) | collective-permute-done | bytes 557088 | tf_op jit(solution)/shard_map/ppermute | solution.py:483
  134.1 3.8 %collective-permute-done.24 = bf16[2,4,16,3968]{3,2,1,0:T(8,128)(2,1)S(1)} collective-permute-done((bf16[2,4,16,3968]{3,2,1,0:T(8,128)(2,1)S(1)}, bf16[2,4,16,3968]{3,2,1,0:T(8,128)(2,1)S(1)}, u32[]{:S(2)}, u32[]{:S(2)}) %collective-permute-start.24) | collective-permute-done | bytes 1015840 | tf_op jit(solution)/shard_map/ppermute | solution.py:483
  138.2 1.6 collective-permute-start.27
  139.8 1.8 collective-permute-start.32
  141.6 5.1 %norm_qkv_back.1 = (f32[576,512]{1,0:T(8,128)}, bf16[384,1024]{1,0:T(8,128)(2,1)S(1)}, bf16[384,1024]{1,0:T(8,128)(2,1)S(1)}) custom-call(s32[1]{0:T(128)} %bitcast.me_ref, f32[512,576]{1,0:T(8,128)S(1)} %get-tuple-element.105.dq_ref, f32[512,384]{1,0:T(8,128)S(1)} %get-tuple-element.106.dkv_ref, bf16[512,384]{1,0:T(8,128)(2,1)S(1)} %collective-permute-done.23.got_ref, ...), custom_call_target="tpu_custom_call" | custom-call | flops 6600000000 | bytes 1048576 | tf_op jit(solution)/shard_map/norm_qkv_back/pallas_call | solution.py:848
  146.7 5.3 %collective-permute-done.32 = bf16[4,16,3968]{2,1,0:T(8,128)(2,1)S(1)} collective-permute-done((bf16[4,16,3968]{2,1,0:T(8,128)(2,1)S(1)}, bf16[4,16,3968]{2,1,0:T(8,128)(2,1)S(1)}, u32[]{:S(2)}, u32[]{:S(2)}) %collective-permute-start.32) | collective-permute-done | bytes 507936 | tf_op jit(solution)/shard_map/ppermute | solution.py:483
  152.6 1.5 collective-permute-start.31
  154.0 2.0 %collective-permute-start.30 = (bf16[16,2176]{1,0:T(8,128)(2,1)S(1)}, bf16[16,2176]{1,0:T(8,128)(2,1)S(1)}, u32[]{:S(2)}, u32[]{:S(2)}) collective-permute-start(bf16[16,2176]{1,0:T(8,128)(2,1)S(1)} %get-tuple-element.133), channel_id=1, source_target_pairs={{0,16},{1,17},{2,18},{3,19},{4,20},{5,21},{6,22},{7,23},{8,24},{9,... | collective-permute-start | bytes 208904 | tf_op jit(solution)/shard_map/ppermute | solution.py:483
  156.7 0.7 collective-permute-done.29
  157.4 1.5 collective-permute-done.31
  158.8 1.7 collective-permute-done.30
  160.6 3.5 %collective-permute-done.28 = bf16[2,4,24,1024]{3,2,1,0:T(8,128)(2,1)S(1)} collective-permute-done((bf16[2,4,24,1024]{3,2,1,0:T(8,128)(2,1)S(1)}, bf16[2,4,24,1024]{3,2,1,0:T(8,128)(2,1)S(1)}, u32[]{:S(2)}, u32[]{:S(2)}) %collective-permute-start.28) | collective-permute-done | bytes 393248 | tf_op jit(solution)/shard_map/ppermute | solution.py:483
  164.3 1.3 collective-permute-start.34
  165.6 1.1 collective-permute-start.36
  166.8 1.1 collective-permute-start.35
  167.9 1.3 collective-permute-start.33
  169.2 1.0 collective-permute-done.34
  170.2 2.2 %collective-permute-done.36 = bf16[16,3968]{1,0:T(8,128)(2,1)S(1)} collective-permute-done((bf16[16,3968]{1,0:T(8,128)(2,1)S(1)}, bf16[16,3968]{1,0:T(8,128)(2,1)S(1)}, u32[]{:S(2)}, u32[]{:S(2)}) %collective-permute-start.36) | collective-permute-done | bytes 127008 | tf_op jit(solution)/shard_map/ppermute | solution.py:483
  172.5 2.9 %collective-permute-done.35 = bf16[16,3968]{1,0:T(8,128)(2,1)S(1)} collective-permute-done((bf16[16,3968]{1,0:T(8,128)(2,1)S(1)}, bf16[16,3968]{1,0:T(8,128)(2,1)S(1)}, u32[]{:S(2)}, u32[]{:S(2)}) %collective-permute-start.35) | collective-permute-done | bytes 127008 | tf_op jit(solution)/shard_map/ppermute | solution.py:483
  176.0 1.6 collective-permute-start.39
  177.6 1.5 collective-permute-start.38
  179.2 0.7 reshape.173
  180.0 0.7 reshape.168
  183.3 0.7 reshape.163
  184.0 0.7 reshape.165
  184.7 0.7 reshape.164
  (111 shorter events, 11.4 us)
Async XLA Ops:
  0.6 18.2 %copy-start.3 = (bf16[27648]{0:T(1024)(128)(2,1)S(1)}, bf16[27648]{0:T(1024)(128)(2,1)}, u32[]{:S(2)}) copy-start(bf16[27648]{0:T(1024)(128)(2,1)} %param.19) | copy-start | bytes 165892
  0.7 18.4 %copy-start.5 = (bf16[27648]{0:T(1024)(128)(2,1)S(1)}, bf16[27648]{0:T(1024)(128)(2,1)}, u32[]{:S(2)}) copy-start(bf16[27648]{0:T(1024)(128)(2,1)} %param.18) | copy-start | bytes 165892
  0.7 18.3 %copy-start.4 = (bf16[27648]{0:T(1024)(128)(2,1)S(1)}, bf16[27648]{0:T(1024)(128)(2,1)}, u32[]{:S(2)}) copy-start(bf16[27648]{0:T(1024)(128)(2,1)} %param.17) | copy-start | bytes 165892
  0.7 18.1 %copy-start.6 = (bf16[10368]{0:T(1024)(128)(2,1)S(1)}, bf16[10368]{0:T(1024)(128)(2,1)}, u32[]{:S(2)}) copy-start(bf16[10368]{0:T(1024)(128)(2,1)} %param.16) | copy-start | bytes 62212
  0.7 18.5 %copy-start.1 = (bf16[512,576]{0,1:T(8,128)(2,1)S(1)}, bf16[512,576]{0,1:T(8,128)(2,1)}, u32[]{:S(2)}) copy-start(bf16[512,576]{0,1:T(8,128)(2,1)} %param.22) | copy-start | bytes 1769476
  0.7 18.5 %copy-start = (bf16[512,576]{0,1:T(8,128)(2,1)S(1)}, bf16[512,576]{0,1:T(8,128)(2,1)}, u32[]{:S(2)}) copy-start(bf16[512,576]{0,1:T(8,128)(2,1)} %param.12) | copy-start | bytes 1769476
  3.9 8.2 %collective-permute-start.1 = (bf16[24,1024]{1,0:T(8,128)(2,1)S(1)}, bf16[24,1024]{1,0:T(8,128)(2,1)S(1)}, u32[]{:S(2)}, u32[]{:S(2)}) collective-permute-start(bf16[24,1024]{1,0:T(8,128)(2,1)S(1)} %fusion.17), channel_id=1, source_target_pairs={{0,16},{1,17},{2,18},{3,19},{4,20},{5,21},{6,22},{7,23},{8,24},{9,... | collective-permute-start | bytes 147464 | tf_op jit(solution)/shard_map/ppermute | solution.py:483
  8.0 4.1 %collective-permute-start = (bf16[24,1024]{1,0:T(8,128)(2,1)S(1)}, bf16[24,1024]{1,0:T(8,128)(2,1)S(1)}, u32[]{:S(2)}, u32[]{:S(2)}) collective-permute-start(bf16[24,1024]{1,0:T(8,128)(2,1)S(1)} %fusion.17), channel_id=1, source_target_pairs={{0,8},{1,9},{2,10},{3,11},{4,12},{5,13},{6,14},{7,15},{8,0},{9,1},... | collective-permute-start | bytes 147464 | tf_op jit(solution)/shard_map/ppermute | solution.py:483
  9.6 5.9 %collective-permute-start.2 = (bf16[24,1024]{1,0:T(8,128)(2,1)S(1)}, bf16[24,1024]{1,0:T(8,128)(2,1)S(1)}, u32[]{:S(2)}, u32[]{:S(2)}) collective-permute-start(bf16[24,1024]{1,0:T(8,128)(2,1)S(1)} %fusion.17), channel_id=1, source_target_pairs={{0,24},{1,25},{2,26},{3,27},{4,28},{5,29},{6,30},{7,31},{8,16},{9,... | collective-permute-start | bytes 147464 | tf_op jit(solution)/shard_map/ppermute | solution.py:483
  15.5 5.7 %collective-permute-start.3 = (bf16[4,24,1024]{2,1,0:T(8,128)(2,1)S(1)}, bf16[4,24,1024]{2,1,0:T(8,128)(2,1)S(1)}, u32[]{:S(2)}, u32[]{:S(2)}) collective-permute-start(bf16[4,24,1024]{2,1,0:T(8,128)(2,1)S(1)} %get-tuple-element.141), channel_id=1, source_target_pairs={{0,1},{1,0},{2,3},{3,2},{4,5},{5,4},{6,7},{7,6},{8,9},{9,8},{10,11... | collective-permute-start | bytes 589832 | tf_op jit(solution)/shard_map/ppermute | solution.py:483
  21.3 6.7 %collective-permute-start.6 = (bf16[16,3328]{1,0:T(8,128)(2,1)S(1)}, bf16[16,3328]{1,0:T(8,128)(2,1)S(1)}, u32[]{:S(2)}, u32[]{:S(2)}) collective-permute-start(bf16[16,3328]{1,0:T(8,128)(2,1)S(1)} %get-tuple-element.76), channel_id=1, source_target_pairs={{0,24},{1,25},{2,26},{3,27},{4,28},{5,29},{6,30},{7,31},{8,16},{9,... | collective-permute-start | bytes 319496 | tf_op jit(solution)/shard_map/ppermute | solution.py:483
  22.0 8.8 %collective-permute-start.5 = (bf16[16,3328]{1,0:T(8,128)(2,1)S(1)}, bf16[16,3328]{1,0:T(8,128)(2,1)S(1)}, u32[]{:S(2)}, u32[]{:S(2)}) collective-permute-start(bf16[16,3328]{1,0:T(8,128)(2,1)S(1)} %get-tuple-element.76), channel_id=1, source_target_pairs={{0,16},{1,17},{2,18},{3,19},{4,20},{5,21},{6,22},{7,23},{8,24},{9,... | collective-permute-start | bytes 319496 | tf_op jit(solution)/shard_map/ppermute | solution.py:483
  22.0 8.8 %collective-permute-start.4 = (bf16[16,3328]{1,0:T(8,128)(2,1)S(1)}, bf16[16,3328]{1,0:T(8,128)(2,1)S(1)}, u32[]{:S(2)}, u32[]{:S(2)}) collective-permute-start(bf16[16,3328]{1,0:T(8,128)(2,1)S(1)} %get-tuple-element.76), channel_id=1, source_target_pairs={{0,8},{1,9},{2,10},{3,11},{4,12},{5,13},{6,14},{7,15},{8,0},{9,1},... | collective-permute-start | bytes 319496 | tf_op jit(solution)/shard_map/ppermute | solution.py:483
  25.9 7.8 %collective-permute-start.7 = (bf16[2,4,24,1024]{3,2,1,0:T(8,128)(2,1)S(1)}, bf16[2,4,24,1024]{3,2,1,0:T(8,128)(2,1)S(1)}, u32[]{:S(2)}, u32[]{:S(2)}) collective-permute-start(bf16[2,4,24,1024]{3,2,1,0:T(8,128)(2,1)S(1)} %pad_maximum_fusion.4), channel_id=1, source_target_pairs={{0,4},{1,5},{2,6},{3,7},{4,0},{5,1},{6,2},{7,3},{8,12},{9,13},{10,... | collective-permute-start | bytes 1179656 | tf_op jit(solution)/shard_map/ppermute | solution.py:483
  33.6 6.5 %collective-permute-start.12 = (bf16[16,2816]{1,0:T(8,128)(2,1)S(1)}, bf16[16,2816]{1,0:T(8,128)(2,1)S(1)}, u32[]{:S(2)}, u32[]{:S(2)}) collective-permute-start(bf16[16,2816]{1,0:T(8,128)(2,1)S(1)} %get-tuple-element.85), channel_id=1, source_target_pairs={{0,24},{1,25},{2,26},{3,27},{4,28},{5,29},{6,30},{7,31},{8,16},{9,... | collective-permute-start | bytes 270344 | tf_op jit(solution)/shard_map/ppermute | solution.py:483
  34.4 7.4 %collective-permute-start.11 = (bf16[16,2816]{1,0:T(8,128)(2,1)S(1)}, bf16[16,2816]{1,0:T(8,128)(2,1)S(1)}, u32[]{:S(2)}, u32[]{:S(2)}) collective-permute-start(bf16[16,2816]{1,0:T(8,128)(2,1)S(1)} %get-tuple-element.85), channel_id=1, source_target_pairs={{0,16},{1,17},{2,18},{3,19},{4,20},{5,21},{6,22},{7,23},{8,24},{9,... | collective-permute-start | bytes 270344 | tf_op jit(solution)/shard_map/ppermute | solution.py:483
  35.1 6.6 %collective-permute-start.10 = (bf16[16,2816]{1,0:T(8,128)(2,1)S(1)}, bf16[16,2816]{1,0:T(8,128)(2,1)S(1)}, u32[]{:S(2)}, u32[]{:S(2)}) collective-permute-start(bf16[16,2816]{1,0:T(8,128)(2,1)S(1)} %get-tuple-element.85), channel_id=1, source_target_pairs={{0,8},{1,9},{2,10},{3,11},{4,12},{5,13},{6,14},{7,15},{8,0},{9,1},... | collective-permute-start | bytes 270344 | tf_op jit(solution)/shard_map/ppermute | solution.py:483
  38.0 8.1 %collective-permute-start.13 = (bf16[4,16,3328]{2,1,0:T(8,128)(2,1)S(1)}, bf16[4,16,3328]{2,1,0:T(8,128)(2,1)S(1)}, u32[]{:S(2)}, u32[]{:S(2)}) collective-permute-start(bf16[4,16,3328]{2,1,0:T(8,128)(2,1)S(1)} %pad_maximum_fusion.3), channel_id=1, source_target_pairs={{0,1},{1,0},{2,3},{3,2},{4,5},{5,4},{6,7},{7,6},{8,9},{9,8},{10,11... | collective-permute-start | bytes 1277960 | tf_op jit(solution)/shard_map/ppermute | solution.py:483
  39.6 6.6 %collective-permute-start.8 = (bf16[384,1024]{1,0:T(8,128)(2,1)S(1)}, bf16[384,1024]{1,0:T(8,128)(2,1)S(1)}, u32[]{:S(2)}, u32[]{:S(2)}) collective-permute-start(bf16[384,1024]{1,0:T(8,128)(2,1)S(1)} %bitcast.116), channel_id=1, source_target_pairs={{0,2},{1,3},{2,0},{3,1},{4,6},{5,7},{6,4},{7,5},{8,10},{9,11},{10,... | collective-permute-start | bytes 2359304 | tf_op jit(solution)/shard_map/ppermute | solution.py:483
  49.0 13.6 %collective-permute-start.9 = (bf16[512,384]{1,0:T(8,128)(2,1)S(1)}, bf16[512,384]{1,0:T(8,128)(2,1)S(1)}, u32[]{:S(2)}, u32[]{:S(2)}) collective-permute-start(bf16[512,384]{1,0:T(8,128)(2,1)S(1)} %get-tuple-element.80.kv_ref), channel_id=1, source_target_pairs={{0,1},{1,0},{2,3},{3,2},{4,5},{5,4},{6,7},{7,6},{8,9},{9,8},{10,11... | collective-permute-start | bytes 1179656 | tf_op jit(solution)/shard_map/ppermute | solution.py:483
  50.5 11.4 %collective-permute-start.14 = (bf16[4,16,2816]{2,1,0:T(8,128)(2,1)S(1)}, bf16[4,16,2816]{2,1,0:T(8,128)(2,1)S(1)}, u32[]{:S(2)}, u32[]{:S(2)}) collective-permute-start(bf16[4,16,2816]{2,1,0:T(8,128)(2,1)S(1)} %pad_maximum_fusion.5), channel_id=1, source_target_pairs={{0,4},{1,5},{2,6},{3,7},{4,0},{5,1},{6,2},{7,3},{8,12},{9,13},{10,... | collective-permute-start | bytes 1081352 | tf_op jit(solution)/shard_map/ppermute | solution.py:483
  52.0 25.7 %collective-permute-start.16 = (bf16[2,4,16,3328]{3,2,1,0:T(8,128)(2,1)S(1)}, bf16[2,4,16,3328]{3,2,1,0:T(8,128)(2,1)S(1)}, u32[]{:S(2)}, u32[]{:S(2)}) collective-permute-start(bf16[2,4,16,3328]{3,2,1,0:T(8,128)(2,1)S(1)} %pad_maximum_fusion), channel_id=1, source_target_pairs={{0,4},{1,5},{2,6},{3,7},{4,0},{5,1},{6,2},{7,3},{8,12},{9,13},{10,... | collective-permute-start | bytes 2555912 | tf_op jit(solution)/shard_map/ppermute | solution.py:483
  52.5 25.7 %collective-permute-start.17 = (bf16[128,3328]{1,0:T(8,128)(2,1)S(1)}, bf16[128,3328]{1,0:T(8,128)(2,1)S(1)}, u32[]{:S(2)}, u32[]{:S(2)}) collective-permute-start(bf16[128,3328]{1,0:T(8,128)(2,1)S(1)} %bitcast.114), channel_id=1, source_target_pairs={{0,2},{1,3},{2,0},{3,1},{4,6},{5,7},{6,4},{7,5},{8,10},{9,11},{10,... | collective-permute-start | bytes 2555912 | tf_op jit(solution)/shard_map/ppermute | solution.py:483
  61.9 15.8 %collective-permute-start.15 = (bf16[2,4,16,2816]{3,2,1,0:T(8,128)(2,1)S(1)}, bf16[2,4,16,2816]{3,2,1,0:T(8,128)(2,1)S(1)}, u32[]{:S(2)}, u32[]{:S(2)}) collective-permute-start(bf16[2,4,16,2816]{3,2,1,0:T(8,128)(2,1)S(1)} %pad_maximum_fusion.2), channel_id=1, source_target_pairs={{0,1},{1,0},{2,3},{3,2},{4,5},{5,4},{6,7},{7,6},{8,9},{9,8},{10,11... | collective-permute-start | bytes 2162696 | tf_op jit(solution)/shard_map/ppermute | solution.py:483
  77.7 4.4 %collective-permute-start.18 = (bf16[128,3328]{1,0:T(8,128)(2,1)S(1)}, bf16[128,3328]{1,0:T(8,128)(2,1)S(1)}, u32[]{:S(2)}, u32[]{:S(2)}) collective-permute-start(bf16[128,3328]{1,0:T(8,128)(2,1)S(1)} %bitcast.123), channel_id=1, source_target_pairs={{0,2},{1,3},{2,0},{3,1},{4,6},{5,7},{6,4},{7,5},{8,10},{9,11},{10,... | collective-permute-start | bytes 2555912 | tf_op jit(solution)/shard_map/ppermute | solution.py:483
  77.7 3.4 %collective-permute-start.19 = (bf16[128,2816]{1,0:T(8,128)(2,1)S(1)}, bf16[128,2816]{1,0:T(8,128)(2,1)S(1)}, u32[]{:S(2)}, u32[]{:S(2)}) collective-permute-start(bf16[128,2816]{1,0:T(8,128)(2,1)S(1)} %bitcast.119), channel_id=1, source_target_pairs={{0,2},{1,3},{2,0},{3,1},{4,6},{5,7},{6,4},{7,5},{8,10},{9,11},{10,... | collective-permute-start | bytes 2162696 | tf_op jit(solution)/shard_map/ppermute | solution.py:483
  78.2 3.9 %collective-permute-start.20 = (bf16[128,2816]{1,0:T(8,128)(2,1)S(1)}, bf16[128,2816]{1,0:T(8,128)(2,1)S(1)}, u32[]{:S(2)}, u32[]{:S(2)}) collective-permute-start(bf16[128,2816]{1,0:T(8,128)(2,1)S(1)} %bitcast.125), channel_id=1, source_target_pairs={{0,2},{1,3},{2,0},{3,1},{4,6},{5,7},{6,4},{7,5},{8,10},{9,11},{10,... | collective-permute-start | bytes 2162696 | tf_op jit(solution)/shard_map/ppermute | solution.py:483
  101.2 11.7 %collective-permute-start.21 = (bf16[256,3968]{1,0:T(8,128)(2,1)S(1)}, bf16[256,3968]{1,0:T(8,128)(2,1)S(1)}, u32[]{:S(2)}, u32[]{:S(2)}) collective-permute-start(bf16[256,3968]{1,0:T(8,128)(2,1)S(1)} %get-tuple-element.101), channel_id=1, source_target_pairs={{0,2},{1,3},{2,0},{3,1},{4,6},{5,7},{6,4},{7,5},{8,10},{9,11},{10,... | collective-permute-start | bytes 6094856 | tf_op jit(solution)/shard_map/ppermute | solution.py:483
  101.4 11.2 %collective-permute-start.22 = (bf16[256,2176]{1,0:T(8,128)(2,1)S(1)}, bf16[256,2176]{1,0:T(8,128)(2,1)S(1)}, u32[]{:S(2)}, u32[]{:S(2)}) collective-permute-start(bf16[256,2176]{1,0:T(8,128)(2,1)S(1)} %get-tuple-element.103), channel_id=1, source_target_pairs={{0,2},{1,3},{2,0},{3,1},{4,6},{5,7},{6,4},{7,5},{8,10},{9,11},{10,... | collective-permute-start | bytes 3342344 | tf_op jit(solution)/shard_map/ppermute | solution.py:483
  102.9 35.2 %collective-permute-start.23 = (bf16[512,384]{1,0:T(8,128)(2,1)S(1)}, bf16[512,384]{1,0:T(8,128)(2,1)S(1)}, u32[]{:S(2)}, u32[]{:S(2)}) collective-permute-start(bf16[512,384]{1,0:T(8,128)(2,1)S(1)} %get-tuple-element.107), channel_id=1, source_target_pairs={{0,1},{1,0},{2,3},{3,2},{4,5},{5,4},{6,7},{7,6},{8,9},{9,8},{10,11... | collective-permute-start | bytes 1179656 | tf_op jit(solution)/shard_map/ppermute | solution.py:483
  113.4 20.5 %collective-permute-start.25 = (bf16[2,4,16,2176]{3,2,1,0:T(8,128)(2,1)S(1)}, bf16[2,4,16,2176]{3,2,1,0:T(8,128)(2,1)S(1)}, u32[]{:S(2)}, u32[]{:S(2)}) collective-permute-start(bf16[2,4,16,2176]{3,2,1,0:T(8,128)(2,1)S(1)} %slice_bitcast_fusion.2), channel_id=1, source_target_pairs={{0,1},{1,0},{2,3},{3,2},{4,5},{5,4},{6,7},{7,6},{8,9},{9,8},{10,11... | collective-permute-start | bytes 1671176 | tf_op jit(solution)/shard_map/ppermute | solution.py:483
  113.6 24.3 %collective-permute-start.24 = (bf16[2,4,16,3968]{3,2,1,0:T(8,128)(2,1)S(1)}, bf16[2,4,16,3968]{3,2,1,0:T(8,128)(2,1)S(1)}, u32[]{:S(2)}, u32[]{:S(2)}) collective-permute-start(bf16[2,4,16,3968]{3,2,1,0:T(8,128)(2,1)S(1)} %slice_bitcast_fusion), channel_id=1, source_target_pairs={{0,4},{1,5},{2,6},{3,7},{4,0},{5,1},{6,2},{7,3},{8,12},{9,13},{10,... | collective-permute-start | bytes 3047432 | tf_op jit(solution)/shard_map/ppermute | solution.py:483
  138.2 8.5 %collective-permute-start.27 = (bf16[4,16,2176]{2,1,0:T(8,128)(2,1)S(1)}, bf16[4,16,2176]{2,1,0:T(8,128)(2,1)S(1)}, u32[]{:S(2)}, u32[]{:S(2)}) collective-permute-start(bf16[4,16,2176]{2,1,0:T(8,128)(2,1)S(1)} %slice_bitcast_fusion.4), channel_id=1, source_target_pairs={{0,4},{1,5},{2,6},{3,7},{4,0},{5,1},{6,2},{7,3},{8,12},{9,13},{10,... | collective-permute-start | bytes 835592 | tf_op jit(solution)/shard_map/ppermute | solution.py:483
  139.8 12.2 %collective-permute-start.32 = (bf16[4,16,3968]{2,1,0:T(8,128)(2,1)S(1)}, bf16[4,16,3968]{2,1,0:T(8,128)(2,1)S(1)}, u32[]{:S(2)}, u32[]{:S(2)}) collective-permute-start(bf16[4,16,3968]{2,1,0:T(8,128)(2,1)S(1)} %slice_bitcast_fusion.3), channel_id=1, source_target_pairs={{0,1},{1,0},{2,3},{3,2},{4,5},{5,4},{6,7},{7,6},{8,9},{9,8},{10,11... | collective-permute-start | bytes 1523720 | tf_op jit(solution)/shard_map/ppermute | solution.py:483
  146.6 5.5 %collective-permute-start.26 = (bf16[384,1024]{1,0:T(8,128)(2,1)S(1)}, bf16[384,1024]{1,0:T(8,128)(2,1)S(1)}, u32[]{:S(2)}, u32[]{:S(2)}) collective-permute-start(bf16[384,1024]{1,0:T(8,128)(2,1)S(1)} %get-tuple-element.116), channel_id=1, source_target_pairs={{0,2},{1,3},{2,0},{3,1},{4,6},{5,7},{6,4},{7,5},{8,10},{9,11},{10,... | collective-permute-start | bytes 2359304 | tf_op jit(solution)/shard_map/ppermute | solution.py:483
  152.5 4.9 %collective-permute-start.29 = (bf16[16,2176]{1,0:T(8,128)(2,1)S(1)}, bf16[16,2176]{1,0:T(8,128)(2,1)S(1)}, u32[]{:S(2)}, u32[]{:S(2)}) collective-permute-start(bf16[16,2176]{1,0:T(8,128)(2,1)S(1)} %get-tuple-element.131), channel_id=1, source_target_pairs={{0,8},{1,9},{2,10},{3,11},{4,12},{5,13},{6,14},{7,15},{8,0},{9,1},... | collective-permute-start | bytes 208904 | tf_op jit(solution)/shard_map/ppermute | solution.py:483
  152.6 6.3 %collective-permute-start.31 = (bf16[16,2176]{1,0:T(8,128)(2,1)S(1)}, bf16[16,2176]{1,0:T(8,128)(2,1)S(1)}, u32[]{:S(2)}, u32[]{:S(2)}) collective-permute-start(bf16[16,2176]{1,0:T(8,128)(2,1)S(1)} %get-tuple-element.132), channel_id=1, source_target_pairs={{0,24},{1,25},{2,26},{3,27},{4,28},{5,29},{6,30},{7,31},{8,16},{9,... | collective-permute-start | bytes 208904 | tf_op jit(solution)/shard_map/ppermute | solution.py:483
  154.0 6.5 %collective-permute-start.30 = (bf16[16,2176]{1,0:T(8,128)(2,1)S(1)}, bf16[16,2176]{1,0:T(8,128)(2,1)S(1)}, u32[]{:S(2)}, u32[]{:S(2)}) collective-permute-start(bf16[16,2176]{1,0:T(8,128)(2,1)S(1)} %get-tuple-element.133), channel_id=1, source_target_pairs={{0,16},{1,17},{2,18},{3,19},{4,20},{5,21},{6,22},{7,23},{8,24},{9,... | collective-permute-start | bytes 208904 | tf_op jit(solution)/shard_map/ppermute | solution.py:483
  156.1 8.0 %collective-permute-start.28 = (bf16[2,4,24,1024]{3,2,1,0:T(8,128)(2,1)S(1)}, bf16[2,4,24,1024]{3,2,1,0:T(8,128)(2,1)S(1)}, u32[]{:S(2)}, u32[]{:S(2)}) collective-permute-start(bf16[2,4,24,1024]{3,2,1,0:T(8,128)(2,1)S(1)} %bitcast.139), channel_id=1, source_target_pairs={{0,4},{1,5},{2,6},{3,7},{4,0},{5,1},{6,2},{7,3},{8,12},{9,13},{10,... | collective-permute-start | bytes 1179656 | tf_op jit(solution)/shard_map/ppermute | solution.py:483
  160.6 14.8 %copy-start.2 = (f32[16,2176]{1,0:T(8,128)}, f32[16,2176]{1,0:T(8,128)S(1)}, u32[]{:S(2)}) copy-start(f32[16,2176]{1,0:T(8,128)S(1)} %fusion.10) | copy-start | bytes 417796
  164.3 5.9 %collective-permute-start.34 = (bf16[16,3968]{1,0:T(8,128)(2,1)S(1)}, bf16[16,3968]{1,0:T(8,128)(2,1)S(1)}, u32[]{:S(2)}, u32[]{:S(2)}) collective-permute-start(bf16[16,3968]{1,0:T(8,128)(2,1)S(1)} %get-tuple-element.128), channel_id=1, source_target_pairs={{0,8},{1,9},{2,10},{3,11},{4,12},{5,13},{6,14},{7,15},{8,0},{9,1},... | collective-permute-start | bytes 380936 | tf_op jit(solution)/shard_map/ppermute | solution.py:483
  165.6 6.8 %collective-permute-start.36 = (bf16[16,3968]{1,0:T(8,128)(2,1)S(1)}, bf16[16,3968]{1,0:T(8,128)(2,1)S(1)}, u32[]{:S(2)}, u32[]{:S(2)}) collective-permute-start(bf16[16,3968]{1,0:T(8,128)(2,1)S(1)} %get-tuple-element.129), channel_id=1, source_target_pairs={{0,24},{1,25},{2,26},{3,27},{4,28},{5,29},{6,30},{7,31},{8,16},{9,... | collective-permute-start | bytes 380936 | tf_op jit(solution)/shard_map/ppermute | solution.py:483
  166.8 8.6 %collective-permute-start.35 = (bf16[16,3968]{1,0:T(8,128)(2,1)S(1)}, bf16[16,3968]{1,0:T(8,128)(2,1)S(1)}, u32[]{:S(2)}, u32[]{:S(2)}) collective-permute-start(bf16[16,3968]{1,0:T(8,128)(2,1)S(1)} %get-tuple-element.130), channel_id=1, source_target_pairs={{0,16},{1,17},{2,18},{3,19},{4,20},{5,21},{6,22},{7,23},{8,24},{9,... | collective-permute-start | bytes 380936 | tf_op jit(solution)/shard_map/ppermute | solution.py:483
  167.9 7.5 %collective-permute-start.33 = (bf16[4,24,1024]{2,1,0:T(8,128)(2,1)S(1)}, bf16[4,24,1024]{2,1,0:T(8,128)(2,1)S(1)}, u32[]{:S(2)}, u32[]{:S(2)}) collective-permute-start(bf16[4,24,1024]{2,1,0:T(8,128)(2,1)S(1)} %slice_bitcast_fusion.5), channel_id=1, source_target_pairs={{0,1},{1,0},{2,3},{3,2},{4,5},{5,4},{6,7},{7,6},{8,9},{9,8},{10,11... | collective-permute-start | bytes 589832 | tf_op jit(solution)/shard_map/ppermute | solution.py:483
  175.4 3.8 %slice-start = ((f32[16,2176]{1,0:T(8,128)}), f32[16,1536]{1,0:T(8,128)S(1)}, s32[]{:S(2)}) async-start(f32[16,2176]{1,0:T(8,128)} %copy-done.2), calls=%async_computation | async-start | bytes 196608 | tf_op jit(solution)/shard_map/slice | solution.py:1030
  175.6 6.4 %collective-permute-start.37 = (bf16[24,1024]{1,0:T(8,128)(2,1)S(1)}, bf16[24,1024]{1,0:T(8,128)(2,1)S(1)}, u32[]{:S(2)}, u32[]{:S(2)}) collective-permute-start(bf16[24,1024]{1,0:T(8,128)(2,1)S(1)} %get-tuple-element.137), channel_id=1, source_target_pairs={{0,8},{1,9},{2,10},{3,11},{4,12},{5,13},{6,14},{7,15},{8,0},{9,1},... | collective-permute-start | bytes 147464 | tf_op jit(solution)/shard_map/ppermute | solution.py:483
  176.0 6.0 %collective-permute-start.39 = (bf16[24,1024]{1,0:T(8,128)(2,1)S(1)}, bf16[24,1024]{1,0:T(8,128)(2,1)S(1)}, u32[]{:S(2)}, u32[]{:S(2)}) collective-permute-start(bf16[24,1024]{1,0:T(8,128)(2,1)S(1)} %get-tuple-element.138), channel_id=1, source_target_pairs={{0,24},{1,25},{2,26},{3,27},{4,28},{5,29},{6,30},{7,31},{8,16},{9,... | collective-permute-start | bytes 147464 | tf_op jit(solution)/shard_map/ppermute | solution.py:483
  177.6 5.0 %collective-permute-start.38 = (bf16[24,1024]{1,0:T(8,128)(2,1)S(1)}, bf16[24,1024]{1,0:T(8,128)(2,1)S(1)}, u32[]{:S(2)}, u32[]{:S(2)}) collective-permute-start(bf16[24,1024]{1,0:T(8,128)(2,1)S(1)} %get-tuple-element.139), channel_id=1, source_target_pairs={{0,16},{1,17},{2,18},{3,19},{4,20},{5,21},{6,22},{7,23},{8,24},{9,... | collective-permute-start | bytes 147464 | tf_op jit(solution)/shard_map/ppermute | solution.py:483
where the time goes:
time: 186 us; the launch traced here: 185 us
  waiting for transfers between devices  71 us (38%)
  starting transfers between devices  51.6 us (28%)
  Pallas kernels  45.6 us (25%)
  local copies, waits for them, and re-layouts  8.76 us (5%)
  other arithmetic  7.27 us (4%)
    ppermute x40, waiting for transfers between devices, swap(): return lax.ppermute(values, AXES, perm)  71 us
    ppermute x40, starting transfers between devices, swap(): return lax.ppermute(values, AXES, perm)  51.6 us
    pallas_call x4, Pallas kernels, call(): pl.pallas_call(kernel, out_shape=shapes, in_specs=specs, out_specs=[here...  27.7 us
    pallas_call x2, Pallas kernels, attention_grad(): pl.pallas_call(functools.partial(attn_grad_kernel, heads, min(rows, 256),...  10.3 us
    pallas_call x1, Pallas kernels, attention_own(): pl.pallas_call(functools.partial(attn_own_kernel, heads, min(rows, 256),...  6.47 us
  transfers between devices with their start and end apart: 40, of which 23 were waited for; matrix products, arithmetic and copies ran while one was open for 5% of the time, Pallas kernels for 13%

commit v1 on v0

--- a/solution.py
+++ b/solution.py
@@ -401,7 +401,7 @@
             pltpu.VMEM((rows, rows), F32), sums, sums,
         ],
         compiler_params=pltpu.CompilerParams(vmem_limit_bytes=20 * 2**20),
-        cost_estimate=cost_of(9 if own else 10),
+        cost_estimate=cost_of(2.5),
         name="attn_grad_own" if own else "attn_grad_others",
     )(info, q, kv, grad_out, lse, delta, *([before] if own else []))
 
@@ -992,9 +992,6 @@
     grad_q_rot, own_kv = attention_grad(
         q_rot, kv_mine, grad_attn, lse, delta, info, docs, dq_others
     )
-    got_kv, h1, h2 = tie(got_kv, h1, h2)
-    h1 = blocks.add(h1[0], blocks.swap(h1[1], blocks.x))
-    h2 = blocks.add(h2[0], blocks.swap(h2[1], blocks.y))
 
     gx, keep_a, give_a = call(
         functools.partial(post_kernel, size),
@@ -1007,14 +1004,18 @@
             ((tok_rows, width + kv_width), F32), ((tok_rows, size.a_width), BF),
             ((1, size.flat), F32),
         ],
-        6,
+        1.5,
         (
             me, grad_q_rot, own_kv, got_kv, cos, sin, n1t, a_mine,
             a_other, tokens, grad_mid, flat, grad_gain,
         ),
         24,
     )
-    held = blocks.add(keep_a, blocks.swap(give_a, blocks.core))
+    got_a = blocks.swap(give_a, blocks.core)
+    got_a, h1, h2 = tie(got_a, h1, h2)
+    held = blocks.add(keep_a, got_a)
+    h1 = blocks.add(h1[0], blocks.swap(h1[1], blocks.x))
+    h2 = blocks.add(h2[0], blocks.swap(h2[1], blocks.y))
     held, h2 = tie(held, h2)
     held = held.reshape(2, 2, blocks.zs, size.tall, size.a_width)
     held = blocks.add(held[0], blocks.swap(held[1], blocks.y))

time: 186 us -> 180 us (0.968)
  waiting for transfers between devices: 71 us -> 64.1 us
    ppermute x40, waiting for transfers between devices: 71 us -> 64.1 us  [swap(): return lax.ppermute(values, AXES, perm)]
  transfers between devices with their start and end apart: 40 -> 40, of which waited for: 23 -> 22; matrix products, arithmetic and copies ran while one was open for 5% -> 5% of each run, Pallas kernels for 13% -> 13%
where the time goes in v1:
time: 180 us; the launch traced here: 179 us
  waiting for transfers between devices  64.1 us (36%)
  starting transfers between devices  52.4 us (29%)
  Pallas kernels  45.5 us (25%)
  local copies, waits for them, and re-layouts  8.76 us (5%)
  other arithmetic  7.22 us (4%)
    ppermute x40, waiting for transfers between devices, swap(): return lax.ppermute(values, AXES, perm)  64.1 us
    ppermute x40, starting transfers between devices, swap(): return lax.ppermute(values, AXES, perm)  52.4 us
    pallas_call x4, Pallas kernels, call(): pl.pallas_call(kernel, out_shape=shapes, in_specs=specs, out_specs=[here...  27.7 us
    pallas_call x2, Pallas kernels, attention_grad(): pl.pallas_call(functools.partial(attn_grad_kernel, heads, min(rows, 256),...  10.3 us
    pallas_call x1, Pallas kernels, attention_own(): pl.pallas_call(functools.partial(attn_own_kernel, heads, min(rows, 256),...  6.47 us
  transfers between devices with their start and end apart: 40, of which 22 were waited for; matrix products, arithmetic and copies ran while one was open for 5% of the time, Pallas kernels for 13%

profile of v1, /device:TPU:0, one launch (start us, length us, event | category | flops | bytes accessed | tf_op | source)
XLA Modules:
  0.0 179.2 jit_solution(17135212118874333294)
XLA Ops:
  0.7 0.9 reshape.148
  1.6 0.8 reshape.149
  2.4 0.8 reshape.147
  3.9 4.1 %collective-permute-start.1 = (bf16[24,1024]{1,0:T(8,128)(2,1)S(1)}, bf16[24,1024]{1,0:T(8,128)(2,1)S(1)}, u32[]{:S(2)}, u32[]{:S(2)}) collective-permute-start(bf16[24,1024]{1,0:T(8,128)(2,1)S(1)} %fusion.17), channel_id=1, source_target_pairs={{0,16},{1,17},{2,18},{3,19},{4,20},{5,21},{6,22},{7,23},{8,24},{9,... | collective-permute-start | bytes 147464 | tf_op jit(solution)/shard_map/ppermute | solution.py:483
  8.0 1.6 collective-permute-start
  9.6 0.8 reduce-window.4
  11.1 0.7 fusion.26
  12.1 3.4 %collective-permute-done.2 = bf16[24,1024]{1,0:T(8,128)(2,1)S(1)} collective-permute-done((bf16[24,1024]{1,0:T(8,128)(2,1)S(1)}, bf16[24,1024]{1,0:T(8,128)(2,1)S(1)}, u32[]{:S(2)}, u32[]{:S(2)}) %collective-permute-start.2) | collective-permute-done | bytes 49184 | tf_op jit(solution)/shard_map/ppermute | solution.py:483
  15.5 1.6 collective-permute-start.3
  17.1 1.6 fusion.6
  19.2 0.9 wire.1
  20.1 1.2 collective-permute-done.3
  21.3 0.7 collective-permute-start.6
  22.0 3.7 %collective-permute-start.4 = (bf16[16,3328]{1,0:T(8,128)(2,1)S(1)}, bf16[16,3328]{1,0:T(8,128)(2,1)S(1)}, u32[]{:S(2)}, u32[]{:S(2)}) collective-permute-start(bf16[16,3328]{1,0:T(8,128)(2,1)S(1)} %get-tuple-element.76), channel_id=1, source_target_pairs={{0,8},{1,9},{2,10},{3,11},{4,12},{5,13},{6,14},{7,15},{8,0},{9,1},... | collective-permute-start | bytes 319496 | tf_op jit(solution)/shard_map/ppermute | solution.py:483
  25.9 1.5 collective-permute-start.7
  27.4 0.7 collective-permute-done.6
  28.1 2.8 %collective-permute-done.5 = bf16[16,3328]{1,0:T(8,128)(2,1)S(1)} collective-permute-done((bf16[16,3328]{1,0:T(8,128)(2,1)S(1)}, bf16[16,3328]{1,0:T(8,128)(2,1)S(1)}, u32[]{:S(2)}, u32[]{:S(2)}) %collective-permute-start.5) | collective-permute-done | bytes 106528 | tf_op jit(solution)/shard_map/ppermute | solution.py:483
  30.9 2.7 %collective-permute-done.7 = bf16[2,4,24,1024]{3,2,1,0:T(8,128)(2,1)S(1)} collective-permute-done((bf16[2,4,24,1024]{3,2,1,0:T(8,128)(2,1)S(1)}, bf16[2,4,24,1024]{3,2,1,0:T(8,128)(2,1)S(1)}, u32[]{:S(2)}, u32[]{:S(2)}) %collective-permute-start.7) | collective-permute-done | bytes 393248 | tf_op jit(solution)/shard_map/ppermute | solution.py:483
  33.6 0.7 collective-permute-start.12
  34.4 0.7 collective-permute-start.11
  35.1 2.9 %collective-permute-start.10 = (bf16[16,2816]{1,0:T(8,128)(2,1)S(1)}, bf16[16,2816]{1,0:T(8,128)(2,1)S(1)}, u32[]{:S(2)}, u32[]{:S(2)}) collective-permute-start(bf16[16,2816]{1,0:T(8,128)(2,1)S(1)} %get-tuple-element.85), channel_id=1, source_target_pairs={{0,8},{1,9},{2,10},{3,11},{4,12},{5,13},{6,14},{7,15},{8,0},{9,1},... | collective-permute-start | bytes 270344 | tf_op jit(solution)/shard_map/ppermute | solution.py:483
  38.0 1.5 collective-permute-start.13
  40.1 1.6 collective-permute-done.11
  41.8 4.4 %collective-permute-done.13 = bf16[4,16,3328]{2,1,0:T(8,128)(2,1)S(1)} collective-permute-done((bf16[4,16,3328]{2,1,0:T(8,128)(2,1)S(1)}, bf16[4,16,3328]{2,1,0:T(8,128)(2,1)S(1)}, u32[]{:S(2)}, u32[]{:S(2)}) %collective-permute-start.13) | collective-permute-done | bytes 426016 | tf_op jit(solution)/shard_map/ppermute | solution.py:483
  46.2 2.7 %norm_qkv.1 = (bf16[512,576]{1,0:T(8,128)(2,1)S(1)}, bf16[512,384]{1,0:T(8,128)(2,1)S(1)}, bf16[768,512]{1,0:T(8,128)(2,1)S(1)}, f32[1,2304]{1,0:T(1,128)S(1)}) custom-call(s32[1]{0:T(128)} %bitcast.me_ref, bf16[512,576]{1,0:T(8,128)(2,1)S(1)} %get-tuple-element.72.x_ref, bf16[384,1024]{1,0:T(8,128)(2,1)S(1)} %bitcast.115, ...), custom_call_target="tpu_custom_call" | custom-call | flops 3300000000 | bytes 1048576 | tf_op jit(solution)/shard_map/norm_qkv/pallas_call | solution.py:848
  49.0 1.6 collective-permute-start.9
  50.5 1.5 collective-permute-start.14
  52.5 6.5 %attn_own.1 = (f32[576,512]{1,0:T(8,128)S(1)}, f32[9,1,512]{2,1,0:T(1,128)S(1)}, f32[9,1,512]{2,1,0:T(1,128)S(1)}) custom-call(s32[6]{0:T(128)S(1)} %pad_add_fusion.info, bf16[512,576]{1,0:T(8,128)(2,1)S(1)} %get-tuple-element.79.q_ref, bf16[512,384]{1,0:T(8,128)(2,1)S(1)} %get-tuple-element.80.kv_ref), custom_call_target="tpu_custom_call" | custom-call | flops 6600000000 | bytes 1048576 | tf_op jit(solution)/shard_map/attn_own/pallas_call | solution.py:361
  59.0 2.8 %collective-permute-done.14 = bf16[4,16,2816]{2,1,0:T(8,128)(2,1)S(1)} collective-permute-done((bf16[4,16,2816]{2,1,0:T(8,128)(2,1)S(1)}, bf16[4,16,2816]{2,1,0:T(8,128)(2,1)S(1)}, u32[]{:S(2)}, u32[]{:S(2)}) %collective-permute-start.14) | collective-permute-done | bytes 360480 | tf_op jit(solution)/shard_map/ppermute | solution.py:483
  62.5 1.1 attn_others.1
  63.6 14.1 %collective-permute-done.15 = bf16[2,4,16,2816]{3,2,1,0:T(8,128)(2,1)S(1)} collective-permute-done((bf16[2,4,16,2816]{3,2,1,0:T(8,128)(2,1)S(1)}, bf16[2,4,16,2816]{3,2,1,0:T(8,128)(2,1)S(1)}, u32[]{:S(2)}, u32[]{:S(2)}) %collective-permute-start.15) | collective-permute-done | bytes 720928 | tf_op jit(solution)/shard_map/ppermute | solution.py:483
  78.2 2.9 %collective-permute-done.19.b2_10 = bf16[128,2816]{1,0:T(8,128)(2,1)S(1)} collective-permute-done((bf16[128,2816]{1,0:T(8,128)(2,1)S(1)}, bf16[128,2816]{1,0:T(8,128)(2,1)S(1)}, u32[]{:S(2)}, u32[]{:S(2)}) %collective-permute-start.19) | collective-permute-done | bytes 720928 | tf_op jit(solution)/shard_map/ppermute | solution.py:483
  81.1 1.0 collective-permute-done.20.b2_11
  82.2 19.0 %feed_forward.1 = (bf16[576,512]{1,0:T(8,128)(2,1)}, bf16[256,3968]{1,0:T(8,128)(2,1)S(1)}, bf16[256,3968]{1,0:T(8,128)(2,1)S(1)}, bf16[256,2176]{1,0:T(8,128)(2...) custom-call(s32[1]{0:T(128)} %bitcast.me_ref, ...), custom_call_target="tpu_custom_call" | custom-call | flops 23100000256 | bytes 1048576 | tf_op jit(solution)/shard_map/feed_forward/pallas_call | solution.py:848
  101.7 1.2 attn_grad_others.1
  102.9 9.7 %collective-permute-start.23 = (bf16[512,384]{1,0:T(8,128)(2,1)S(1)}, bf16[512,384]{1,0:T(8,128)(2,1)S(1)}, u32[]{:S(2)}, u32[]{:S(2)}) collective-permute-start(bf16[512,384]{1,0:T(8,128)(2,1)S(1)} %get-tuple-element.107), channel_id=1, source_target_pairs={{0,1},{1,0},{2,3},{3,2},{4,5},{5,4},{6,7},{7,6},{8,9},{9,8},{10,11... | collective-permute-start | bytes 1179656 | tf_op jit(solution)/shard_map/ppermute | solution.py:483
  113.5 1.6 collective-permute-start.25
  115.1 9.1 %attn_grad_own.1 = (f32[512,576]{1,0:T(8,128)S(1)}, f32[512,384]{1,0:T(8,128)S(1)}) custom-call(s32[6]{0:T(128)S(1)} %pad_add_fusion.info, bf16[512,576]{1,0:T(8,128)(2,1)S(1)} %get-tuple-element.79.q_ref, bf16[512,384]{1,0:T(8,128)(2,1)S(1)} %get-tuple-element.80.kv_ref, bf16[512,576]{1,0:T(8,128)(2,1)S(1)} %get-tuple-element.96.do_ref, ...), custom_call_target="tpu_custom_call" | custom-call | flops 2750000128 | bytes 1048576 | tf_op jit(solution)/shard_map/attn_grad_own/pallas_call | solution.py:394
  124.2 5.0 %norm_qkv_back.1 = (f32[576,512]{1,0:T(8,128)}, bf16[384,1024]{1,0:T(8,128)(2,1)S(1)}, bf16[384,1024]{1,0:T(8,128)(2,1)S(1)}) custom-call(s32[1]{0:T(128)} %bitcast.me_ref, f32[512,576]{1,0:T(8,128)S(1)} %get-tuple-element.105.dq_ref, f32[512,384]{1,0:T(8,128)S(1)} %get-tuple-element.106.dkv_ref, bf16[512,384]{1,0:T(8,128)(2,1)S(1)} %collective-permute-done.23.got_ref, ...), custom_call_target="tpu_custom_call" | custom-call | flops 1650000000 | bytes 1048576 | tf_op jit(solution)/shard_map/norm_qkv_back/pallas_call | solution.py:848
  129.3 4.6 %collective-permute-done.26 = bf16[2,4,16,2176]{3,2,1,0:T(8,128)(2,1)S(1)} collective-permute-done((bf16[2,4,16,2176]{3,2,1,0:T(8,128)(2,1)S(1)}, bf16[2,4,16,2176]{3,2,1,0:T(8,128)(2,1)S(1)}, u32[]{:S(2)}, u32[]{:S(2)}) %collective-permute-start.26) | collective-permute-done | bytes 557088 | tf_op jit(solution)/shard_map/ppermute | solution.py:483
  134.1 3.8 %collective-permute-done.25 = bf16[2,4,16,3968]{3,2,1,0:T(8,128)(2,1)S(1)} collective-permute-done((bf16[2,4,16,3968]{3,2,1,0:T(8,128)(2,1)S(1)}, bf16[2,4,16,3968]{3,2,1,0:T(8,128)(2,1)S(1)}, u32[]{:S(2)}, u32[]{:S(2)}) %collective-permute-start.25) | collective-permute-done | bytes 1015840 | tf_op jit(solution)/shard_map/ppermute | solution.py:483
  138.1 1.6 collective-permute-start.27
  139.7 1.8 collective-permute-start.32
  141.8 3.9 %collective-permute-done.27 = bf16[4,16,2176]{2,1,0:T(8,128)(2,1)S(1)} collective-permute-done((bf16[4,16,2176]{2,1,0:T(8,128)(2,1)S(1)}, bf16[4,16,2176]{2,1,0:T(8,128)(2,1)S(1)}, u32[]{:S(2)}, u32[]{:S(2)}) %collective-permute-start.27) | collective-permute-done | bytes 278560 | tf_op jit(solution)/shard_map/ppermute | solution.py:483
  145.9 1.5 collective-permute-start.31
  147.3 2.0 %collective-permute-start.30 = (bf16[16,2176]{1,0:T(8,128)(2,1)S(1)}, bf16[16,2176]{1,0:T(8,128)(2,1)S(1)}, u32[]{:S(2)}, u32[]{:S(2)}) collective-permute-start(bf16[16,2176]{1,0:T(8,128)(2,1)S(1)} %get-tuple-element.133), channel_id=1, source_target_pairs={{0,16},{1,17},{2,18},{3,19},{4,20},{5,21},{6,22},{7,23},{8,24},{9,... | collective-permute-start | bytes 208904 | tf_op jit(solution)/shard_map/ppermute | solution.py:483
  149.4 1.6 collective-permute-start.28
  151.0 1.2 collective-permute-done.31
  152.2 1.7 collective-permute-done.30
  154.1 3.6 %collective-permute-done.28 = bf16[2,4,24,1024]{3,2,1,0:T(8,128)(2,1)S(1)} collective-permute-done((bf16[2,4,24,1024]{3,2,1,0:T(8,128)(2,1)S(1)}, bf16[2,4,24,1024]{3,2,1,0:T(8,128)(2,1)S(1)}, u32[]{:S(2)}, u32[]{:S(2)}) %collective-permute-start.28) | collective-permute-done | bytes 393248 | tf_op jit(solution)/shard_map/ppermute | solution.py:483
  157.9 1.3 collective-permute-start.34
  159.3 1.1 collective-permute-start.36
  160.4 1.1 collective-permute-start.35
  161.5 1.1 collective-permute-start.33
  162.7 1.0 collective-permute-done.34
  163.6 2.5 %collective-permute-done.36 = bf16[16,3968]{1,0:T(8,128)(2,1)S(1)} collective-permute-done((bf16[16,3968]{1,0:T(8,128)(2,1)S(1)}, bf16[16,3968]{1,0:T(8,128)(2,1)S(1)}, u32[]{:S(2)}, u32[]{:S(2)}) %collective-permute-start.36) | collective-permute-done | bytes 127008 | tf_op jit(solution)/shard_map/ppermute | solution.py:483
  166.1 3.2 %collective-permute-done.35 = bf16[16,3968]{1,0:T(8,128)(2,1)S(1)} collective-permute-done((bf16[16,3968]{1,0:T(8,128)(2,1)S(1)}, bf16[16,3968]{1,0:T(8,128)(2,1)S(1)}, u32[]{:S(2)}, u32[]{:S(2)}) %collective-permute-start.35) | collective-permute-done | bytes 127008 | tf_op jit(solution)/shard_map/ppermute | solution.py:483
  169.7 1.9 %collective-permute-start.39 = (bf16[24,1024]{1,0:T(8,128)(2,1)S(1)}, bf16[24,1024]{1,0:T(8,128)(2,1)S(1)}, u32[]{:S(2)}, u32[]{:S(2)}) collective-permute-start(bf16[24,1024]{1,0:T(8,128)(2,1)S(1)} %get-tuple-element.138), channel_id=1, source_target_pairs={{0,24},{1,25},{2,26},{3,27},{4,28},{5,29},{6,30},{7,31},{8,16},{9,... | collective-permute-start | bytes 147464 | tf_op jit(solution)/shard_map/ppermute | solution.py:483
  171.5 1.5 collective-permute-start.38
  173.1 0.7 reshape.173
  173.9 0.7 reshape.168
  177.2 0.7 reshape.163
  177.9 0.7 reshape.165
  178.5 0.7 reshape.164
  (112 shorter events, 10.5 us)
Async XLA Ops:
  0.6 18.2 %copy-start.3 = (bf16[27648]{0:T(1024)(128)(2,1)S(1)}, bf16[27648]{0:T(1024)(128)(2,1)}, u32[]{:S(2)}) copy-start(bf16[27648]{0:T(1024)(128)(2,1)} %param.19) | copy-start | bytes 165892
  0.7 18.4 %copy-start.5 = (bf16[27648]{0:T(1024)(128)(2,1)S(1)}, bf16[27648]{0:T(1024)(128)(2,1)}, u32[]{:S(2)}) copy-start(bf16[27648]{0:T(1024)(128)(2,1)} %param.18) | copy-start | bytes 165892
  0.7 18.3 %copy-start.4 = (bf16[27648]{0:T(1024)(128)(2,1)S(1)}, bf16[27648]{0:T(1024)(128)(2,1)}, u32[]{:S(2)}) copy-start(bf16[27648]{0:T(1024)(128)(2,1)} %param.17) | copy-start | bytes 165892
  0.7 18.1 %copy-start.6 = (bf16[10368]{0:T(1024)(128)(2,1)S(1)}, bf16[10368]{0:T(1024)(128)(2,1)}, u32[]{:S(2)}) copy-start(bf16[10368]{0:T(1024)(128)(2,1)} %param.16) | copy-start | bytes 62212
  0.7 18.5 %copy-start.1 = (bf16[512,576]{0,1:T(8,128)(2,1)S(1)}, bf16[512,576]{0,1:T(8,128)(2,1)}, u32[]{:S(2)}) copy-start(bf16[512,576]{0,1:T(8,128)(2,1)} %param.22) | copy-start | bytes 1769476
  0.7 18.5 %copy-start = (bf16[512,576]{0,1:T(8,128)(2,1)S(1)}, bf16[512,576]{0,1:T(8,128)(2,1)}, u32[]{:S(2)}) copy-start(bf16[512,576]{0,1:T(8,128)(2,1)} %param.12) | copy-start | bytes 1769476
  3.9 8.2 %collective-permute-start.1 = (bf16[24,1024]{1,0:T(8,128)(2,1)S(1)}, bf16[24,1024]{1,0:T(8,128)(2,1)S(1)}, u32[]{:S(2)}, u32[]{:S(2)}) collective-permute-start(bf16[24,1024]{1,0:T(8,128)(2,1)S(1)} %fusion.17), channel_id=1, source_target_pairs={{0,16},{1,17},{2,18},{3,19},{4,20},{5,21},{6,22},{7,23},{8,24},{9,... | collective-permute-start | bytes 147464 | tf_op jit(solution)/shard_map/ppermute | solution.py:483
  8.0 4.1 %collective-permute-start = (bf16[24,1024]{1,0:T(8,128)(2,1)S(1)}, bf16[24,1024]{1,0:T(8,128)(2,1)S(1)}, u32[]{:S(2)}, u32[]{:S(2)}) collective-permute-start(bf16[24,1024]{1,0:T(8,128)(2,1)S(1)} %fusion.17), channel_id=1, source_target_pairs={{0,8},{1,9},{2,10},{3,11},{4,12},{5,13},{6,14},{7,15},{8,0},{9,1},... | collective-permute-start | bytes 147464 | tf_op jit(solution)/shard_map/ppermute | solution.py:483
  9.6 5.9 %collective-permute-start.2 = (bf16[24,1024]{1,0:T(8,128)(2,1)S(1)}, bf16[24,1024]{1,0:T(8,128)(2,1)S(1)}, u32[]{:S(2)}, u32[]{:S(2)}) collective-permute-start(bf16[24,1024]{1,0:T(8,128)(2,1)S(1)} %fusion.17), channel_id=1, source_target_pairs={{0,24},{1,25},{2,26},{3,27},{4,28},{5,29},{6,30},{7,31},{8,16},{9,... | collective-permute-start | bytes 147464 | tf_op jit(solution)/shard_map/ppermute | solution.py:483
  15.5 5.7 %collective-permute-start.3 = (bf16[4,24,1024]{2,1,0:T(8,128)(2,1)S(1)}, bf16[4,24,1024]{2,1,0:T(8,128)(2,1)S(1)}, u32[]{:S(2)}, u32[]{:S(2)}) collective-permute-start(bf16[4,24,1024]{2,1,0:T(8,128)(2,1)S(1)} %get-tuple-element.141), channel_id=1, source_target_pairs={{0,1},{1,0},{2,3},{3,2},{4,5},{5,4},{6,7},{7,6},{8,9},{9,8},{10,11... | collective-permute-start | bytes 589832 | tf_op jit(solution)/shard_map/ppermute | solution.py:483
  21.3 6.7 %collective-permute-start.6 = (bf16[16,3328]{1,0:T(8,128)(2,1)S(1)}, bf16[16,3328]{1,0:T(8,128)(2,1)S(1)}, u32[]{:S(2)}, u32[]{:S(2)}) collective-permute-start(bf16[16,3328]{1,0:T(8,128)(2,1)S(1)} %get-tuple-element.76), channel_id=1, source_target_pairs={{0,24},{1,25},{2,26},{3,27},{4,28},{5,29},{6,30},{7,31},{8,16},{9,... | collective-permute-start | bytes 319496 | tf_op jit(solution)/shard_map/ppermute | solution.py:483
  22.0 8.8 %collective-permute-start.5 = (bf16[16,3328]{1,0:T(8,128)(2,1)S(1)}, bf16[16,3328]{1,0:T(8,128)(2,1)S(1)}, u32[]{:S(2)}, u32[]{:S(2)}) collective-permute-start(bf16[16,3328]{1,0:T(8,128)(2,1)S(1)} %get-tuple-element.76), channel_id=1, source_target_pairs={{0,16},{1,17},{2,18},{3,19},{4,20},{5,21},{6,22},{7,23},{8,24},{9,... | collective-permute-start | bytes 319496 | tf_op jit(solution)/shard_map/ppermute | solution.py:483
  22.0 8.8 %collective-permute-start.4 = (bf16[16,3328]{1,0:T(8,128)(2,1)S(1)}, bf16[16,3328]{1,0:T(8,128)(2,1)S(1)}, u32[]{:S(2)}, u32[]{:S(2)}) collective-permute-start(bf16[16,3328]{1,0:T(8,128)(2,1)S(1)} %get-tuple-element.76), channel_id=1, source_target_pairs={{0,8},{1,9},{2,10},{3,11},{4,12},{5,13},{6,14},{7,15},{8,0},{9,1},... | collective-permute-start | bytes 319496 | tf_op jit(solution)/shard_map/ppermute | solution.py:483
  25.9 7.8 %collective-permute-start.7 = (bf16[2,4,24,1024]{3,2,1,0:T(8,128)(2,1)S(1)}, bf16[2,4,24,1024]{3,2,1,0:T(8,128)(2,1)S(1)}, u32[]{:S(2)}, u32[]{:S(2)}) collective-permute-start(bf16[2,4,24,1024]{3,2,1,0:T(8,128)(2,1)S(1)} %pad_maximum_fusion.4), channel_id=1, source_target_pairs={{0,4},{1,5},{2,6},{3,7},{4,0},{5,1},{6,2},{7,3},{8,12},{9,13},{10,... | collective-permute-start | bytes 1179656 | tf_op jit(solution)/shard_map/ppermute | solution.py:483
  33.6 6.5 %collective-permute-start.12 = (bf16[16,2816]{1,0:T(8,128)(2,1)S(1)}, bf16[16,2816]{1,0:T(8,128)(2,1)S(1)}, u32[]{:S(2)}, u32[]{:S(2)}) collective-permute-start(bf16[16,2816]{1,0:T(8,128)(2,1)S(1)} %get-tuple-element.85), channel_id=1, source_target_pairs={{0,24},{1,25},{2,26},{3,27},{4,28},{5,29},{6,30},{7,31},{8,16},{9,... | collective-permute-start | bytes 270344 | tf_op jit(solution)/shard_map/ppermute | solution.py:483
  34.4 7.4 %collective-permute-start.11 = (bf16[16,2816]{1,0:T(8,128)(2,1)S(1)}, bf16[16,2816]{1,0:T(8,128)(2,1)S(1)}, u32[]{:S(2)}, u32[]{:S(2)}) collective-permute-start(bf16[16,2816]{1,0:T(8,128)(2,1)S(1)} %get-tuple-element.85), channel_id=1, source_target_pairs={{0,16},{1,17},{2,18},{3,19},{4,20},{5,21},{6,22},{7,23},{8,24},{9,... | collective-permute-start | bytes 270344 | tf_op jit(solution)/shard_map/ppermute | solution.py:483
  35.1 6.6 %collective-permute-start.10 = (bf16[16,2816]{1,0:T(8,128)(2,1)S(1)}, bf16[16,2816]{1,0:T(8,128)(2,1)S(1)}, u32[]{:S(2)}, u32[]{:S(2)}) collective-permute-start(bf16[16,2816]{1,0:T(8,128)(2,1)S(1)} %get-tuple-element.85), channel_id=1, source_target_pairs={{0,8},{1,9},{2,10},{3,11},{4,12},{5,13},{6,14},{7,15},{8,0},{9,1},... | collective-permute-start | bytes 270344 | tf_op jit(solution)/shard_map/ppermute | solution.py:483
  38.0 8.1 %collective-permute-start.13 = (bf16[4,16,3328]{2,1,0:T(8,128)(2,1)S(1)}, bf16[4,16,3328]{2,1,0:T(8,128)(2,1)S(1)}, u32[]{:S(2)}, u32[]{:S(2)}) collective-permute-start(bf16[4,16,3328]{2,1,0:T(8,128)(2,1)S(1)} %pad_maximum_fusion.3), channel_id=1, source_target_pairs={{0,1},{1,0},{2,3},{3,2},{4,5},{5,4},{6,7},{7,6},{8,9},{9,8},{10,11... | collective-permute-start | bytes 1277960 | tf_op jit(solution)/shard_map/ppermute | solution.py:483
  39.6 6.6 %collective-permute-start.8 = (bf16[384,1024]{1,0:T(8,128)(2,1)S(1)}, bf16[384,1024]{1,0:T(8,128)(2,1)S(1)}, u32[]{:S(2)}, u32[]{:S(2)}) collective-permute-start(bf16[384,1024]{1,0:T(8,128)(2,1)S(1)} %bitcast.114), channel_id=1, source_target_pairs={{0,2},{1,3},{2,0},{3,1},{4,6},{5,7},{6,4},{7,5},{8,10},{9,11},{10,... | collective-permute-start | bytes 2359304 | tf_op jit(solution)/shard_map/ppermute | solution.py:483
  49.0 13.6 %collective-permute-start.9 = (bf16[512,384]{1,0:T(8,128)(2,1)S(1)}, bf16[512,384]{1,0:T(8,128)(2,1)S(1)}, u32[]{:S(2)}, u32[]{:S(2)}) collective-permute-start(bf16[512,384]{1,0:T(8,128)(2,1)S(1)} %get-tuple-element.80.kv_ref), channel_id=1, source_target_pairs={{0,1},{1,0},{2,3},{3,2},{4,5},{5,4},{6,7},{7,6},{8,9},{9,8},{10,11... | collective-permute-start | bytes 1179656 | tf_op jit(solution)/shard_map/ppermute | solution.py:483
  50.5 11.4 %collective-permute-start.14 = (bf16[4,16,2816]{2,1,0:T(8,128)(2,1)S(1)}, bf16[4,16,2816]{2,1,0:T(8,128)(2,1)S(1)}, u32[]{:S(2)}, u32[]{:S(2)}) collective-permute-start(bf16[4,16,2816]{2,1,0:T(8,128)(2,1)S(1)} %pad_maximum_fusion.5), channel_id=1, source_target_pairs={{0,4},{1,5},{2,6},{3,7},{4,0},{5,1},{6,2},{7,3},{8,12},{9,13},{10,... | collective-permute-start | bytes 1081352 | tf_op jit(solution)/shard_map/ppermute | solution.py:483
  52.0 25.7 %collective-permute-start.16 = (bf16[2,4,16,3328]{3,2,1,0:T(8,128)(2,1)S(1)}, bf16[2,4,16,3328]{3,2,1,0:T(8,128)(2,1)S(1)}, u32[]{:S(2)}, u32[]{:S(2)}) collective-permute-start(bf16[2,4,16,3328]{3,2,1,0:T(8,128)(2,1)S(1)} %pad_maximum_fusion), channel_id=1, source_target_pairs={{0,4},{1,5},{2,6},{3,7},{4,0},{5,1},{6,2},{7,3},{8,12},{9,13},{10,... | collective-permute-start | bytes 2555912 | tf_op jit(solution)/shard_map/ppermute | solution.py:483
  52.5 25.7 %collective-permute-start.17 = (bf16[128,3328]{1,0:T(8,128)(2,1)S(1)}, bf16[128,3328]{1,0:T(8,128)(2,1)S(1)}, u32[]{:S(2)}, u32[]{:S(2)}) collective-permute-start(bf16[128,3328]{1,0:T(8,128)(2,1)S(1)} %bitcast.117), channel_id=1, source_target_pairs={{0,2},{1,3},{2,0},{3,1},{4,6},{5,7},{6,4},{7,5},{8,10},{9,11},{10,... | collective-permute-start | bytes 2555912 | tf_op jit(solution)/shard_map/ppermute | solution.py:483
  61.9 15.8 %collective-permute-start.15 = (bf16[2,4,16,2816]{3,2,1,0:T(8,128)(2,1)S(1)}, bf16[2,4,16,2816]{3,2,1,0:T(8,128)(2,1)S(1)}, u32[]{:S(2)}, u32[]{:S(2)}) collective-permute-start(bf16[2,4,16,2816]{3,2,1,0:T(8,128)(2,1)S(1)} %pad_maximum_fusion.2), channel_id=1, source_target_pairs={{0,1},{1,0},{2,3},{3,2},{4,5},{5,4},{6,7},{7,6},{8,9},{9,8},{10,11... | collective-permute-start | bytes 2162696 | tf_op jit(solution)/shard_map/ppermute | solution.py:483
  77.7 4.4 %collective-permute-start.18 = (bf16[128,3328]{1,0:T(8,128)(2,1)S(1)}, bf16[128,3328]{1,0:T(8,128)(2,1)S(1)}, u32[]{:S(2)}, u32[]{:S(2)}) collective-permute-start(bf16[128,3328]{1,0:T(8,128)(2,1)S(1)} %bitcast.123), channel_id=1, source_target_pairs={{0,2},{1,3},{2,0},{3,1},{4,6},{5,7},{6,4},{7,5},{8,10},{9,11},{10,... | collective-permute-start | bytes 2555912 | tf_op jit(solution)/shard_map/ppermute | solution.py:483
  77.7 3.4 %collective-permute-start.19 = (bf16[128,2816]{1,0:T(8,128)(2,1)S(1)}, bf16[128,2816]{1,0:T(8,128)(2,1)S(1)}, u32[]{:S(2)}, u32[]{:S(2)}) collective-permute-start(bf16[128,2816]{1,0:T(8,128)(2,1)S(1)} %bitcast.119), channel_id=1, source_target_pairs={{0,2},{1,3},{2,0},{3,1},{4,6},{5,7},{6,4},{7,5},{8,10},{9,11},{10,... | collective-permute-start | bytes 2162696 | tf_op jit(solution)/shard_map/ppermute | solution.py:483
  78.2 3.9 %collective-permute-start.20 = (bf16[128,2816]{1,0:T(8,128)(2,1)S(1)}, bf16[128,2816]{1,0:T(8,128)(2,1)S(1)}, u32[]{:S(2)}, u32[]{:S(2)}) collective-permute-start(bf16[128,2816]{1,0:T(8,128)(2,1)S(1)} %bitcast.125), channel_id=1, source_target_pairs={{0,2},{1,3},{2,0},{3,1},{4,6},{5,7},{6,4},{7,5},{8,10},{9,11},{10,... | collective-permute-start | bytes 2162696 | tf_op jit(solution)/shard_map/ppermute | solution.py:483
  101.2 11.6 %collective-permute-start.21 = (bf16[256,3968]{1,0:T(8,128)(2,1)S(1)}, bf16[256,3968]{1,0:T(8,128)(2,1)S(1)}, u32[]{:S(2)}, u32[]{:S(2)}) collective-permute-start(bf16[256,3968]{1,0:T(8,128)(2,1)S(1)} %get-tuple-element.101), channel_id=1, source_target_pairs={{0,2},{1,3},{2,0},{3,1},{4,6},{5,7},{6,4},{7,5},{8,10},{9,11},{10,... | collective-permute-start | bytes 6094856 | tf_op jit(solution)/shard_map/ppermute | solution.py:483
  101.3 11.2 %collective-permute-start.22 = (bf16[256,2176]{1,0:T(8,128)(2,1)S(1)}, bf16[256,2176]{1,0:T(8,128)(2,1)S(1)}, u32[]{:S(2)}, u32[]{:S(2)}) collective-permute-start(bf16[256,2176]{1,0:T(8,128)(2,1)S(1)} %get-tuple-element.103), channel_id=1, source_target_pairs={{0,2},{1,3},{2,0},{3,1},{4,6},{5,7},{6,4},{7,5},{8,10},{9,11},{10,... | collective-permute-start | bytes 3342344 | tf_op jit(solution)/shard_map/ppermute | solution.py:483
  102.9 21.3 %collective-permute-start.23 = (bf16[512,384]{1,0:T(8,128)(2,1)S(1)}, bf16[512,384]{1,0:T(8,128)(2,1)S(1)}, u32[]{:S(2)}, u32[]{:S(2)}) collective-permute-start(bf16[512,384]{1,0:T(8,128)(2,1)S(1)} %get-tuple-element.107), channel_id=1, source_target_pairs={{0,1},{1,0},{2,3},{3,2},{4,5},{5,4},{6,7},{7,6},{8,9},{9,8},{10,11... | collective-permute-start | bytes 1179656 | tf_op jit(solution)/shard_map/ppermute | solution.py:483
  113.4 20.6 %collective-permute-start.26 = (bf16[2,4,16,2176]{3,2,1,0:T(8,128)(2,1)S(1)}, bf16[2,4,16,2176]{3,2,1,0:T(8,128)(2,1)S(1)}, u32[]{:S(2)}, u32[]{:S(2)}) collective-permute-start(bf16[2,4,16,2176]{3,2,1,0:T(8,128)(2,1)S(1)} %slice_bitcast_fusion.2), channel_id=1, source_target_pairs={{0,1},{1,0},{2,3},{3,2},{4,5},{5,4},{6,7},{7,6},{8,9},{9,8},{10,11... | collective-permute-start | bytes 1671176 | tf_op jit(solution)/shard_map/ppermute | solution.py:483
  113.5 24.3 %collective-permute-start.25 = (bf16[2,4,16,3968]{3,2,1,0:T(8,128)(2,1)S(1)}, bf16[2,4,16,3968]{3,2,1,0:T(8,128)(2,1)S(1)}, u32[]{:S(2)}, u32[]{:S(2)}) collective-permute-start(bf16[2,4,16,3968]{3,2,1,0:T(8,128)(2,1)S(1)} %slice_bitcast_fusion), channel_id=1, source_target_pairs={{0,4},{1,5},{2,6},{3,7},{4,0},{5,1},{6,2},{7,3},{8,12},{9,13},{10,... | collective-permute-start | bytes 3047432 | tf_op jit(solution)/shard_map/ppermute | solution.py:483
  129.3 8.8 %collective-permute-start.24 = (bf16[384,1024]{1,0:T(8,128)(2,1)S(1)}, bf16[384,1024]{1,0:T(8,128)(2,1)S(1)}, u32[]{:S(2)}, u32[]{:S(2)}) collective-permute-start(bf16[384,1024]{1,0:T(8,128)(2,1)S(1)} %get-tuple-element.113), channel_id=1, source_target_pairs={{0,2},{1,3},{2,0},{3,1},{4,6},{5,7},{6,4},{7,5},{8,10},{9,11},{10,... | collective-permute-start | bytes 2359304 | tf_op jit(solution)/shard_map/ppermute | solution.py:483
  138.1 7.6 %collective-permute-start.27 = (bf16[4,16,2176]{2,1,0:T(8,128)(2,1)S(1)}, bf16[4,16,2176]{2,1,0:T(8,128)(2,1)S(1)}, u32[]{:S(2)}, u32[]{:S(2)}) collective-permute-start(bf16[4,16,2176]{2,1,0:T(8,128)(2,1)S(1)} %slice_bitcast_fusion.4), channel_id=1, source_target_pairs={{0,4},{1,5},{2,6},{3,7},{4,0},{5,1},{6,2},{7,3},{8,12},{9,13},{10,... | collective-permute-start | bytes 835592 | tf_op jit(solution)/shard_map/ppermute | solution.py:483
  139.7 14.2 %collective-permute-start.32 = (bf16[4,16,3968]{2,1,0:T(8,128)(2,1)S(1)}, bf16[4,16,3968]{2,1,0:T(8,128)(2,1)S(1)}, u32[]{:S(2)}, u32[]{:S(2)}) collective-permute-start(bf16[4,16,3968]{2,1,0:T(8,128)(2,1)S(1)} %slice_bitcast_fusion.3), channel_id=1, source_target_pairs={{0,1},{1,0},{2,3},{3,2},{4,5},{5,4},{6,7},{7,6},{8,9},{9,8},{10,11... | collective-permute-start | bytes 1523720 | tf_op jit(solution)/shard_map/ppermute | solution.py:483
  145.8 5.2 %collective-permute-start.29 = (bf16[16,2176]{1,0:T(8,128)(2,1)S(1)}, bf16[16,2176]{1,0:T(8,128)(2,1)S(1)}, u32[]{:S(2)}, u32[]{:S(2)}) collective-permute-start(bf16[16,2176]{1,0:T(8,128)(2,1)S(1)} %get-tuple-element.131), channel_id=1, source_target_pairs={{0,8},{1,9},{2,10},{3,11},{4,12},{5,13},{6,14},{7,15},{8,0},{9,1},... | collective-permute-start | bytes 208904 | tf_op jit(solution)/shard_map/ppermute | solution.py:483
  145.9 6.3 %collective-permute-start.31 = (bf16[16,2176]{1,0:T(8,128)(2,1)S(1)}, bf16[16,2176]{1,0:T(8,128)(2,1)S(1)}, u32[]{:S(2)}, u32[]{:S(2)}) collective-permute-start(bf16[16,2176]{1,0:T(8,128)(2,1)S(1)} %get-tuple-element.132), channel_id=1, source_target_pairs={{0,24},{1,25},{2,26},{3,27},{4,28},{5,29},{6,30},{7,31},{8,16},{9,... | collective-permute-start | bytes 208904 | tf_op jit(solution)/shard_map/ppermute | solution.py:483
  147.3 6.5 %collective-permute-start.30 = (bf16[16,2176]{1,0:T(8,128)(2,1)S(1)}, bf16[16,2176]{1,0:T(8,128)(2,1)S(1)}, u32[]{:S(2)}, u32[]{:S(2)}) collective-permute-start(bf16[16,2176]{1,0:T(8,128)(2,1)S(1)} %get-tuple-element.133), channel_id=1, source_target_pairs={{0,16},{1,17},{2,18},{3,19},{4,20},{5,21},{6,22},{7,23},{8,24},{9,... | collective-permute-start | bytes 208904 | tf_op jit(solution)/shard_map/ppermute | solution.py:483
  149.4 8.3 %collective-permute-start.28 = (bf16[2,4,24,1024]{3,2,1,0:T(8,128)(2,1)S(1)}, bf16[2,4,24,1024]{3,2,1,0:T(8,128)(2,1)S(1)}, u32[]{:S(2)}, u32[]{:S(2)}) collective-permute-start(bf16[2,4,24,1024]{3,2,1,0:T(8,128)(2,1)S(1)} %bitcast.139), channel_id=1, source_target_pairs={{0,4},{1,5},{2,6},{3,7},{4,0},{5,1},{6,2},{7,3},{8,12},{9,13},{10,... | collective-permute-start | bytes 1179656 | tf_op jit(solution)/shard_map/ppermute | solution.py:483
  153.9 4.0 %copy-start.2 = (f32[16,2176]{1,0:T(8,128)}, f32[16,2176]{1,0:T(8,128)S(1)}, u32[]{:S(2)}) copy-start(f32[16,2176]{1,0:T(8,128)S(1)} %fusion.10) | copy-start | bytes 417796
  157.9 15.1 %slice-start = ((f32[16,2176]{1,0:T(8,128)}), f32[16,576]{1,0:T(8,128)S(1)}, s32[]{:S(2)}) async-start(f32[16,2176]{1,0:T(8,128)} %copy-done.2), calls=%async_computation | async-start | bytes 81920 | tf_op jit(solution)/shard_map/slice | solution.py:1034
  157.9 15.2 %slice-start.1 = ((f32[16,2176]{1,0:T(8,128)}), f32[16,1536]{1,0:T(8,128)S(1)}, s32[]{:S(2)}) async-start(f32[16,2176]{1,0:T(8,128)} %copy-done.2), calls=%async_computation.1 | async-start | bytes 196608 | tf_op jit(solution)/shard_map/slice | solution.py:1031
  157.9 5.7 %collective-permute-start.34 = (bf16[16,3968]{1,0:T(8,128)(2,1)S(1)}, bf16[16,3968]{1,0:T(8,128)(2,1)S(1)}, u32[]{:S(2)}, u32[]{:S(2)}) collective-permute-start(bf16[16,3968]{1,0:T(8,128)(2,1)S(1)} %get-tuple-element.128), channel_id=1, source_target_pairs={{0,8},{1,9},{2,10},{3,11},{4,12},{5,13},{6,14},{7,15},{8,0},{9,1},... | collective-permute-start | bytes 380936 | tf_op jit(solution)/shard_map/ppermute | solution.py:483
  159.3 6.8 %collective-permute-start.36 = (bf16[16,3968]{1,0:T(8,128)(2,1)S(1)}, bf16[16,3968]{1,0:T(8,128)(2,1)S(1)}, u32[]{:S(2)}, u32[]{:S(2)}) collective-permute-start(bf16[16,3968]{1,0:T(8,128)(2,1)S(1)} %get-tuple-element.129), channel_id=1, source_target_pairs={{0,24},{1,25},{2,26},{3,27},{4,28},{5,29},{6,30},{7,31},{8,16},{9,... | collective-permute-start | bytes 380936 | tf_op jit(solution)/shard_map/ppermute | solution.py:483
  160.4 8.9 %collective-permute-start.35 = (bf16[16,3968]{1,0:T(8,128)(2,1)S(1)}, bf16[16,3968]{1,0:T(8,128)(2,1)S(1)}, u32[]{:S(2)}, u32[]{:S(2)}) collective-permute-start(bf16[16,3968]{1,0:T(8,128)(2,1)S(1)} %get-tuple-element.130), channel_id=1, source_target_pairs={{0,16},{1,17},{2,18},{3,19},{4,20},{5,21},{6,22},{7,23},{8,24},{9,... | collective-permute-start | bytes 380936 | tf_op jit(solution)/shard_map/ppermute | solution.py:483
  161.5 7.8 %collective-permute-start.33 = (bf16[4,24,1024]{2,1,0:T(8,128)(2,1)S(1)}, bf16[4,24,1024]{2,1,0:T(8,128)(2,1)S(1)}, u32[]{:S(2)}, u32[]{:S(2)}) collective-permute-start(bf16[4,24,1024]{2,1,0:T(8,128)(2,1)S(1)} %slice_bitcast_fusion.5), channel_id=1, source_target_pairs={{0,1},{1,0},{2,3},{3,2},{4,5},{5,4},{6,7},{7,6},{8,9},{9,8},{10,11... | collective-permute-start | bytes 589832 | tf_op jit(solution)/shard_map/ppermute | solution.py:483
  169.5 6.4 %collective-permute-start.37 = (bf16[24,1024]{1,0:T(8,128)(2,1)S(1)}, bf16[24,1024]{1,0:T(8,128)(2,1)S(1)}, u32[]{:S(2)}, u32[]{:S(2)}) collective-permute-start(bf16[24,1024]{1,0:T(8,128)(2,1)S(1)} %get-tuple-element.137), channel_id=1, source_target_pairs={{0,8},{1,9},{2,10},{3,11},{4,12},{5,13},{6,14},{7,15},{8,0},{9,1},... | collective-permute-start | bytes 147464 | tf_op jit(solution)/shard_map/ppermute | solution.py:483
  169.7 6.2 %collective-permute-start.39 = (bf16[24,1024]{1,0:T(8,128)(2,1)S(1)}, bf16[24,1024]{1,0:T(8,128)(2,1)S(1)}, u32[]{:S(2)}, u32[]{:S(2)}) collective-permute-start(bf16[24,1024]{1,0:T(8,128)(2,1)S(1)} %get-tuple-element.138), channel_id=1, source_target_pairs={{0,24},{1,25},{2,26},{3,27},{4,28},{5,29},{6,30},{7,31},{8,16},{9,... | collective-permute-start | bytes 147464 | tf_op jit(solution)/shard_map/ppermute | solution.py:483
  171.5 5.0 %collective-permute-start.38 = (bf16[24,1024]{1,0:T(8,128)(2,1)S(1)}, bf16[24,1024]{1,0:T(8,128)(2,1)S(1)}, u32[]{:S(2)}, u32[]{:S(2)}) collective-permute-start(bf16[24,1024]{1,0:T(8,128)(2,1)S(1)} %get-tuple-element.139), channel_id=1, source_target_pairs={{0,16},{1,17},{2,18},{3,19},{4,20},{5,21},{6,22},{7,23},{8,24},{9,... | collective-permute-start | bytes 147464 | tf_op jit(solution)/shard_map/ppermute | solution.py:483

commit v2 on v1

--- a/solution.py
+++ b/solution.py
@@ -1019,7 +1019,7 @@
     held, h2 = tie(held, h2)
     held = held.reshape(2, 2, blocks.zs, size.tall, size.a_width)
     held = blocks.add(held[0], blocks.swap(held[1], blocks.y))
-    held, share2, h1 = tie(held, blocks.sum_z(h2), h1)
+    held, share2 = tie(held, blocks.sum_z(h2))
     held = blocks.add(held[0], blocks.swap(held[1], blocks.x))
     held, share1 = tie(held, blocks.sum_z(h1))
     share_a = blocks.sum_z(held)

time: 180 us -> 177 us (0.983)
  waiting for transfers between devices: 64.1 us -> 61.2 us
    ppermute x40, waiting for transfers between devices: 64.1 us -> 61.2 us  [swap(): return lax.ppermute(values, AXES, perm)]
  transfers between devices with their start and end apart: 40 -> 40, of which waited for: 22 -> 21; matrix products, arithmetic and copies ran while one was open for 5% -> 6% of each run, Pallas kernels for 13% -> 13%
where the time goes in v2:
time: 177 us
  waiting for transfers between devices  61.2 us (35%)
  starting transfers between devices  52.8 us (30%)
  Pallas kernels  45.5 us (26%)
  local copies, waits for them, and re-layouts  8.76 us (5%)
  other arithmetic  7.22 us (4%)
    ppermute x40, waiting for transfers between devices, swap(): return lax.ppermute(values, AXES, perm)  61.2 us
    ppermute x40, starting transfers between devices, swap(): return lax.ppermute(values, AXES, perm)  52.8 us
    pallas_call x4, Pallas kernels, call(): pl.pallas_call(kernel, out_shape=shapes, in_specs=specs, out_specs=[here...  27.7 us
    pallas_call x2, Pallas kernels, attention_grad(): pl.pallas_call(functools.partial(attn_grad_kernel, heads, min(rows, 256),...  10.3 us
    pallas_call x1, Pallas kernels, attention_own(): pl.pallas_call(functools.partial(attn_own_kernel, heads, min(rows, 256),...  6.47 us
  transfers between devices with their start and end apart: 40, of which 21 were waited for; matrix products, arithmetic and copies ran while one was open for 6% of the time, Pallas kernels for 13%

profile of v2, /device:TPU:0, one launch (start us, length us, event | category | flops | bytes accessed | tf_op | source)
XLA Modules:
  0.0 176.7 jit_solution(14551252262380150976)
XLA Ops:
  0.7 0.9 reshape.148
  1.6 0.8 reshape.149
  2.4 0.8 reshape.147
  3.3 0.7 fusion.17
  3.9 4.1 %collective-permute-start.1 = (bf16[24,1024]{1,0:T(8,128)(2,1)S(1)}, bf16[24,1024]{1,0:T(8,128)(2,1)S(1)}, u32[]{:S(2)}, u32[]{:S(2)}) collective-permute-start(bf16[24,1024]{1,0:T(8,128)(2,1)S(1)} %fusion.17), channel_id=1, source_target_pairs={{0,16},{1,17},{2,18},{3,19},{4,20},{5,21},{6,22},{7,23},{8,24},{9,... | collective-permute-start | bytes 147464 | tf_op jit(solution)/shard_map/ppermute | solution.py:483
  8.0 1.6 collective-permute-start
  9.6 0.8 reduce-window.4
  10.4 0.7 fusion.20
  11.1 0.7 fusion.26
  12.1 3.4 %collective-permute-done.2 = bf16[24,1024]{1,0:T(8,128)(2,1)S(1)} collective-permute-done((bf16[24,1024]{1,0:T(8,128)(2,1)S(1)}, bf16[24,1024]{1,0:T(8,128)(2,1)S(1)}, u32[]{:S(2)}, u32[]{:S(2)}) %collective-permute-start.2) | collective-permute-done | bytes 49184 | tf_op jit(solution)/shard_map/ppermute | solution.py:483
  15.5 1.6 collective-permute-start.3
  17.1 1.6 fusion.6
  19.2 0.9 wire.1
  20.1 1.2 collective-permute-done.3
  21.3 0.7 collective-permute-start.6
  22.0 3.7 %collective-permute-start.4 = (bf16[16,3328]{1,0:T(8,128)(2,1)S(1)}, bf16[16,3328]{1,0:T(8,128)(2,1)S(1)}, u32[]{:S(2)}, u32[]{:S(2)}) collective-permute-start(bf16[16,3328]{1,0:T(8,128)(2,1)S(1)} %get-tuple-element.75), channel_id=1, source_target_pairs={{0,8},{1,9},{2,10},{3,11},{4,12},{5,13},{6,14},{7,15},{8,0},{9,1},... | collective-permute-start | bytes 319496 | tf_op jit(solution)/shard_map/ppermute | solution.py:483
  25.9 1.5 collective-permute-start.7
  27.4 0.7 collective-permute-done.6
  28.1 2.8 %collective-permute-done.5 = bf16[16,3328]{1,0:T(8,128)(2,1)S(1)} collective-permute-done((bf16[16,3328]{1,0:T(8,128)(2,1)S(1)}, bf16[16,3328]{1,0:T(8,128)(2,1)S(1)}, u32[]{:S(2)}, u32[]{:S(2)}) %collective-permute-start.5) | collective-permute-done | bytes 106528 | tf_op jit(solution)/shard_map/ppermute | solution.py:483
  30.9 2.7 %collective-permute-done.7 = bf16[2,4,24,1024]{3,2,1,0:T(8,128)(2,1)S(1)} collective-permute-done((bf16[2,4,24,1024]{3,2,1,0:T(8,128)(2,1)S(1)}, bf16[2,4,24,1024]{3,2,1,0:T(8,128)(2,1)S(1)}, u32[]{:S(2)}, u32[]{:S(2)}) %collective-permute-start.7) | collective-permute-done | bytes 393248 | tf_op jit(solution)/shard_map/ppermute | solution.py:483
  33.6 0.7 collective-permute-start.12
  34.4 0.7 collective-permute-start.11
  35.1 2.9 %collective-permute-start.10 = (bf16[16,2816]{1,0:T(8,128)(2,1)S(1)}, bf16[16,2816]{1,0:T(8,128)(2,1)S(1)}, u32[]{:S(2)}, u32[]{:S(2)}) collective-permute-start(bf16[16,2816]{1,0:T(8,128)(2,1)S(1)} %get-tuple-element.84), channel_id=1, source_target_pairs={{0,8},{1,9},{2,10},{3,11},{4,12},{5,13},{6,14},{7,15},{8,0},{9,1},... | collective-permute-start | bytes 270344 | tf_op jit(solution)/shard_map/ppermute | solution.py:483
  38.0 1.5 collective-permute-start.13
  40.1 1.6 collective-permute-done.11
  41.8 4.4 %collective-permute-done.13 = bf16[4,16,3328]{2,1,0:T(8,128)(2,1)S(1)} collective-permute-done((bf16[4,16,3328]{2,1,0:T(8,128)(2,1)S(1)}, bf16[4,16,3328]{2,1,0:T(8,128)(2,1)S(1)}, u32[]{:S(2)}, u32[]{:S(2)}) %collective-permute-start.13) | collective-permute-done | bytes 426016 | tf_op jit(solution)/shard_map/ppermute | solution.py:483
  46.2 2.7 %norm_qkv.1 = (bf16[512,576]{1,0:T(8,128)(2,1)S(1)}, bf16[512,384]{1,0:T(8,128)(2,1)S(1)}, bf16[768,512]{1,0:T(8,128)(2,1)S(1)}, f32[1,2304]{1,0:T(1,128)S(1)}) custom-call(s32[1]{0:T(128)} %bitcast.me_ref, bf16[512,576]{1,0:T(8,128)(2,1)S(1)} %get-tuple-element.71.x_ref, bf16[384,1024]{1,0:T(8,128)(2,1)S(1)} %bitcast.117, ...), custom_call_target="tpu_custom_call" | custom-call | flops 3300000000 | bytes 1048576 | tf_op jit(solution)/shard_map/norm_qkv/pallas_call | solution.py:848
  49.0 1.6 collective-permute-start.9
  50.5 1.5 collective-permute-start.14
  52.5 6.5 %attn_own.1 = (f32[576,512]{1,0:T(8,128)S(1)}, f32[9,1,512]{2,1,0:T(1,128)S(1)}, f32[9,1,512]{2,1,0:T(1,128)S(1)}) custom-call(s32[6]{0:T(128)S(1)} %pad_add_fusion.info, bf16[512,576]{1,0:T(8,128)(2,1)S(1)} %get-tuple-element.78.q_ref, bf16[512,384]{1,0:T(8,128)(2,1)S(1)} %get-tuple-element.79.kv_ref), custom_call_target="tpu_custom_call" | custom-call | flops 6600000000 | bytes 1048576 | tf_op jit(solution)/shard_map/attn_own/pallas_call | solution.py:361
  59.0 2.8 %collective-permute-done.14 = bf16[4,16,2816]{2,1,0:T(8,128)(2,1)S(1)} collective-permute-done((bf16[4,16,2816]{2,1,0:T(8,128)(2,1)S(1)}, bf16[4,16,2816]{2,1,0:T(8,128)(2,1)S(1)}, u32[]{:S(2)}, u32[]{:S(2)}) %collective-permute-start.14) | collective-permute-done | bytes 360480 | tf_op jit(solution)/shard_map/ppermute | solution.py:483
  62.5 1.1 attn_others.1
  63.6 14.1 %collective-permute-done.15 = bf16[2,4,16,2816]{3,2,1,0:T(8,128)(2,1)S(1)} collective-permute-done((bf16[2,4,16,2816]{3,2,1,0:T(8,128)(2,1)S(1)}, bf16[2,4,16,2816]{3,2,1,0:T(8,128)(2,1)S(1)}, u32[]{:S(2)}, u32[]{:S(2)}) %collective-permute-start.15) | collective-permute-done | bytes 720928 | tf_op jit(solution)/shard_map/ppermute | solution.py:483
  78.2 2.9 %collective-permute-done.19.b2_10 = bf16[128,2816]{1,0:T(8,128)(2,1)S(1)} collective-permute-done((bf16[128,2816]{1,0:T(8,128)(2,1)S(1)}, bf16[128,2816]{1,0:T(8,128)(2,1)S(1)}, u32[]{:S(2)}, u32[]{:S(2)}) %collective-permute-start.19) | collective-permute-done | bytes 720928 | tf_op jit(solution)/shard_map/ppermute | solution.py:483
  81.1 1.0 collective-permute-done.20.b2_11
  82.2 19.0 %feed_forward.1 = (bf16[576,512]{1,0:T(8,128)(2,1)}, bf16[256,3968]{1,0:T(8,128)(2,1)S(1)}, bf16[256,3968]{1,0:T(8,128)(2,1)S(1)}, bf16[256,2176]{1,0:T(8,128)(2...) custom-call(s32[1]{0:T(128)} %bitcast.me_ref, ...), custom_call_target="tpu_custom_call" | custom-call | flops 23100000256 | bytes 1048576 | tf_op jit(solution)/shard_map/feed_forward/pallas_call | solution.py:848
  101.7 1.2 attn_grad_others.1
  102.9 9.7 %collective-permute-start.23 = (bf16[512,384]{1,0:T(8,128)(2,1)S(1)}, bf16[512,384]{1,0:T(8,128)(2,1)S(1)}, u32[]{:S(2)}, u32[]{:S(2)}) collective-permute-start(bf16[512,384]{1,0:T(8,128)(2,1)S(1)} %get-tuple-element.106), channel_id=1, source_target_pairs={{0,1},{1,0},{2,3},{3,2},{4,5},{5,4},{6,7},{7,6},{8,9},{9,8},{10,11... | collective-permute-start | bytes 1179656 | tf_op jit(solution)/shard_map/ppermute | solution.py:483
  113.5 1.6 collective-permute-start.25
  115.1 9.1 %attn_grad_own.1 = (f32[512,576]{1,0:T(8,128)S(1)}, f32[512,384]{1,0:T(8,128)S(1)}) custom-call(s32[6]{0:T(128)S(1)} %pad_add_fusion.info, bf16[512,576]{1,0:T(8,128)(2,1)S(1)} %get-tuple-element.78.q_ref, bf16[512,384]{1,0:T(8,128)(2,1)S(1)} %get-tuple-element.79.kv_ref, bf16[512,576]{1,0:T(8,128)(2,1)S(1)} %get-tuple-element.95.do_ref, ...), custom_call_target="tpu_custom_call" | custom-call | flops 2750000128 | bytes 1048576 | tf_op jit(solution)/shard_map/attn_grad_own/pallas_call | solution.py:394
  124.2 5.0 %norm_qkv_back.1 = (f32[576,512]{1,0:T(8,128)}, bf16[384,1024]{1,0:T(8,128)(2,1)S(1)}, bf16[384,1024]{1,0:T(8,128)(2,1)S(1)}) custom-call(s32[1]{0:T(128)} %bitcast.me_ref, f32[512,576]{1,0:T(8,128)S(1)} %get-tuple-element.104.dq_ref, f32[512,384]{1,0:T(8,128)S(1)} %get-tuple-element.105.dkv_ref, bf16[512,384]{1,0:T(8,128)(2,1)S(1)} %collective-permute-done.23.got_ref, ...), custom_call_target="tpu_custom_call" | custom-call | flops 1650000000 | bytes 1048576 | tf_op jit(solution)/shard_map/norm_qkv_back/pallas_call | solution.py:848
  129.3 4.6 %collective-permute-done.26 = bf16[2,4,16,2176]{3,2,1,0:T(8,128)(2,1)S(1)} collective-permute-done((bf16[2,4,16,2176]{3,2,1,0:T(8,128)(2,1)S(1)}, bf16[2,4,16,2176]{3,2,1,0:T(8,128)(2,1)S(1)}, u32[]{:S(2)}, u32[]{:S(2)}) %collective-permute-start.26) | collective-permute-done | bytes 557088 | tf_op jit(solution)/shard_map/ppermute | solution.py:483
  134.1 3.8 %collective-permute-done.25 = bf16[2,4,16,3968]{3,2,1,0:T(8,128)(2,1)S(1)} collective-permute-done((bf16[2,4,16,3968]{3,2,1,0:T(8,128)(2,1)S(1)}, bf16[2,4,16,3968]{3,2,1,0:T(8,128)(2,1)S(1)}, u32[]{:S(2)}, u32[]{:S(2)}) %collective-permute-start.25) | collective-permute-done | bytes 1015840 | tf_op jit(solution)/shard_map/ppermute | solution.py:483
  138.1 1.6 collective-permute-start.27
  139.7 1.8 %collective-permute-start.33 = (bf16[4,16,3968]{2,1,0:T(8,128)(2,1)S(1)}, bf16[4,16,3968]{2,1,0:T(8,128)(2,1)S(1)}, u32[]{:S(2)}, u32[]{:S(2)}) collective-permute-start(bf16[4,16,3968]{2,1,0:T(8,128)(2,1)S(1)} %slice_bitcast_fusion.3), channel_id=1, source_target_pairs={{0,1},{1,0},{2,3},{3,2},{4,5},{5,4},{6,7},{7,6},{8,9},{9,8},{10,11... | collective-permute-start | bytes 1523720 | tf_op jit(solution)/shard_map/ppermute | solution.py:483
  141.8 3.9 %collective-permute-done.27 = bf16[4,16,2176]{2,1,0:T(8,128)(2,1)S(1)} collective-permute-done((bf16[4,16,2176]{2,1,0:T(8,128)(2,1)S(1)}, bf16[4,16,2176]{2,1,0:T(8,128)(2,1)S(1)}, u32[]{:S(2)}, u32[]{:S(2)}) %collective-permute-start.27) | collective-permute-done | bytes 278560 | tf_op jit(solution)/shard_map/ppermute | solution.py:483
  145.9 1.5 collective-permute-start.31
  147.3 2.0 %collective-permute-start.30 = (bf16[16,2176]{1,0:T(8,128)(2,1)S(1)}, bf16[16,2176]{1,0:T(8,128)(2,1)S(1)}, u32[]{:S(2)}, u32[]{:S(2)}) collective-permute-start(bf16[16,2176]{1,0:T(8,128)(2,1)S(1)} %get-tuple-element.131), channel_id=1, source_target_pairs={{0,16},{1,17},{2,18},{3,19},{4,20},{5,21},{6,22},{7,23},{8,24},{9,... | collective-permute-start | bytes 208904 | tf_op jit(solution)/shard_map/ppermute | solution.py:483
  149.4 1.6 collective-permute-start.28
  151.0 1.2 collective-permute-done.31
  152.2 1.8 %collective-permute-done.30 = bf16[16,2176]{1,0:T(8,128)(2,1)S(1)} collective-permute-done((bf16[16,2176]{1,0:T(8,128)(2,1)S(1)}, bf16[16,2176]{1,0:T(8,128)(2,1)S(1)}, u32[]{:S(2)}, u32[]{:S(2)}) %collective-permute-start.30) | collective-permute-done | bytes 69664 | tf_op jit(solution)/shard_map/ppermute | solution.py:483
  154.3 2.2 %collective-permute-start.36 = (bf16[16,3968]{1,0:T(8,128)(2,1)S(1)}, bf16[16,3968]{1,0:T(8,128)(2,1)S(1)}, u32[]{:S(2)}, u32[]{:S(2)}) collective-permute-start(bf16[16,3968]{1,0:T(8,128)(2,1)S(1)} %get-tuple-element.127), channel_id=1, source_target_pairs={{0,24},{1,25},{2,26},{3,27},{4,28},{5,29},{6,30},{7,31},{8,16},{9,... | collective-permute-start | bytes 380936 | tf_op jit(solution)/shard_map/ppermute | solution.py:483
  156.4 1.3 collective-permute-start.35
  157.9 1.5 collective-permute-start.32
  159.7 2.0 %collective-permute-done.36 = bf16[16,3968]{1,0:T(8,128)(2,1)S(1)} collective-permute-done((bf16[16,3968]{1,0:T(8,128)(2,1)S(1)}, bf16[16,3968]{1,0:T(8,128)(2,1)S(1)}, u32[]{:S(2)}, u32[]{:S(2)}) %collective-permute-start.36) | collective-permute-done | bytes 127008 | tf_op jit(solution)/shard_map/ppermute | solution.py:483
  161.7 4.2 %collective-permute-done.35 = bf16[16,3968]{1,0:T(8,128)(2,1)S(1)} collective-permute-done((bf16[16,3968]{1,0:T(8,128)(2,1)S(1)}, bf16[16,3968]{1,0:T(8,128)(2,1)S(1)}, u32[]{:S(2)}, u32[]{:S(2)}) %collective-permute-start.35) | collective-permute-done | bytes 127008 | tf_op jit(solution)/shard_map/ppermute | solution.py:483
  166.3 2.7 %collective-permute-start.39 = (bf16[24,1024]{1,0:T(8,128)(2,1)S(1)}, bf16[24,1024]{1,0:T(8,128)(2,1)S(1)}, u32[]{:S(2)}, u32[]{:S(2)}) collective-permute-start(bf16[24,1024]{1,0:T(8,128)(2,1)S(1)} %get-tuple-element.136), channel_id=1, source_target_pairs={{0,24},{1,25},{2,26},{3,27},{4,28},{5,29},{6,30},{7,31},{8,16},{9,... | collective-permute-start | bytes 147464 | tf_op jit(solution)/shard_map/ppermute | solution.py:483
  169.0 0.8 collective-permute-start.38
  169.8 0.7 reshape.173
  170.6 0.7 reshape.168
  172.6 1.4 collective-permute-done.38
  174.6 0.7 reshape.163
  175.3 0.7 reshape.165
  176.0 0.7 reshape.164
  (111 shorter events, 8.8 us)
Async XLA Ops:
  0.6 18.2 %copy-start.3 = (bf16[27648]{0:T(1024)(128)(2,1)S(1)}, bf16[27648]{0:T(1024)(128)(2,1)}, u32[]{:S(2)}) copy-start(bf16[27648]{0:T(1024)(128)(2,1)} %param.19) | copy-start | bytes 165892
  0.7 18.4 %copy-start.5 = (bf16[27648]{0:T(1024)(128)(2,1)S(1)}, bf16[27648]{0:T(1024)(128)(2,1)}, u32[]{:S(2)}) copy-start(bf16[27648]{0:T(1024)(128)(2,1)} %param.18) | copy-start | bytes 165892
  0.7 18.3 %copy-start.4 = (bf16[27648]{0:T(1024)(128)(2,1)S(1)}, bf16[27648]{0:T(1024)(128)(2,1)}, u32[]{:S(2)}) copy-start(bf16[27648]{0:T(1024)(128)(2,1)} %param.17) | copy-start | bytes 165892
  0.7 18.1 %copy-start.6 = (bf16[10368]{0:T(1024)(128)(2,1)S(1)}, bf16[10368]{0:T(1024)(128)(2,1)}, u32[]{:S(2)}) copy-start(bf16[10368]{0:T(1024)(128)(2,1)} %param.16) | copy-start | bytes 62212
  0.7 18.5 %copy-start.1 = (bf16[512,576]{0,1:T(8,128)(2,1)S(1)}, bf16[512,576]{0,1:T(8,128)(2,1)}, u32[]{:S(2)}) copy-start(bf16[512,576]{0,1:T(8,128)(2,1)} %param.22) | copy-start | bytes 1769476
  0.7 18.5 %copy-start = (bf16[512,576]{0,1:T(8,128)(2,1)S(1)}, bf16[512,576]{0,1:T(8,128)(2,1)}, u32[]{:S(2)}) copy-start(bf16[512,576]{0,1:T(8,128)(2,1)} %param.12) | copy-start | bytes 1769476
  3.9 8.2 %collective-permute-start.1 = (bf16[24,1024]{1,0:T(8,128)(2,1)S(1)}, bf16[24,1024]{1,0:T(8,128)(2,1)S(1)}, u32[]{:S(2)}, u32[]{:S(2)}) collective-permute-start(bf16[24,1024]{1,0:T(8,128)(2,1)S(1)} %fusion.17), channel_id=1, source_target_pairs={{0,16},{1,17},{2,18},{3,19},{4,20},{5,21},{6,22},{7,23},{8,24},{9,... | collective-permute-start | bytes 147464 | tf_op jit(solution)/shard_map/ppermute | solution.py:483
  8.0 4.1 %collective-permute-start = (bf16[24,1024]{1,0:T(8,128)(2,1)S(1)}, bf16[24,1024]{1,0:T(8,128)(2,1)S(1)}, u32[]{:S(2)}, u32[]{:S(2)}) collective-permute-start(bf16[24,1024]{1,0:T(8,128)(2,1)S(1)} %fusion.17), channel_id=1, source_target_pairs={{0,8},{1,9},{2,10},{3,11},{4,12},{5,13},{6,14},{7,15},{8,0},{9,1},... | collective-permute-start | bytes 147464 | tf_op jit(solution)/shard_map/ppermute | solution.py:483
  9.6 5.9 %collective-permute-start.2 = (bf16[24,1024]{1,0:T(8,128)(2,1)S(1)}, bf16[24,1024]{1,0:T(8,128)(2,1)S(1)}, u32[]{:S(2)}, u32[]{:S(2)}) collective-permute-start(bf16[24,1024]{1,0:T(8,128)(2,1)S(1)} %fusion.17), channel_id=1, source_target_pairs={{0,24},{1,25},{2,26},{3,27},{4,28},{5,29},{6,30},{7,31},{8,16},{9,... | collective-permute-start | bytes 147464 | tf_op jit(solution)/shard_map/ppermute | solution.py:483
  15.5 5.7 %collective-permute-start.3 = (bf16[4,24,1024]{2,1,0:T(8,128)(2,1)S(1)}, bf16[4,24,1024]{2,1,0:T(8,128)(2,1)S(1)}, u32[]{:S(2)}, u32[]{:S(2)}) collective-permute-start(bf16[4,24,1024]{2,1,0:T(8,128)(2,1)S(1)} %get-tuple-element.139), channel_id=1, source_target_pairs={{0,1},{1,0},{2,3},{3,2},{4,5},{5,4},{6,7},{7,6},{8,9},{9,8},{10,11... | collective-permute-start | bytes 589832 | tf_op jit(solution)/shard_map/ppermute | solution.py:483
  21.3 6.7 %collective-permute-start.6 = (bf16[16,3328]{1,0:T(8,128)(2,1)S(1)}, bf16[16,3328]{1,0:T(8,128)(2,1)S(1)}, u32[]{:S(2)}, u32[]{:S(2)}) collective-permute-start(bf16[16,3328]{1,0:T(8,128)(2,1)S(1)} %get-tuple-element.75), channel_id=1, source_target_pairs={{0,24},{1,25},{2,26},{3,27},{4,28},{5,29},{6,30},{7,31},{8,16},{9,... | collective-permute-start | bytes 319496 | tf_op jit(solution)/shard_map/ppermute | solution.py:483
  22.0 8.8 %collective-permute-start.5 = (bf16[16,3328]{1,0:T(8,128)(2,1)S(1)}, bf16[16,3328]{1,0:T(8,128)(2,1)S(1)}, u32[]{:S(2)}, u32[]{:S(2)}) collective-permute-start(bf16[16,3328]{1,0:T(8,128)(2,1)S(1)} %get-tuple-element.75), channel_id=1, source_target_pairs={{0,16},{1,17},{2,18},{3,19},{4,20},{5,21},{6,22},{7,23},{8,24},{9,... | collective-permute-start | bytes 319496 | tf_op jit(solution)/shard_map/ppermute | solution.py:483
  22.0 8.8 %collective-permute-start.4 = (bf16[16,3328]{1,0:T(8,128)(2,1)S(1)}, bf16[16,3328]{1,0:T(8,128)(2,1)S(1)}, u32[]{:S(2)}, u32[]{:S(2)}) collective-permute-start(bf16[16,3328]{1,0:T(8,128)(2,1)S(1)} %get-tuple-element.75), channel_id=1, source_target_pairs={{0,8},{1,9},{2,10},{3,11},{4,12},{5,13},{6,14},{7,15},{8,0},{9,1},... | collective-permute-start | bytes 319496 | tf_op jit(solution)/shard_map/ppermute | solution.py:483
  25.9 7.8 %collective-permute-start.7 = (bf16[2,4,24,1024]{3,2,1,0:T(8,128)(2,1)S(1)}, bf16[2,4,24,1024]{3,2,1,0:T(8,128)(2,1)S(1)}, u32[]{:S(2)}, u32[]{:S(2)}) collective-permute-start(bf16[2,4,24,1024]{3,2,1,0:T(8,128)(2,1)S(1)} %pad_maximum_fusion.4), channel_id=1, source_target_pairs={{0,4},{1,5},{2,6},{3,7},{4,0},{5,1},{6,2},{7,3},{8,12},{9,13},{10,... | collective-permute-start | bytes 1179656 | tf_op jit(solution)/shard_map/ppermute | solution.py:483
  33.6 6.5 %collective-permute-start.12 = (bf16[16,2816]{1,0:T(8,128)(2,1)S(1)}, bf16[16,2816]{1,0:T(8,128)(2,1)S(1)}, u32[]{:S(2)}, u32[]{:S(2)}) collective-permute-start(bf16[16,2816]{1,0:T(8,128)(2,1)S(1)} %get-tuple-element.84), channel_id=1, source_target_pairs={{0,24},{1,25},{2,26},{3,27},{4,28},{5,29},{6,30},{7,31},{8,16},{9,... | collective-permute-start | bytes 270344 | tf_op jit(solution)/shard_map/ppermute | solution.py:483
  34.4 7.4 %collective-permute-start.11 = (bf16[16,2816]{1,0:T(8,128)(2,1)S(1)}, bf16[16,2816]{1,0:T(8,128)(2,1)S(1)}, u32[]{:S(2)}, u32[]{:S(2)}) collective-permute-start(bf16[16,2816]{1,0:T(8,128)(2,1)S(1)} %get-tuple-element.84), channel_id=1, source_target_pairs={{0,16},{1,17},{2,18},{3,19},{4,20},{5,21},{6,22},{7,23},{8,24},{9,... | collective-permute-start | bytes 270344 | tf_op jit(solution)/shard_map/ppermute | solution.py:483
  35.1 6.6 %collective-permute-start.10 = (bf16[16,2816]{1,0:T(8,128)(2,1)S(1)}, bf16[16,2816]{1,0:T(8,128)(2,1)S(1)}, u32[]{:S(2)}, u32[]{:S(2)}) collective-permute-start(bf16[16,2816]{1,0:T(8,128)(2,1)S(1)} %get-tuple-element.84), channel_id=1, source_target_pairs={{0,8},{1,9},{2,10},{3,11},{4,12},{5,13},{6,14},{7,15},{8,0},{9,1},... | collective-permute-start | bytes 270344 | tf_op jit(solution)/shard_map/ppermute | solution.py:483
  38.0 8.1 %collective-permute-start.13 = (bf16[4,16,3328]{2,1,0:T(8,128)(2,1)S(1)}, bf16[4,16,3328]{2,1,0:T(8,128)(2,1)S(1)}, u32[]{:S(2)}, u32[]{:S(2)}) collective-permute-start(bf16[4,16,3328]{2,1,0:T(8,128)(2,1)S(1)} %pad_maximum_fusion.3), channel_id=1, source_target_pairs={{0,1},{1,0},{2,3},{3,2},{4,5},{5,4},{6,7},{7,6},{8,9},{9,8},{10,11... | collective-permute-start | bytes 1277960 | tf_op jit(solution)/shard_map/ppermute | solution.py:483
  39.6 6.6 %collective-permute-start.8 = (bf16[384,1024]{1,0:T(8,128)(2,1)S(1)}, bf16[384,1024]{1,0:T(8,128)(2,1)S(1)}, u32[]{:S(2)}, u32[]{:S(2)}) collective-permute-start(bf16[384,1024]{1,0:T(8,128)(2,1)S(1)} %bitcast.116), channel_id=1, source_target_pairs={{0,2},{1,3},{2,0},{3,1},{4,6},{5,7},{6,4},{7,5},{8,10},{9,11},{10,... | collective-permute-start | bytes 2359304 | tf_op jit(solution)/shard_map/ppermute | solution.py:483
  49.0 13.6 %collective-permute-start.9 = (bf16[512,384]{1,0:T(8,128)(2,1)S(1)}, bf16[512,384]{1,0:T(8,128)(2,1)S(1)}, u32[]{:S(2)}, u32[]{:S(2)}) collective-permute-start(bf16[512,384]{1,0:T(8,128)(2,1)S(1)} %get-tuple-element.79.kv_ref), channel_id=1, source_target_pairs={{0,1},{1,0},{2,3},{3,2},{4,5},{5,4},{6,7},{7,6},{8,9},{9,8},{10,11... | collective-permute-start | bytes 1179656 | tf_op jit(solution)/shard_map/ppermute | solution.py:483
  50.5 11.4 %collective-permute-start.14 = (bf16[4,16,2816]{2,1,0:T(8,128)(2,1)S(1)}, bf16[4,16,2816]{2,1,0:T(8,128)(2,1)S(1)}, u32[]{:S(2)}, u32[]{:S(2)}) collective-permute-start(bf16[4,16,2816]{2,1,0:T(8,128)(2,1)S(1)} %pad_maximum_fusion.5), channel_id=1, source_target_pairs={{0,4},{1,5},{2,6},{3,7},{4,0},{5,1},{6,2},{7,3},{8,12},{9,13},{10,... | collective-permute-start | bytes 1081352 | tf_op jit(solution)/shard_map/ppermute | solution.py:483
  52.0 25.7 %collective-permute-start.16 = (bf16[2,4,16,3328]{3,2,1,0:T(8,128)(2,1)S(1)}, bf16[2,4,16,3328]{3,2,1,0:T(8,128)(2,1)S(1)}, u32[]{:S(2)}, u32[]{:S(2)}) collective-permute-start(bf16[2,4,16,3328]{3,2,1,0:T(8,128)(2,1)S(1)} %pad_maximum_fusion), channel_id=1, source_target_pairs={{0,4},{1,5},{2,6},{3,7},{4,0},{5,1},{6,2},{7,3},{8,12},{9,13},{10,... | collective-permute-start | bytes 2555912 | tf_op jit(solution)/shard_map/ppermute | solution.py:483
  52.5 25.7 %collective-permute-start.17 = (bf16[128,3328]{1,0:T(8,128)(2,1)S(1)}, bf16[128,3328]{1,0:T(8,128)(2,1)S(1)}, u32[]{:S(2)}, u32[]{:S(2)}) collective-permute-start(bf16[128,3328]{1,0:T(8,128)(2,1)S(1)} %bitcast.119), channel_id=1, source_target_pairs={{0,2},{1,3},{2,0},{3,1},{4,6},{5,7},{6,4},{7,5},{8,10},{9,11},{10,... | collective-permute-start | bytes 2555912 | tf_op jit(solution)/shard_map/ppermute | solution.py:483
  61.9 15.8 %collective-permute-start.15 = (bf16[2,4,16,2816]{3,2,1,0:T(8,128)(2,1)S(1)}, bf16[2,4,16,2816]{3,2,1,0:T(8,128)(2,1)S(1)}, u32[]{:S(2)}, u32[]{:S(2)}) collective-permute-start(bf16[2,4,16,2816]{3,2,1,0:T(8,128)(2,1)S(1)} %pad_maximum_fusion.2), channel_id=1, source_target_pairs={{0,1},{1,0},{2,3},{3,2},{4,5},{5,4},{6,7},{7,6},{8,9},{9,8},{10,11... | collective-permute-start | bytes 2162696 | tf_op jit(solution)/shard_map/ppermute | solution.py:483
  77.7 4.4 %collective-permute-start.18 = (bf16[128,3328]{1,0:T(8,128)(2,1)S(1)}, bf16[128,3328]{1,0:T(8,128)(2,1)S(1)}, u32[]{:S(2)}, u32[]{:S(2)}) collective-permute-start(bf16[128,3328]{1,0:T(8,128)(2,1)S(1)} %bitcast.125), channel_id=1, source_target_pairs={{0,2},{1,3},{2,0},{3,1},{4,6},{5,7},{6,4},{7,5},{8,10},{9,11},{10,... | collective-permute-start | bytes 2555912 | tf_op jit(solution)/shard_map/ppermute | solution.py:483
  77.7 3.4 %collective-permute-start.19 = (bf16[128,2816]{1,0:T(8,128)(2,1)S(1)}, bf16[128,2816]{1,0:T(8,128)(2,1)S(1)}, u32[]{:S(2)}, u32[]{:S(2)}) collective-permute-start(bf16[128,2816]{1,0:T(8,128)(2,1)S(1)} %bitcast.121), channel_id=1, source_target_pairs={{0,2},{1,3},{2,0},{3,1},{4,6},{5,7},{6,4},{7,5},{8,10},{9,11},{10,... | collective-permute-start | bytes 2162696 | tf_op jit(solution)/shard_map/ppermute | solution.py:483
  78.2 3.9 %collective-permute-start.20 = (bf16[128,2816]{1,0:T(8,128)(2,1)S(1)}, bf16[128,2816]{1,0:T(8,128)(2,1)S(1)}, u32[]{:S(2)}, u32[]{:S(2)}) collective-permute-start(bf16[128,2816]{1,0:T(8,128)(2,1)S(1)} %bitcast.127), channel_id=1, source_target_pairs={{0,2},{1,3},{2,0},{3,1},{4,6},{5,7},{6,4},{7,5},{8,10},{9,11},{10,... | collective-permute-start | bytes 2162696 | tf_op jit(solution)/shard_map/ppermute | solution.py:483
  101.2 11.6 %collective-permute-start.21 = (bf16[256,3968]{1,0:T(8,128)(2,1)S(1)}, bf16[256,3968]{1,0:T(8,128)(2,1)S(1)}, u32[]{:S(2)}, u32[]{:S(2)}) collective-permute-start(bf16[256,3968]{1,0:T(8,128)(2,1)S(1)} %get-tuple-element.100), channel_id=1, source_target_pairs={{0,2},{1,3},{2,0},{3,1},{4,6},{5,7},{6,4},{7,5},{8,10},{9,11},{10,... | collective-permute-start | bytes 6094856 | tf_op jit(solution)/shard_map/ppermute | solution.py:483
  101.3 11.2 %collective-permute-start.22 = (bf16[256,2176]{1,0:T(8,128)(2,1)S(1)}, bf16[256,2176]{1,0:T(8,128)(2,1)S(1)}, u32[]{:S(2)}, u32[]{:S(2)}) collective-permute-start(bf16[256,2176]{1,0:T(8,128)(2,1)S(1)} %get-tuple-element.102), channel_id=1, source_target_pairs={{0,2},{1,3},{2,0},{3,1},{4,6},{5,7},{6,4},{7,5},{8,10},{9,11},{10,... | collective-permute-start | bytes 3342344 | tf_op jit(solution)/shard_map/ppermute | solution.py:483
  102.9 21.3 %collective-permute-start.23 = (bf16[512,384]{1,0:T(8,128)(2,1)S(1)}, bf16[512,384]{1,0:T(8,128)(2,1)S(1)}, u32[]{:S(2)}, u32[]{:S(2)}) collective-permute-start(bf16[512,384]{1,0:T(8,128)(2,1)S(1)} %get-tuple-element.106), channel_id=1, source_target_pairs={{0,1},{1,0},{2,3},{3,2},{4,5},{5,4},{6,7},{7,6},{8,9},{9,8},{10,11... | collective-permute-start | bytes 1179656 | tf_op jit(solution)/shard_map/ppermute | solution.py:483
  113.4 20.6 %collective-permute-start.26 = (bf16[2,4,16,2176]{3,2,1,0:T(8,128)(2,1)S(1)}, bf16[2,4,16,2176]{3,2,1,0:T(8,128)(2,1)S(1)}, u32[]{:S(2)}, u32[]{:S(2)}) collective-permute-start(bf16[2,4,16,2176]{3,2,1,0:T(8,128)(2,1)S(1)} %slice_bitcast_fusion.2), channel_id=1, source_target_pairs={{0,1},{1,0},{2,3},{3,2},{4,5},{5,4},{6,7},{7,6},{8,9},{9,8},{10,11... | collective-permute-start | bytes 1671176 | tf_op jit(solution)/shard_map/ppermute | solution.py:483
  113.5 24.3 %collective-permute-start.25 = (bf16[2,4,16,3968]{3,2,1,0:T(8,128)(2,1)S(1)}, bf16[2,4,16,3968]{3,2,1,0:T(8,128)(2,1)S(1)}, u32[]{:S(2)}, u32[]{:S(2)}) collective-permute-start(bf16[2,4,16,3968]{3,2,1,0:T(8,128)(2,1)S(1)} %slice_bitcast_fusion), channel_id=1, source_target_pairs={{0,4},{1,5},{2,6},{3,7},{4,0},{5,1},{6,2},{7,3},{8,12},{9,13},{10,... | collective-permute-start | bytes 3047432 | tf_op jit(solution)/shard_map/ppermute | solution.py:483
  129.3 8.8 %collective-permute-start.24 = (bf16[384,1024]{1,0:T(8,128)(2,1)S(1)}, bf16[384,1024]{1,0:T(8,128)(2,1)S(1)}, u32[]{:S(2)}, u32[]{:S(2)}) collective-permute-start(bf16[384,1024]{1,0:T(8,128)(2,1)S(1)} %get-tuple-element.112), channel_id=1, source_target_pairs={{0,2},{1,3},{2,0},{3,1},{4,6},{5,7},{6,4},{7,5},{8,10},{9,11},{10,... | collective-permute-start | bytes 2359304 | tf_op jit(solution)/shard_map/ppermute | solution.py:483
  138.1 7.6 %collective-permute-start.27 = (bf16[4,16,2176]{2,1,0:T(8,128)(2,1)S(1)}, bf16[4,16,2176]{2,1,0:T(8,128)(2,1)S(1)}, u32[]{:S(2)}, u32[]{:S(2)}) collective-permute-start(bf16[4,16,2176]{2,1,0:T(8,128)(2,1)S(1)} %slice_bitcast_fusion.4), channel_id=1, source_target_pairs={{0,4},{1,5},{2,6},{3,7},{4,0},{5,1},{6,2},{7,3},{8,12},{9,13},{10,... | collective-permute-start | bytes 835592 | tf_op jit(solution)/shard_map/ppermute | solution.py:483
  139.7 14.3 %collective-permute-start.33 = (bf16[4,16,3968]{2,1,0:T(8,128)(2,1)S(1)}, bf16[4,16,3968]{2,1,0:T(8,128)(2,1)S(1)}, u32[]{:S(2)}, u32[]{:S(2)}) collective-permute-start(bf16[4,16,3968]{2,1,0:T(8,128)(2,1)S(1)} %slice_bitcast_fusion.3), channel_id=1, source_target_pairs={{0,1},{1,0},{2,3},{3,2},{4,5},{5,4},{6,7},{7,6},{8,9},{9,8},{10,11... | collective-permute-start | bytes 1523720 | tf_op jit(solution)/shard_map/ppermute | solution.py:483
  145.8 5.2 %collective-permute-start.29 = (bf16[16,2176]{1,0:T(8,128)(2,1)S(1)}, bf16[16,2176]{1,0:T(8,128)(2,1)S(1)}, u32[]{:S(2)}, u32[]{:S(2)}) collective-permute-start(bf16[16,2176]{1,0:T(8,128)(2,1)S(1)} %get-tuple-element.129), channel_id=1, source_target_pairs={{0,8},{1,9},{2,10},{3,11},{4,12},{5,13},{6,14},{7,15},{8,0},{9,1},... | collective-permute-start | bytes 208904 | tf_op jit(solution)/shard_map/ppermute | solution.py:483
  145.9 6.3 %collective-permute-start.31 = (bf16[16,2176]{1,0:T(8,128)(2,1)S(1)}, bf16[16,2176]{1,0:T(8,128)(2,1)S(1)}, u32[]{:S(2)}, u32[]{:S(2)}) collective-permute-start(bf16[16,2176]{1,0:T(8,128)(2,1)S(1)} %get-tuple-element.130), channel_id=1, source_target_pairs={{0,24},{1,25},{2,26},{3,27},{4,28},{5,29},{6,30},{7,31},{8,16},{9,... | collective-permute-start | bytes 208904 | tf_op jit(solution)/shard_map/ppermute | solution.py:483
  147.3 6.6 %collective-permute-start.30 = (bf16[16,2176]{1,0:T(8,128)(2,1)S(1)}, bf16[16,2176]{1,0:T(8,128)(2,1)S(1)}, u32[]{:S(2)}, u32[]{:S(2)}) collective-permute-start(bf16[16,2176]{1,0:T(8,128)(2,1)S(1)} %get-tuple-element.131), channel_id=1, source_target_pairs={{0,16},{1,17},{2,18},{3,19},{4,20},{5,21},{6,22},{7,23},{8,24},{9,... | collective-permute-start | bytes 208904 | tf_op jit(solution)/shard_map/ppermute | solution.py:483
  149.4 8.3 %collective-permute-start.28 = (bf16[2,4,24,1024]{3,2,1,0:T(8,128)(2,1)S(1)}, bf16[2,4,24,1024]{3,2,1,0:T(8,128)(2,1)S(1)}, u32[]{:S(2)}, u32[]{:S(2)}) collective-permute-start(bf16[2,4,24,1024]{3,2,1,0:T(8,128)(2,1)S(1)} %bitcast.140), channel_id=1, source_target_pairs={{0,4},{1,5},{2,6},{3,7},{4,0},{5,1},{6,2},{7,3},{8,12},{9,13},{10,... | collective-permute-start | bytes 1179656 | tf_op jit(solution)/shard_map/ppermute | solution.py:483
  154.0 12.0 %copy-start.2 = (f32[16,2176]{1,0:T(8,128)}, f32[16,2176]{1,0:T(8,128)S(1)}, u32[]{:S(2)}) copy-start(f32[16,2176]{1,0:T(8,128)S(1)} %fusion.10) | copy-start | bytes 417796
  154.2 5.5 %collective-permute-start.34 = (bf16[16,3968]{1,0:T(8,128)(2,1)S(1)}, bf16[16,3968]{1,0:T(8,128)(2,1)S(1)}, u32[]{:S(2)}, u32[]{:S(2)}) collective-permute-start(bf16[16,3968]{1,0:T(8,128)(2,1)S(1)} %get-tuple-element.126), channel_id=1, source_target_pairs={{0,8},{1,9},{2,10},{3,11},{4,12},{5,13},{6,14},{7,15},{8,0},{9,1},... | collective-permute-start | bytes 380936 | tf_op jit(solution)/shard_map/ppermute | solution.py:483
  154.3 7.4 %collective-permute-start.36 = (bf16[16,3968]{1,0:T(8,128)(2,1)S(1)}, bf16[16,3968]{1,0:T(8,128)(2,1)S(1)}, u32[]{:S(2)}, u32[]{:S(2)}) collective-permute-start(bf16[16,3968]{1,0:T(8,128)(2,1)S(1)} %get-tuple-element.127), channel_id=1, source_target_pairs={{0,24},{1,25},{2,26},{3,27},{4,28},{5,29},{6,30},{7,31},{8,16},{9,... | collective-permute-start | bytes 380936 | tf_op jit(solution)/shard_map/ppermute | solution.py:483
  156.4 9.5 %collective-permute-start.35 = (bf16[16,3968]{1,0:T(8,128)(2,1)S(1)}, bf16[16,3968]{1,0:T(8,128)(2,1)S(1)}, u32[]{:S(2)}, u32[]{:S(2)}) collective-permute-start(bf16[16,3968]{1,0:T(8,128)(2,1)S(1)} %get-tuple-element.128), channel_id=1, source_target_pairs={{0,16},{1,17},{2,18},{3,19},{4,20},{5,21},{6,22},{7,23},{8,24},{9,... | collective-permute-start | bytes 380936 | tf_op jit(solution)/shard_map/ppermute | solution.py:483
  157.9 8.1 %collective-permute-start.32 = (bf16[4,24,1024]{2,1,0:T(8,128)(2,1)S(1)}, bf16[4,24,1024]{2,1,0:T(8,128)(2,1)S(1)}, u32[]{:S(2)}, u32[]{:S(2)}) collective-permute-start(bf16[4,24,1024]{2,1,0:T(8,128)(2,1)S(1)} %slice_bitcast_fusion.5), channel_id=1, source_target_pairs={{0,1},{1,0},{2,3},{3,2},{4,5},{5,4},{6,7},{7,6},{8,9},{9,8},{10,11... | collective-permute-start | bytes 589832 | tf_op jit(solution)/shard_map/ppermute | solution.py:483
  166.0 3.8 %slice-start = ((f32[16,2176]{1,0:T(8,128)}), f32[16,1536]{1,0:T(8,128)S(1)}, s32[]{:S(2)}) async-start(f32[16,2176]{1,0:T(8,128)} %copy-done.2), calls=%async_computation | async-start | bytes 196608 | tf_op jit(solution)/shard_map/slice | solution.py:1031
  166.2 6.4 %collective-permute-start.37 = (bf16[24,1024]{1,0:T(8,128)(2,1)S(1)}, bf16[24,1024]{1,0:T(8,128)(2,1)S(1)}, u32[]{:S(2)}, u32[]{:S(2)}) collective-permute-start(bf16[24,1024]{1,0:T(8,128)(2,1)S(1)} %get-tuple-element.135), channel_id=1, source_target_pairs={{0,8},{1,9},{2,10},{3,11},{4,12},{5,13},{6,14},{7,15},{8,0},{9,1},... | collective-permute-start | bytes 147464 | tf_op jit(solution)/shard_map/ppermute | solution.py:483
  166.3 6.3 %collective-permute-start.39 = (bf16[24,1024]{1,0:T(8,128)(2,1)S(1)}, bf16[24,1024]{1,0:T(8,128)(2,1)S(1)}, u32[]{:S(2)}, u32[]{:S(2)}) collective-permute-start(bf16[24,1024]{1,0:T(8,128)(2,1)S(1)} %get-tuple-element.136), channel_id=1, source_target_pairs={{0,24},{1,25},{2,26},{3,27},{4,28},{5,29},{6,30},{7,31},{8,16},{9,... | collective-permute-start | bytes 147464 | tf_op jit(solution)/shard_map/ppermute | solution.py:483
  169.0 5.0 %collective-permute-start.38 = (bf16[24,1024]{1,0:T(8,128)(2,1)S(1)}, bf16[24,1024]{1,0:T(8,128)(2,1)S(1)}, u32[]{:S(2)}, u32[]{:S(2)}) collective-permute-start(bf16[24,1024]{1,0:T(8,128)(2,1)S(1)} %get-tuple-element.137), channel_id=1, source_target_pairs={{0,16},{1,17},{2,18},{3,19},{4,20},{5,21},{6,22},{7,23},{8,24},{9,... | collective-permute-start | bytes 147464 | tf_op jit(solution)/shard_map/ppermute | solution.py:483

commit v3 on v2

--- a/solution.py
+++ b/solution.py
@@ -227,24 +227,25 @@
             vs[g] = kv_ref[:, kv_width + lo : kv_width + lo + HEAD_DIM]
         kts[...] = jnp.transpose(kv_ref[:, :kv_width].astype(F32)).astype(BF)
 
-        @pl.loop(0, heads)
-        def _(h):
-            g = h // group
+        @pl.loop(0, KV_HEADS)
+        def _(g):
             k_rows = pl.ds(pl.multiple_of(g * HEAD_DIM, HEAD_DIM), HEAD_DIM)
-            out_rows = pl.ds(pl.multiple_of(h * HEAD_DIM, HEAD_DIM), HEAD_DIM)
-            for at in range(rows // block):
-                stop = (at + 1) * block if own else rows
-                cols = slice(at * block, (at + 1) * block)
-                q = qs[h, cols]
-                do = dos[h, cols]
-                s = times_back(ks[g, :stop], q) + bias[:stop, cols]
-                p = jnp.exp(s - lse_ref[h, :, cols])
-                dp = times_back(vs[g, :stop], do)
-                ds = (p * (dp - delta_ref[h, :, cols])).astype(BF)
-                dk[g, :stop] += times(ds, q)
-                dv[g, :stop] += times(p.astype(BF), do)
-                dq = times(kts[k_rows, :stop], ds) * HEAD_DIM**-0.5
-                dq_t[out_rows, cols] = before[out_rows, cols] + dq if own else dq
+            for j in range(group):
+                h = g * group + j
+                out_rows = pl.ds(pl.multiple_of(h * HEAD_DIM, HEAD_DIM), HEAD_DIM)
+                for at in range(rows // block):
+                    stop = (at + 1) * block if own else rows
+                    cols = slice(at * block, (at + 1) * block)
+                    q = qs[h, cols]
+                    do = dos[h, cols]
+                    s = times_back(ks[g, :stop], q) + bias[:stop, cols]
+                    p = jnp.exp(s - lse_ref[h, :, cols])
+                    dp = times_back(vs[g, :stop], do)
+                    ds = (p * (dp - delta_ref[h, :, cols])).astype(BF)
+                    dk[g, :stop] += times(ds, q)
+                    dv[g, :stop] += times(p.astype(BF), do)
+                    dq = times(kts[k_rows, :stop], ds) * HEAD_DIM**-0.5
+                    dq_t[out_rows, cols] = before[out_rows, cols] + dq if own else dq
 
     if own:
         run()

time: 177 us -> 176 us (level)
  no operation moved by 1% of the time
where the time goes in v3:
time: 176 us
  waiting for transfers between devices  62.1 us (35%)
  starting transfers between devices  51.9 us (29%)
  Pallas kernels  44.7 us (25%)
  local copies, waits for them, and re-layouts  8.76 us (5%)
  other arithmetic  7.22 us (4%)
    ppermute x40, waiting for transfers between devices, swap(): return lax.ppermute(values, AXES, perm)  62.1 us
    ppermute x40, starting transfers between devices, swap(): return lax.ppermute(values, AXES, perm)  51.9 us
    pallas_call x4, Pallas kernels, call(): pl.pallas_call(kernel, out_shape=shapes, in_specs=specs, out_specs=[here...  27.7 us
    pallas_call x2, Pallas kernels, attention_grad(): pl.pallas_call(functools.partial(attn_grad_kernel, heads, min(rows, 256),...  9.49 us
    pallas_call x1, Pallas kernels, attention_own(): pl.pallas_call(functools.partial(attn_own_kernel, heads, min(rows, 256),...  6.47 us
  transfers between devices with their start and end apart: 40, of which 21 were waited for; matrix products, arithmetic and copies ran while one was open for 6% of the time, Pallas kernels for 13%

profile of v3, /device:TPU:0, one launch (start us, length us, event | category | flops | bytes accessed | tf_op | source)
XLA Modules:
  0.0 175.8 jit_solution(16082444882091452735)
XLA Ops:
  0.7 0.9 reshape.148
  1.6 0.8 reshape.149
  2.4 0.8 reshape.147
  3.3 0.7 fusion.17
  3.9 4.1 %collective-permute-start.1 = (bf16[24,1024]{1,0:T(8,128)(2,1)S(1)}, bf16[24,1024]{1,0:T(8,128)(2,1)S(1)}, u32[]{:S(2)}, u32[]{:S(2)}) collective-permute-start(bf16[24,1024]{1,0:T(8,128)(2,1)S(1)} %fusion.17), channel_id=1, source_target_pairs={{0,16},{1,17},{2,18},{3,19},{4,20},{5,21},{6,22},{7,23},{8,24},{9,... | collective-permute-start | bytes 147464 | tf_op jit(solution)/shard_map/ppermute | solution.py:484
  8.0 1.6 collective-permute-start
  9.6 0.8 reduce-window.4
  10.4 0.7 fusion.20
  11.1 0.7 fusion.26
  12.1 3.4 %collective-permute-done.2 = bf16[24,1024]{1,0:T(8,128)(2,1)S(1)} collective-permute-done((bf16[24,1024]{1,0:T(8,128)(2,1)S(1)}, bf16[24,1024]{1,0:T(8,128)(2,1)S(1)}, u32[]{:S(2)}, u32[]{:S(2)}) %collective-permute-start.2) | collective-permute-done | bytes 49184 | tf_op jit(solution)/shard_map/ppermute | solution.py:484
  15.5 1.6 collective-permute-start.3
  17.1 1.6 fusion.6
  19.2 0.9 wire.1
  20.1 1.2 collective-permute-done.3
  21.3 0.7 collective-permute-start.6
  22.0 3.7 %collective-permute-start.4 = (bf16[16,3328]{1,0:T(8,128)(2,1)S(1)}, bf16[16,3328]{1,0:T(8,128)(2,1)S(1)}, u32[]{:S(2)}, u32[]{:S(2)}) collective-permute-start(bf16[16,3328]{1,0:T(8,128)(2,1)S(1)} %get-tuple-element.75), channel_id=1, source_target_pairs={{0,8},{1,9},{2,10},{3,11},{4,12},{5,13},{6,14},{7,15},{8,0},{9,1},... | collective-permute-start | bytes 319496 | tf_op jit(solution)/shard_map/ppermute | solution.py:484
  25.9 1.5 collective-permute-start.7
  27.4 0.7 collective-permute-done.6
  28.1 2.8 %collective-permute-done.5 = bf16[16,3328]{1,0:T(8,128)(2,1)S(1)} collective-permute-done((bf16[16,3328]{1,0:T(8,128)(2,1)S(1)}, bf16[16,3328]{1,0:T(8,128)(2,1)S(1)}, u32[]{:S(2)}, u32[]{:S(2)}) %collective-permute-start.5) | collective-permute-done | bytes 106528 | tf_op jit(solution)/shard_map/ppermute | solution.py:484
  30.9 2.7 %collective-permute-done.7 = bf16[2,4,24,1024]{3,2,1,0:T(8,128)(2,1)S(1)} collective-permute-done((bf16[2,4,24,1024]{3,2,1,0:T(8,128)(2,1)S(1)}, bf16[2,4,24,1024]{3,2,1,0:T(8,128)(2,1)S(1)}, u32[]{:S(2)}, u32[]{:S(2)}) %collective-permute-start.7) | collective-permute-done | bytes 393248 | tf_op jit(solution)/shard_map/ppermute | solution.py:484
  33.6 0.7 collective-permute-start.12
  34.4 0.7 collective-permute-start.11
  35.1 2.9 %collective-permute-start.10 = (bf16[16,2816]{1,0:T(8,128)(2,1)S(1)}, bf16[16,2816]{1,0:T(8,128)(2,1)S(1)}, u32[]{:S(2)}, u32[]{:S(2)}) collective-permute-start(bf16[16,2816]{1,0:T(8,128)(2,1)S(1)} %get-tuple-element.84), channel_id=1, source_target_pairs={{0,8},{1,9},{2,10},{3,11},{4,12},{5,13},{6,14},{7,15},{8,0},{9,1},... | collective-permute-start | bytes 270344 | tf_op jit(solution)/shard_map/ppermute | solution.py:484
  38.0 1.5 collective-permute-start.13
  40.1 1.6 collective-permute-done.11
  41.8 4.4 %collective-permute-done.13 = bf16[4,16,3328]{2,1,0:T(8,128)(2,1)S(1)} collective-permute-done((bf16[4,16,3328]{2,1,0:T(8,128)(2,1)S(1)}, bf16[4,16,3328]{2,1,0:T(8,128)(2,1)S(1)}, u32[]{:S(2)}, u32[]{:S(2)}) %collective-permute-start.13) | collective-permute-done | bytes 426016 | tf_op jit(solution)/shard_map/ppermute | solution.py:484
  46.2 2.7 %norm_qkv.1 = (bf16[512,576]{1,0:T(8,128)(2,1)S(1)}, bf16[512,384]{1,0:T(8,128)(2,1)S(1)}, bf16[768,512]{1,0:T(8,128)(2,1)S(1)}, f32[1,2304]{1,0:T(1,128)S(1)}) custom-call(s32[1]{0:T(128)} %bitcast.me_ref, bf16[512,576]{1,0:T(8,128)(2,1)S(1)} %get-tuple-element.71.x_ref, bf16[384,1024]{1,0:T(8,128)(2,1)S(1)} %bitcast.117, ...), custom_call_target="tpu_custom_call" | custom-call | flops 3300000000 | bytes 1048576 | tf_op jit(solution)/shard_map/norm_qkv/pallas_call | solution.py:849
  49.0 1.6 collective-permute-start.9
  50.5 1.5 collective-permute-start.14
  52.5 6.5 %attn_own.1 = (f32[576,512]{1,0:T(8,128)S(1)}, f32[9,1,512]{2,1,0:T(1,128)S(1)}, f32[9,1,512]{2,1,0:T(1,128)S(1)}) custom-call(s32[6]{0:T(128)S(1)} %pad_add_fusion.info, bf16[512,576]{1,0:T(8,128)(2,1)S(1)} %get-tuple-element.78.q_ref, bf16[512,384]{1,0:T(8,128)(2,1)S(1)} %get-tuple-element.79.kv_ref), custom_call_target="tpu_custom_call" | custom-call | flops 6600000000 | bytes 1048576 | tf_op jit(solution)/shard_map/attn_own/pallas_call | solution.py:362
  59.0 2.8 %collective-permute-done.14 = bf16[4,16,2816]{2,1,0:T(8,128)(2,1)S(1)} collective-permute-done((bf16[4,16,2816]{2,1,0:T(8,128)(2,1)S(1)}, bf16[4,16,2816]{2,1,0:T(8,128)(2,1)S(1)}, u32[]{:S(2)}, u32[]{:S(2)}) %collective-permute-start.14) | collective-permute-done | bytes 360480 | tf_op jit(solution)/shard_map/ppermute | solution.py:484
  62.5 1.1 attn_others.1
  63.6 14.1 %collective-permute-done.15 = bf16[2,4,16,2816]{3,2,1,0:T(8,128)(2,1)S(1)} collective-permute-done((bf16[2,4,16,2816]{3,2,1,0:T(8,128)(2,1)S(1)}, bf16[2,4,16,2816]{3,2,1,0:T(8,128)(2,1)S(1)}, u32[]{:S(2)}, u32[]{:S(2)}) %collective-permute-start.15) | collective-permute-done | bytes 720928 | tf_op jit(solution)/shard_map/ppermute | solution.py:484
  78.2 2.9 %collective-permute-done.19.b2_10 = bf16[128,2816]{1,0:T(8,128)(2,1)S(1)} collective-permute-done((bf16[128,2816]{1,0:T(8,128)(2,1)S(1)}, bf16[128,2816]{1,0:T(8,128)(2,1)S(1)}, u32[]{:S(2)}, u32[]{:S(2)}) %collective-permute-start.19) | collective-permute-done | bytes 720928 | tf_op jit(solution)/shard_map/ppermute | solution.py:484
  81.1 1.0 collective-permute-done.20.b2_11
  82.2 19.0 %feed_forward.1 = (bf16[576,512]{1,0:T(8,128)(2,1)}, bf16[256,3968]{1,0:T(8,128)(2,1)S(1)}, bf16[256,3968]{1,0:T(8,128)(2,1)S(1)}, bf16[256,2176]{1,0:T(8,128)(2...) custom-call(s32[1]{0:T(128)} %bitcast.me_ref, ...), custom_call_target="tpu_custom_call" | custom-call | flops 23100000256 | bytes 1048576 | tf_op jit(solution)/shard_map/feed_forward/pallas_call | solution.py:849
  101.7 1.2 attn_grad_others.1
  102.9 8.8 %collective-permute-start.23 = (bf16[512,384]{1,0:T(8,128)(2,1)S(1)}, bf16[512,384]{1,0:T(8,128)(2,1)S(1)}, u32[]{:S(2)}, u32[]{:S(2)}) collective-permute-start(bf16[512,384]{1,0:T(8,128)(2,1)S(1)} %get-tuple-element.106), channel_id=1, source_target_pairs={{0,1},{1,0},{2,3},{3,2},{4,5},{5,4},{6,7},{7,6},{8,9},{9,8},{10,11... | collective-permute-start | bytes 1179656 | tf_op jit(solution)/shard_map/ppermute | solution.py:484
  112.6 1.6 collective-permute-start.25
  114.2 8.3 %attn_grad_own.1 = (f32[512,576]{1,0:T(8,128)S(1)}, f32[512,384]{1,0:T(8,128)S(1)}) custom-call(s32[6]{0:T(128)S(1)} %pad_add_fusion.info, bf16[512,576]{1,0:T(8,128)(2,1)S(1)} %get-tuple-element.78.q_ref, bf16[512,384]{1,0:T(8,128)(2,1)S(1)} %get-tuple-element.79.kv_ref, bf16[512,576]{1,0:T(8,128)(2,1)S(1)} %get-tuple-element.95.do_ref, ...), custom_call_target="tpu_custom_call" | custom-call | flops 2750000128 | bytes 1048576 | tf_op jit(solution)/shard_map/attn_grad_own/pallas_call | solution.py:395
  122.5 5.0 %norm_qkv_back.1 = (f32[576,512]{1,0:T(8,128)}, bf16[384,1024]{1,0:T(8,128)(2,1)S(1)}, bf16[384,1024]{1,0:T(8,128)(2,1)S(1)}) custom-call(s32[1]{0:T(128)} %bitcast.me_ref, f32[512,576]{1,0:T(8,128)S(1)} %get-tuple-element.104.dq_ref, f32[512,384]{1,0:T(8,128)S(1)} %get-tuple-element.105.dkv_ref, bf16[512,384]{1,0:T(8,128)(2,1)S(1)} %collective-permute-done.23.got_ref, ...), custom_call_target="tpu_custom_call" | custom-call | flops 1650000000 | bytes 1048576 | tf_op jit(solution)/shard_map/norm_qkv_back/pallas_call | solution.py:849
  127.6 5.5 %collective-permute-done.26 = bf16[2,4,16,2176]{3,2,1,0:T(8,128)(2,1)S(1)} collective-permute-done((bf16[2,4,16,2176]{3,2,1,0:T(8,128)(2,1)S(1)}, bf16[2,4,16,2176]{3,2,1,0:T(8,128)(2,1)S(1)}, u32[]{:S(2)}, u32[]{:S(2)}) %collective-permute-start.26) | collective-permute-done | bytes 557088 | tf_op jit(solution)/shard_map/ppermute | solution.py:484
  133.2 3.8 %collective-permute-done.25 = bf16[2,4,16,3968]{3,2,1,0:T(8,128)(2,1)S(1)} collective-permute-done((bf16[2,4,16,3968]{3,2,1,0:T(8,128)(2,1)S(1)}, bf16[2,4,16,3968]{3,2,1,0:T(8,128)(2,1)S(1)}, u32[]{:S(2)}, u32[]{:S(2)}) %collective-permute-start.25) | collective-permute-done | bytes 1015840 | tf_op jit(solution)/shard_map/ppermute | solution.py:484
  137.2 1.6 collective-permute-start.27
  138.8 1.8 %collective-permute-start.33 = (bf16[4,16,3968]{2,1,0:T(8,128)(2,1)S(1)}, bf16[4,16,3968]{2,1,0:T(8,128)(2,1)S(1)}, u32[]{:S(2)}, u32[]{:S(2)}) collective-permute-start(bf16[4,16,3968]{2,1,0:T(8,128)(2,1)S(1)} %slice_bitcast_fusion.3), channel_id=1, source_target_pairs={{0,1},{1,0},{2,3},{3,2},{4,5},{5,4},{6,7},{7,6},{8,9},{9,8},{10,11... | collective-permute-start | bytes 1523720 | tf_op jit(solution)/shard_map/ppermute | solution.py:484
  140.9 3.9 %collective-permute-done.27 = bf16[4,16,2176]{2,1,0:T(8,128)(2,1)S(1)} collective-permute-done((bf16[4,16,2176]{2,1,0:T(8,128)(2,1)S(1)}, bf16[4,16,2176]{2,1,0:T(8,128)(2,1)S(1)}, u32[]{:S(2)}, u32[]{:S(2)}) %collective-permute-start.27) | collective-permute-done | bytes 278560 | tf_op jit(solution)/shard_map/ppermute | solution.py:484
  145.0 1.5 collective-permute-start.31
  146.5 2.0 %collective-permute-start.30 = (bf16[16,2176]{1,0:T(8,128)(2,1)S(1)}, bf16[16,2176]{1,0:T(8,128)(2,1)S(1)}, u32[]{:S(2)}, u32[]{:S(2)}) collective-permute-start(bf16[16,2176]{1,0:T(8,128)(2,1)S(1)} %get-tuple-element.131), channel_id=1, source_target_pairs={{0,16},{1,17},{2,18},{3,19},{4,20},{5,21},{6,22},{7,23},{8,24},{9,... | collective-permute-start | bytes 208904 | tf_op jit(solution)/shard_map/ppermute | solution.py:484
  148.5 1.6 collective-permute-start.28
  150.1 1.2 collective-permute-done.31
  151.3 1.8 %collective-permute-done.30 = bf16[16,2176]{1,0:T(8,128)(2,1)S(1)} collective-permute-done((bf16[16,2176]{1,0:T(8,128)(2,1)S(1)}, bf16[16,2176]{1,0:T(8,128)(2,1)S(1)}, u32[]{:S(2)}, u32[]{:S(2)}) %collective-permute-start.30) | collective-permute-done | bytes 69664 | tf_op jit(solution)/shard_map/ppermute | solution.py:484
  153.4 2.2 %collective-permute-start.36 = (bf16[16,3968]{1,0:T(8,128)(2,1)S(1)}, bf16[16,3968]{1,0:T(8,128)(2,1)S(1)}, u32[]{:S(2)}, u32[]{:S(2)}) collective-permute-start(bf16[16,3968]{1,0:T(8,128)(2,1)S(1)} %get-tuple-element.127), channel_id=1, source_target_pairs={{0,24},{1,25},{2,26},{3,27},{4,28},{5,29},{6,30},{7,31},{8,16},{9,... | collective-permute-start | bytes 380936 | tf_op jit(solution)/shard_map/ppermute | solution.py:484
  155.6 1.3 collective-permute-start.35
  157.0 1.5 collective-permute-start.32
  158.8 2.0 %collective-permute-done.36 = bf16[16,3968]{1,0:T(8,128)(2,1)S(1)} collective-permute-done((bf16[16,3968]{1,0:T(8,128)(2,1)S(1)}, bf16[16,3968]{1,0:T(8,128)(2,1)S(1)}, u32[]{:S(2)}, u32[]{:S(2)}) %collective-permute-start.36) | collective-permute-done | bytes 127008 | tf_op jit(solution)/shard_map/ppermute | solution.py:484
  160.8 4.2 %collective-permute-done.35 = bf16[16,3968]{1,0:T(8,128)(2,1)S(1)} collective-permute-done((bf16[16,3968]{1,0:T(8,128)(2,1)S(1)}, bf16[16,3968]{1,0:T(8,128)(2,1)S(1)}, u32[]{:S(2)}, u32[]{:S(2)}) %collective-permute-start.35) | collective-permute-done | bytes 127008 | tf_op jit(solution)/shard_map/ppermute | solution.py:484
  165.4 2.7 %collective-permute-start.39 = (bf16[24,1024]{1,0:T(8,128)(2,1)S(1)}, bf16[24,1024]{1,0:T(8,128)(2,1)S(1)}, u32[]{:S(2)}, u32[]{:S(2)}) collective-permute-start(bf16[24,1024]{1,0:T(8,128)(2,1)S(1)} %get-tuple-element.136), channel_id=1, source_target_pairs={{0,24},{1,25},{2,26},{3,27},{4,28},{5,29},{6,30},{7,31},{8,16},{9,... | collective-permute-start | bytes 147464 | tf_op jit(solution)/shard_map/ppermute | solution.py:484
  168.1 0.8 collective-permute-start.38
  169.0 0.7 reshape.173
  169.7 0.7 reshape.168
  171.7 1.4 collective-permute-done.38
  173.7 0.7 reshape.163
  174.4 0.7 reshape.165
  175.1 0.7 reshape.164
  (111 shorter events, 8.8 us)
Async XLA Ops:
  0.6 18.2 %copy-start.3 = (bf16[27648]{0:T(1024)(128)(2,1)S(1)}, bf16[27648]{0:T(1024)(128)(2,1)}, u32[]{:S(2)}) copy-start(bf16[27648]{0:T(1024)(128)(2,1)} %param.19) | copy-start | bytes 165892
  0.7 18.4 %copy-start.5 = (bf16[27648]{0:T(1024)(128)(2,1)S(1)}, bf16[27648]{0:T(1024)(128)(2,1)}, u32[]{:S(2)}) copy-start(bf16[27648]{0:T(1024)(128)(2,1)} %param.18) | copy-start | bytes 165892
  0.7 18.3 %copy-start.4 = (bf16[27648]{0:T(1024)(128)(2,1)S(1)}, bf16[27648]{0:T(1024)(128)(2,1)}, u32[]{:S(2)}) copy-start(bf16[27648]{0:T(1024)(128)(2,1)} %param.17) | copy-start | bytes 165892
  0.7 18.1 %copy-start.6 = (bf16[10368]{0:T(1024)(128)(2,1)S(1)}, bf16[10368]{0:T(1024)(128)(2,1)}, u32[]{:S(2)}) copy-start(bf16[10368]{0:T(1024)(128)(2,1)} %param.16) | copy-start | bytes 62212
  0.7 18.5 %copy-start.1 = (bf16[512,576]{0,1:T(8,128)(2,1)S(1)}, bf16[512,576]{0,1:T(8,128)(2,1)}, u32[]{:S(2)}) copy-start(bf16[512,576]{0,1:T(8,128)(2,1)} %param.22) | copy-start | bytes 1769476
  0.7 18.5 %copy-start = (bf16[512,576]{0,1:T(8,128)(2,1)S(1)}, bf16[512,576]{0,1:T(8,128)(2,1)}, u32[]{:S(2)}) copy-start(bf16[512,576]{0,1:T(8,128)(2,1)} %param.12) | copy-start | bytes 1769476
  3.9 8.2 %collective-permute-start.1 = (bf16[24,1024]{1,0:T(8,128)(2,1)S(1)}, bf16[24,1024]{1,0:T(8,128)(2,1)S(1)}, u32[]{:S(2)}, u32[]{:S(2)}) collective-permute-start(bf16[24,1024]{1,0:T(8,128)(2,1)S(1)} %fusion.17), channel_id=1, source_target_pairs={{0,16},{1,17},{2,18},{3,19},{4,20},{5,21},{6,22},{7,23},{8,24},{9,... | collective-permute-start | bytes 147464 | tf_op jit(solution)/shard_map/ppermute | solution.py:484
  8.0 4.1 %collective-permute-start = (bf16[24,1024]{1,0:T(8,128)(2,1)S(1)}, bf16[24,1024]{1,0:T(8,128)(2,1)S(1)}, u32[]{:S(2)}, u32[]{:S(2)}) collective-permute-start(bf16[24,1024]{1,0:T(8,128)(2,1)S(1)} %fusion.17), channel_id=1, source_target_pairs={{0,8},{1,9},{2,10},{3,11},{4,12},{5,13},{6,14},{7,15},{8,0},{9,1},... | collective-permute-start | bytes 147464 | tf_op jit(solution)/shard_map/ppermute | solution.py:484
  9.6 5.9 %collective-permute-start.2 = (bf16[24,1024]{1,0:T(8,128)(2,1)S(1)}, bf16[24,1024]{1,0:T(8,128)(2,1)S(1)}, u32[]{:S(2)}, u32[]{:S(2)}) collective-permute-start(bf16[24,1024]{1,0:T(8,128)(2,1)S(1)} %fusion.17), channel_id=1, source_target_pairs={{0,24},{1,25},{2,26},{3,27},{4,28},{5,29},{6,30},{7,31},{8,16},{9,... | collective-permute-start | bytes 147464 | tf_op jit(solution)/shard_map/ppermute | solution.py:484
  15.5 5.7 %collective-permute-start.3 = (bf16[4,24,1024]{2,1,0:T(8,128)(2,1)S(1)}, bf16[4,24,1024]{2,1,0:T(8,128)(2,1)S(1)}, u32[]{:S(2)}, u32[]{:S(2)}) collective-permute-start(bf16[4,24,1024]{2,1,0:T(8,128)(2,1)S(1)} %get-tuple-element.139), channel_id=1, source_target_pairs={{0,1},{1,0},{2,3},{3,2},{4,5},{5,4},{6,7},{7,6},{8,9},{9,8},{10,11... | collective-permute-start | bytes 589832 | tf_op jit(solution)/shard_map/ppermute | solution.py:484
  21.3 6.7 %collective-permute-start.6 = (bf16[16,3328]{1,0:T(8,128)(2,1)S(1)}, bf16[16,3328]{1,0:T(8,128)(2,1)S(1)}, u32[]{:S(2)}, u32[]{:S(2)}) collective-permute-start(bf16[16,3328]{1,0:T(8,128)(2,1)S(1)} %get-tuple-element.75), channel_id=1, source_target_pairs={{0,24},{1,25},{2,26},{3,27},{4,28},{5,29},{6,30},{7,31},{8,16},{9,... | collective-permute-start | bytes 319496 | tf_op jit(solution)/shard_map/ppermute | solution.py:484
  22.0 8.8 %collective-permute-start.5 = (bf16[16,3328]{1,0:T(8,128)(2,1)S(1)}, bf16[16,3328]{1,0:T(8,128)(2,1)S(1)}, u32[]{:S(2)}, u32[]{:S(2)}) collective-permute-start(bf16[16,3328]{1,0:T(8,128)(2,1)S(1)} %get-tuple-element.75), channel_id=1, source_target_pairs={{0,16},{1,17},{2,18},{3,19},{4,20},{5,21},{6,22},{7,23},{8,24},{9,... | collective-permute-start | bytes 319496 | tf_op jit(solution)/shard_map/ppermute | solution.py:484
  22.0 8.8 %collective-permute-start.4 = (bf16[16,3328]{1,0:T(8,128)(2,1)S(1)}, bf16[16,3328]{1,0:T(8,128)(2,1)S(1)}, u32[]{:S(2)}, u32[]{:S(2)}) collective-permute-start(bf16[16,3328]{1,0:T(8,128)(2,1)S(1)} %get-tuple-element.75), channel_id=1, source_target_pairs={{0,8},{1,9},{2,10},{3,11},{4,12},{5,13},{6,14},{7,15},{8,0},{9,1},... | collective-permute-start | bytes 319496 | tf_op jit(solution)/shard_map/ppermute | solution.py:484
  25.9 7.8 %collective-permute-start.7 = (bf16[2,4,24,1024]{3,2,1,0:T(8,128)(2,1)S(1)}, bf16[2,4,24,1024]{3,2,1,0:T(8,128)(2,1)S(1)}, u32[]{:S(2)}, u32[]{:S(2)}) collective-permute-start(bf16[2,4,24,1024]{3,2,1,0:T(8,128)(2,1)S(1)} %pad_maximum_fusion.4), channel_id=1, source_target_pairs={{0,4},{1,5},{2,6},{3,7},{4,0},{5,1},{6,2},{7,3},{8,12},{9,13},{10,... | collective-permute-start | bytes 1179656 | tf_op jit(solution)/shard_map/ppermute | solution.py:484
  33.6 6.5 %collective-permute-start.12 = (bf16[16,2816]{1,0:T(8,128)(2,1)S(1)}, bf16[16,2816]{1,0:T(8,128)(2,1)S(1)}, u32[]{:S(2)}, u32[]{:S(2)}) collective-permute-start(bf16[16,2816]{1,0:T(8,128)(2,1)S(1)} %get-tuple-element.84), channel_id=1, source_target_pairs={{0,24},{1,25},{2,26},{3,27},{4,28},{5,29},{6,30},{7,31},{8,16},{9,... | collective-permute-start | bytes 270344 | tf_op jit(solution)/shard_map/ppermute | solution.py:484
  34.4 7.4 %collective-permute-start.11 = (bf16[16,2816]{1,0:T(8,128)(2,1)S(1)}, bf16[16,2816]{1,0:T(8,128)(2,1)S(1)}, u32[]{:S(2)}, u32[]{:S(2)}) collective-permute-start(bf16[16,2816]{1,0:T(8,128)(2,1)S(1)} %get-tuple-element.84), channel_id=1, source_target_pairs={{0,16},{1,17},{2,18},{3,19},{4,20},{5,21},{6,22},{7,23},{8,24},{9,... | collective-permute-start | bytes 270344 | tf_op jit(solution)/shard_map/ppermute | solution.py:484
  35.1 6.6 %collective-permute-start.10 = (bf16[16,2816]{1,0:T(8,128)(2,1)S(1)}, bf16[16,2816]{1,0:T(8,128)(2,1)S(1)}, u32[]{:S(2)}, u32[]{:S(2)}) collective-permute-start(bf16[16,2816]{1,0:T(8,128)(2,1)S(1)} %get-tuple-element.84), channel_id=1, source_target_pairs={{0,8},{1,9},{2,10},{3,11},{4,12},{5,13},{6,14},{7,15},{8,0},{9,1},... | collective-permute-start | bytes 270344 | tf_op jit(solution)/shard_map/ppermute | solution.py:484
  38.0 8.1 %collective-permute-start.13 = (bf16[4,16,3328]{2,1,0:T(8,128)(2,1)S(1)}, bf16[4,16,3328]{2,1,0:T(8,128)(2,1)S(1)}, u32[]{:S(2)}, u32[]{:S(2)}) collective-permute-start(bf16[4,16,3328]{2,1,0:T(8,128)(2,1)S(1)} %pad_maximum_fusion.3), channel_id=1, source_target_pairs={{0,1},{1,0},{2,3},{3,2},{4,5},{5,4},{6,7},{7,6},{8,9},{9,8},{10,11... | collective-permute-start | bytes 1277960 | tf_op jit(solution)/shard_map/ppermute | solution.py:484
  39.6 6.6 %collective-permute-start.8 = (bf16[384,1024]{1,0:T(8,128)(2,1)S(1)}, bf16[384,1024]{1,0:T(8,128)(2,1)S(1)}, u32[]{:S(2)}, u32[]{:S(2)}) collective-permute-start(bf16[384,1024]{1,0:T(8,128)(2,1)S(1)} %bitcast.116), channel_id=1, source_target_pairs={{0,2},{1,3},{2,0},{3,1},{4,6},{5,7},{6,4},{7,5},{8,10},{9,11},{10,... | collective-permute-start | bytes 2359304 | tf_op jit(solution)/shard_map/ppermute | solution.py:484
  49.0 13.6 %collective-permute-start.9 = (bf16[512,384]{1,0:T(8,128)(2,1)S(1)}, bf16[512,384]{1,0:T(8,128)(2,1)S(1)}, u32[]{:S(2)}, u32[]{:S(2)}) collective-permute-start(bf16[512,384]{1,0:T(8,128)(2,1)S(1)} %get-tuple-element.79.kv_ref), channel_id=1, source_target_pairs={{0,1},{1,0},{2,3},{3,2},{4,5},{5,4},{6,7},{7,6},{8,9},{9,8},{10,11... | collective-permute-start | bytes 1179656 | tf_op jit(solution)/shard_map/ppermute | solution.py:484
  50.5 11.4 %collective-permute-start.14 = (bf16[4,16,2816]{2,1,0:T(8,128)(2,1)S(1)}, bf16[4,16,2816]{2,1,0:T(8,128)(2,1)S(1)}, u32[]{:S(2)}, u32[]{:S(2)}) collective-permute-start(bf16[4,16,2816]{2,1,0:T(8,128)(2,1)S(1)} %pad_maximum_fusion.5), channel_id=1, source_target_pairs={{0,4},{1,5},{2,6},{3,7},{4,0},{5,1},{6,2},{7,3},{8,12},{9,13},{10,... | collective-permute-start | bytes 1081352 | tf_op jit(solution)/shard_map/ppermute | solution.py:484
  52.0 25.7 %collective-permute-start.16 = (bf16[2,4,16,3328]{3,2,1,0:T(8,128)(2,1)S(1)}, bf16[2,4,16,3328]{3,2,1,0:T(8,128)(2,1)S(1)}, u32[]{:S(2)}, u32[]{:S(2)}) collective-permute-start(bf16[2,4,16,3328]{3,2,1,0:T(8,128)(2,1)S(1)} %pad_maximum_fusion), channel_id=1, source_target_pairs={{0,4},{1,5},{2,6},{3,7},{4,0},{5,1},{6,2},{7,3},{8,12},{9,13},{10,... | collective-permute-start | bytes 2555912 | tf_op jit(solution)/shard_map/ppermute | solution.py:484
  52.5 25.7 %collective-permute-start.17 = (bf16[128,3328]{1,0:T(8,128)(2,1)S(1)}, bf16[128,3328]{1,0:T(8,128)(2,1)S(1)}, u32[]{:S(2)}, u32[]{:S(2)}) collective-permute-start(bf16[128,3328]{1,0:T(8,128)(2,1)S(1)} %bitcast.119), channel_id=1, source_target_pairs={{0,2},{1,3},{2,0},{3,1},{4,6},{5,7},{6,4},{7,5},{8,10},{9,11},{10,... | collective-permute-start | bytes 2555912 | tf_op jit(solution)/shard_map/ppermute | solution.py:484
  61.9 15.8 %collective-permute-start.15 = (bf16[2,4,16,2816]{3,2,1,0:T(8,128)(2,1)S(1)}, bf16[2,4,16,2816]{3,2,1,0:T(8,128)(2,1)S(1)}, u32[]{:S(2)}, u32[]{:S(2)}) collective-permute-start(bf16[2,4,16,2816]{3,2,1,0:T(8,128)(2,1)S(1)} %pad_maximum_fusion.2), channel_id=1, source_target_pairs={{0,1},{1,0},{2,3},{3,2},{4,5},{5,4},{6,7},{7,6},{8,9},{9,8},{10,11... | collective-permute-start | bytes 2162696 | tf_op jit(solution)/shard_map/ppermute | solution.py:484
  77.7 4.4 %collective-permute-start.18 = (bf16[128,3328]{1,0:T(8,128)(2,1)S(1)}, bf16[128,3328]{1,0:T(8,128)(2,1)S(1)}, u32[]{:S(2)}, u32[]{:S(2)}) collective-permute-start(bf16[128,3328]{1,0:T(8,128)(2,1)S(1)} %bitcast.125), channel_id=1, source_target_pairs={{0,2},{1,3},{2,0},{3,1},{4,6},{5,7},{6,4},{7,5},{8,10},{9,11},{10,... | collective-permute-start | bytes 2555912 | tf_op jit(solution)/shard_map/ppermute | solution.py:484
  77.7 3.4 %collective-permute-start.19 = (bf16[128,2816]{1,0:T(8,128)(2,1)S(1)}, bf16[128,2816]{1,0:T(8,128)(2,1)S(1)}, u32[]{:S(2)}, u32[]{:S(2)}) collective-permute-start(bf16[128,2816]{1,0:T(8,128)(2,1)S(1)} %bitcast.121), channel_id=1, source_target_pairs={{0,2},{1,3},{2,0},{3,1},{4,6},{5,7},{6,4},{7,5},{8,10},{9,11},{10,... | collective-permute-start | bytes 2162696 | tf_op jit(solution)/shard_map/ppermute | solution.py:484
  78.2 3.9 %collective-permute-start.20 = (bf16[128,2816]{1,0:T(8,128)(2,1)S(1)}, bf16[128,2816]{1,0:T(8,128)(2,1)S(1)}, u32[]{:S(2)}, u32[]{:S(2)}) collective-permute-start(bf16[128,2816]{1,0:T(8,128)(2,1)S(1)} %bitcast.127), channel_id=1, source_target_pairs={{0,2},{1,3},{2,0},{3,1},{4,6},{5,7},{6,4},{7,5},{8,10},{9,11},{10,... | collective-permute-start | bytes 2162696 | tf_op jit(solution)/shard_map/ppermute | solution.py:484
  101.2 10.8 %collective-permute-start.21 = (bf16[256,3968]{1,0:T(8,128)(2,1)S(1)}, bf16[256,3968]{1,0:T(8,128)(2,1)S(1)}, u32[]{:S(2)}, u32[]{:S(2)}) collective-permute-start(bf16[256,3968]{1,0:T(8,128)(2,1)S(1)} %get-tuple-element.100), channel_id=1, source_target_pairs={{0,2},{1,3},{2,0},{3,1},{4,6},{5,7},{6,4},{7,5},{8,10},{9,11},{10,... | collective-permute-start | bytes 6094856 | tf_op jit(solution)/shard_map/ppermute | solution.py:484
  101.3 10.3 %collective-permute-start.22 = (bf16[256,2176]{1,0:T(8,128)(2,1)S(1)}, bf16[256,2176]{1,0:T(8,128)(2,1)S(1)}, u32[]{:S(2)}, u32[]{:S(2)}) collective-permute-start(bf16[256,2176]{1,0:T(8,128)(2,1)S(1)} %get-tuple-element.102), channel_id=1, source_target_pairs={{0,2},{1,3},{2,0},{3,1},{4,6},{5,7},{6,4},{7,5},{8,10},{9,11},{10,... | collective-permute-start | bytes 3342344 | tf_op jit(solution)/shard_map/ppermute | solution.py:484
  102.9 19.6 %collective-permute-start.23 = (bf16[512,384]{1,0:T(8,128)(2,1)S(1)}, bf16[512,384]{1,0:T(8,128)(2,1)S(1)}, u32[]{:S(2)}, u32[]{:S(2)}) collective-permute-start(bf16[512,384]{1,0:T(8,128)(2,1)S(1)} %get-tuple-element.106), channel_id=1, source_target_pairs={{0,1},{1,0},{2,3},{3,2},{4,5},{5,4},{6,7},{7,6},{8,9},{9,8},{10,11... | collective-permute-start | bytes 1179656 | tf_op jit(solution)/shard_map/ppermute | solution.py:484
  112.5 20.6 %collective-permute-start.26 = (bf16[2,4,16,2176]{3,2,1,0:T(8,128)(2,1)S(1)}, bf16[2,4,16,2176]{3,2,1,0:T(8,128)(2,1)S(1)}, u32[]{:S(2)}, u32[]{:S(2)}) collective-permute-start(bf16[2,4,16,2176]{3,2,1,0:T(8,128)(2,1)S(1)} %slice_bitcast_fusion.2), channel_id=1, source_target_pairs={{0,1},{1,0},{2,3},{3,2},{4,5},{5,4},{6,7},{7,6},{8,9},{9,8},{10,11... | collective-permute-start | bytes 1671176 | tf_op jit(solution)/shard_map/ppermute | solution.py:484
  112.6 24.3 %collective-permute-start.25 = (bf16[2,4,16,3968]{3,2,1,0:T(8,128)(2,1)S(1)}, bf16[2,4,16,3968]{3,2,1,0:T(8,128)(2,1)S(1)}, u32[]{:S(2)}, u32[]{:S(2)}) collective-permute-start(bf16[2,4,16,3968]{3,2,1,0:T(8,128)(2,1)S(1)} %slice_bitcast_fusion), channel_id=1, source_target_pairs={{0,4},{1,5},{2,6},{3,7},{4,0},{5,1},{6,2},{7,3},{8,12},{9,13},{10,... | collective-permute-start | bytes 3047432 | tf_op jit(solution)/shard_map/ppermute | solution.py:484
  127.6 9.6 %collective-permute-start.24 = (bf16[384,1024]{1,0:T(8,128)(2,1)S(1)}, bf16[384,1024]{1,0:T(8,128)(2,1)S(1)}, u32[]{:S(2)}, u32[]{:S(2)}) collective-permute-start(bf16[384,1024]{1,0:T(8,128)(2,1)S(1)} %get-tuple-element.112), channel_id=1, source_target_pairs={{0,2},{1,3},{2,0},{3,1},{4,6},{5,7},{6,4},{7,5},{8,10},{9,11},{10,... | collective-permute-start | bytes 2359304 | tf_op jit(solution)/shard_map/ppermute | solution.py:484
  137.2 7.6 %collective-permute-start.27 = (bf16[4,16,2176]{2,1,0:T(8,128)(2,1)S(1)}, bf16[4,16,2176]{2,1,0:T(8,128)(2,1)S(1)}, u32[]{:S(2)}, u32[]{:S(2)}) collective-permute-start(bf16[4,16,2176]{2,1,0:T(8,128)(2,1)S(1)} %slice_bitcast_fusion.4), channel_id=1, source_target_pairs={{0,4},{1,5},{2,6},{3,7},{4,0},{5,1},{6,2},{7,3},{8,12},{9,13},{10,... | collective-permute-start | bytes 835592 | tf_op jit(solution)/shard_map/ppermute | solution.py:484
  138.8 14.3 %collective-permute-start.33 = (bf16[4,16,3968]{2,1,0:T(8,128)(2,1)S(1)}, bf16[4,16,3968]{2,1,0:T(8,128)(2,1)S(1)}, u32[]{:S(2)}, u32[]{:S(2)}) collective-permute-start(bf16[4,16,3968]{2,1,0:T(8,128)(2,1)S(1)} %slice_bitcast_fusion.3), channel_id=1, source_target_pairs={{0,1},{1,0},{2,3},{3,2},{4,5},{5,4},{6,7},{7,6},{8,9},{9,8},{10,11... | collective-permute-start | bytes 1523720 | tf_op jit(solution)/shard_map/ppermute | solution.py:484
  144.9 5.2 %collective-permute-start.29 = (bf16[16,2176]{1,0:T(8,128)(2,1)S(1)}, bf16[16,2176]{1,0:T(8,128)(2,1)S(1)}, u32[]{:S(2)}, u32[]{:S(2)}) collective-permute-start(bf16[16,2176]{1,0:T(8,128)(2,1)S(1)} %get-tuple-element.129), channel_id=1, source_target_pairs={{0,8},{1,9},{2,10},{3,11},{4,12},{5,13},{6,14},{7,15},{8,0},{9,1},... | collective-permute-start | bytes 208904 | tf_op jit(solution)/shard_map/ppermute | solution.py:484
  145.0 6.3 %collective-permute-start.31 = (bf16[16,2176]{1,0:T(8,128)(2,1)S(1)}, bf16[16,2176]{1,0:T(8,128)(2,1)S(1)}, u32[]{:S(2)}, u32[]{:S(2)}) collective-permute-start(bf16[16,2176]{1,0:T(8,128)(2,1)S(1)} %get-tuple-element.130), channel_id=1, source_target_pairs={{0,24},{1,25},{2,26},{3,27},{4,28},{5,29},{6,30},{7,31},{8,16},{9,... | collective-permute-start | bytes 208904 | tf_op jit(solution)/shard_map/ppermute | solution.py:484
  146.5 6.6 %collective-permute-start.30 = (bf16[16,2176]{1,0:T(8,128)(2,1)S(1)}, bf16[16,2176]{1,0:T(8,128)(2,1)S(1)}, u32[]{:S(2)}, u32[]{:S(2)}) collective-permute-start(bf16[16,2176]{1,0:T(8,128)(2,1)S(1)} %get-tuple-element.131), channel_id=1, source_target_pairs={{0,16},{1,17},{2,18},{3,19},{4,20},{5,21},{6,22},{7,23},{8,24},{9,... | collective-permute-start | bytes 208904 | tf_op jit(solution)/shard_map/ppermute | solution.py:484
  148.5 8.3 %collective-permute-start.28 = (bf16[2,4,24,1024]{3,2,1,0:T(8,128)(2,1)S(1)}, bf16[2,4,24,1024]{3,2,1,0:T(8,128)(2,1)S(1)}, u32[]{:S(2)}, u32[]{:S(2)}) collective-permute-start(bf16[2,4,24,1024]{3,2,1,0:T(8,128)(2,1)S(1)} %bitcast.140), channel_id=1, source_target_pairs={{0,4},{1,5},{2,6},{3,7},{4,0},{5,1},{6,2},{7,3},{8,12},{9,13},{10,... | collective-permute-start | bytes 1179656 | tf_op jit(solution)/shard_map/ppermute | solution.py:484
  153.1 12.0 %copy-start.2 = (f32[16,2176]{1,0:T(8,128)}, f32[16,2176]{1,0:T(8,128)S(1)}, u32[]{:S(2)}) copy-start(f32[16,2176]{1,0:T(8,128)S(1)} %fusion.10) | copy-start | bytes 417796
  153.3 5.5 %collective-permute-start.34 = (bf16[16,3968]{1,0:T(8,128)(2,1)S(1)}, bf16[16,3968]{1,0:T(8,128)(2,1)S(1)}, u32[]{:S(2)}, u32[]{:S(2)}) collective-permute-start(bf16[16,3968]{1,0:T(8,128)(2,1)S(1)} %get-tuple-element.126), channel_id=1, source_target_pairs={{0,8},{1,9},{2,10},{3,11},{4,12},{5,13},{6,14},{7,15},{8,0},{9,1},... | collective-permute-start | bytes 380936 | tf_op jit(solution)/shard_map/ppermute | solution.py:484
  153.4 7.4 %collective-permute-start.36 = (bf16[16,3968]{1,0:T(8,128)(2,1)S(1)}, bf16[16,3968]{1,0:T(8,128)(2,1)S(1)}, u32[]{:S(2)}, u32[]{:S(2)}) collective-permute-start(bf16[16,3968]{1,0:T(8,128)(2,1)S(1)} %get-tuple-element.127), channel_id=1, source_target_pairs={{0,24},{1,25},{2,26},{3,27},{4,28},{5,29},{6,30},{7,31},{8,16},{9,... | collective-permute-start | bytes 380936 | tf_op jit(solution)/shard_map/ppermute | solution.py:484
  155.6 9.5 %collective-permute-start.35 = (bf16[16,3968]{1,0:T(8,128)(2,1)S(1)}, bf16[16,3968]{1,0:T(8,128)(2,1)S(1)}, u32[]{:S(2)}, u32[]{:S(2)}) collective-permute-start(bf16[16,3968]{1,0:T(8,128)(2,1)S(1)} %get-tuple-element.128), channel_id=1, source_target_pairs={{0,16},{1,17},{2,18},{3,19},{4,20},{5,21},{6,22},{7,23},{8,24},{9,... | collective-permute-start | bytes 380936 | tf_op jit(solution)/shard_map/ppermute | solution.py:484
  157.0 8.1 %collective-permute-start.32 = (bf16[4,24,1024]{2,1,0:T(8,128)(2,1)S(1)}, bf16[4,24,1024]{2,1,0:T(8,128)(2,1)S(1)}, u32[]{:S(2)}, u32[]{:S(2)}) collective-permute-start(bf16[4,24,1024]{2,1,0:T(8,128)(2,1)S(1)} %slice_bitcast_fusion.5), channel_id=1, source_target_pairs={{0,1},{1,0},{2,3},{3,2},{4,5},{5,4},{6,7},{7,6},{8,9},{9,8},{10,11... | collective-permute-start | bytes 589832 | tf_op jit(solution)/shard_map/ppermute | solution.py:484
  165.1 3.8 %slice-start = ((f32[16,2176]{1,0:T(8,128)}), f32[16,1536]{1,0:T(8,128)S(1)}, s32[]{:S(2)}) async-start(f32[16,2176]{1,0:T(8,128)} %copy-done.2), calls=%async_computation | async-start | bytes 196608 | tf_op jit(solution)/shard_map/slice | solution.py:1032
  165.3 6.4 %collective-permute-start.37 = (bf16[24,1024]{1,0:T(8,128)(2,1)S(1)}, bf16[24,1024]{1,0:T(8,128)(2,1)S(1)}, u32[]{:S(2)}, u32[]{:S(2)}) collective-permute-start(bf16[24,1024]{1,0:T(8,128)(2,1)S(1)} %get-tuple-element.135), channel_id=1, source_target_pairs={{0,8},{1,9},{2,10},{3,11},{4,12},{5,13},{6,14},{7,15},{8,0},{9,1},... | collective-permute-start | bytes 147464 | tf_op jit(solution)/shard_map/ppermute | solution.py:484
  165.4 6.3 %collective-permute-start.39 = (bf16[24,1024]{1,0:T(8,128)(2,1)S(1)}, bf16[24,1024]{1,0:T(8,128)(2,1)S(1)}, u32[]{:S(2)}, u32[]{:S(2)}) collective-permute-start(bf16[24,1024]{1,0:T(8,128)(2,1)S(1)} %get-tuple-element.136), channel_id=1, source_target_pairs={{0,24},{1,25},{2,26},{3,27},{4,28},{5,29},{6,30},{7,31},{8,16},{9,... | collective-permute-start | bytes 147464 | tf_op jit(solution)/shard_map/ppermute | solution.py:484
  168.1 5.0 %collective-permute-start.38 = (bf16[24,1024]{1,0:T(8,128)(2,1)S(1)}, bf16[24,1024]{1,0:T(8,128)(2,1)S(1)}, u32[]{:S(2)}, u32[]{:S(2)}) collective-permute-start(bf16[24,1024]{1,0:T(8,128)(2,1)S(1)} %get-tuple-element.137), channel_id=1, source_target_pairs={{0,16},{1,17},{2,18},{3,19},{4,20},{5,21},{6,22},{7,23},{8,24},{9,... | collective-permute-start | bytes 147464 | tf_op jit(solution)/shard_map/ppermute | solution.py:484
